TPU v7x, 128 devices: a whole 4x4x4 slice. The times are simulated.
128 devices in a mesh: section: 4 (over z), seq: 32 (over x, y, core).
Axes of the slice: x: 4, y: 4, z: 4, core: 2. Of those that a mesh axis runs over, the one named last changes fastest.
Arguments:
- section_input: bfloat16 [4, 4096, 4096], P('section', 'seq'), may hold values from -54 to 54, as said below
- sent_grad: bfloat16 [4, 4096, 4096], P('section', 'seq'), may hold values from -6 to 6
- norm_gain: float32 [4, 4096], P('section'), may hold values from 0.1 to 1.9
- short_filter: float32 [4, 21, 4096], P('section'), may hold values from -3.3 to 3.3
- log_rate: float32 [4, 16, 256], P('section'), may hold values from -10 to -3.4, as said below
- residue: float32 [4, 16, 256], P('section'), may hold values from -1 to 1
- skip_gain: float32 [4, 4096], P('section'), may hold values from -1 to 1
Outputs:
- block_out: bfloat16 [4, 4096, 4096], P('section', 'seq')
- input_grad: bfloat16 [4, 4096, 4096], P('section', 'seq')
- channel_grads: float32 [4, 32, 23, 4096], P('section', 'seq')
- residue_grads: float32 [4, 32, 16, 256], P('section', 'seq')
- rate_grads: float32 [4, 32, 16, 256], P('section', 'seq')
Inputs may be any that keep to these rules, and one draw needn't show every extreme that they name: `section_input`: row and channel scales of the inputs vary. log_rate and residue are drawn together.
All inputs are finite; a program needn't handle non-finite values.
Results may differ from a plain program's by a relative error of at most 0.0072.
Values may be sent and summed in bfloat16 or wider, within the bound.
No kernel may reach another device: no remote copies, remote signals or barrier semaphores. Data moves between devices by JAX's collectives and lax.ppermute only.
A program may use at most 320 MiB of HBM per device.

v0:
```python
import jax
import jax.numpy as jnp
from jax import lax
from jax.sharding import PartitionSpec as P

EPSILON = 1e-06
HIGHEST = lax.Precision.HIGHEST


def shifted(shard, axis, by):
    devices = lax.axis_size(axis)
    return lax.ppermute(shard, axis, [(i, (i + by) % devices) for i in range(devices)])


def shifted_2(value, axis, steps):
    count = lax.axis_size(axis)
    initial, last = (max(0, -steps), min(count, count - steps))
    return lax.ppermute(value, axis, [(source, source + steps) for source in range(initial, last)])


def prefix(shard, axis, combine, identity, reverse):
    devices, mine = (lax.axis_size(axis), lax.axis_index(axis))
    everything = jax.tree.map(lambda part: lax.all_gather(part, axis), shard)
    start = jax.tree.map(
        lambda part, zero: jnp.broadcast_to(jnp.asarray(zero, part.dtype), part.shape),
        shard,
        identity,
    )

    def hop(k, before):
        at = devices - 1 - k if reverse else k
        reached = at > mine if reverse else at < mine
        new = combine(before, jax.tree.map(lambda part: part[at], everything))
        return jax.tree.map(lambda a, b: jnp.where(reached, a, b), new, before)

    return lax.fori_loop(0, devices, hop, start)


def combine(earlier, latter):
    return (earlier[0] * latter[0], latter[0][:, :, None] * earlier[1] + latter[1])


def depthwise(rows, kernel):
    channels = rows.shape[1]
    result = lax.conv_general_dilated(
        rows[None],
        kernel[:, None, :],
        (1,),
        "VALID",
        dimension_numbers=("NWC", "WIO", "NWC"),
        feature_group_count=channels,
        precision=HIGHEST,
    )
    return result[0]


def on_device(section_input, sent_grad, norm_gain, short_filter, log_rate, residue, skip_gain):
    inputs = section_input[0]
    row_count, channels = inputs.shape
    groups = log_rate.shape[2]
    group_size = channels // groups
    tap_count = short_filter.shape[1] // 3
    border_rows = tap_count - 1
    arrived = shifted(sent_grad, "section", -1)[0].astype(jnp.float32)
    before = shifted_2(inputs[row_count - border_rows :], "seq", 1)
    extended = jnp.concatenate([before, inputs], 0).astype(jnp.float32)
    inverse = lax.rsqrt(jnp.mean(extended * extended, axis=-1, keepdims=True) + EPSILON)
    unscaled_normalized = extended * inverse
    gain_row = norm_gain[0]
    rounded = lax.optimization_barrier((unscaled_normalized * gain_row).astype(jnp.bfloat16))
    normed = rounded.astype(jnp.float32)
    filters = short_filter[0].reshape(3, tap_count, channels)

    def feature(stream):
        return depthwise(normed, filters[stream, ::-1])

    query_rows = feature(0)
    key_rows = feature(1)
    value_rows = feature(2)
    product = key_rows * value_rows
    skip_row = skip_gain[0]
    weights = residue[0]
    decay_log = -jnp.exp(log_rate[0])
    decay_base = jnp.exp(decay_log)
    block_len = min(64, row_count)
    blocks = row_count // block_len
    lag_values = jnp.arange(block_len, dtype=jnp.float32)
    powers = jnp.exp(decay_log[:, :, None] * lag_values)
    reversed_pow = jnp.exp(decay_log[:, :, None] * (block_len - 1 - lag_values))
    lag_ints = jnp.arange(block_len, dtype=jnp.int32)
    lag_table = (
        lag_ints[:, None, None] - lag_ints[None, :, None] == lag_ints[None, None, :]
    ).astype(jnp.float32)
    kernel = jnp.sum(weights[:, :, None] * powers, 0)
    toeplitz = jnp.einsum("gj,tsj->gts", kernel, lag_table, precision=HIGHEST)
    block_index = jnp.arange(blocks, dtype=jnp.float32)
    later_gap = block_index[:, None] - 1 - block_index[None, :]
    carry_table = jnp.where(
        later_gap >= 0,
        jnp.exp(decay_log[:, :, None, None] * block_len * jnp.maximum(later_gap, 0.0)),
        0.0,
    )
    span_pow = jnp.exp(decay_log * block_len)
    shard_pow = jnp.exp(decay_log * row_count)
    product_blocks = product.reshape(blocks, block_len, groups, group_size)
    inside = jnp.einsum("gts,bsgr->btgr", toeplitz, product_blocks, precision=HIGHEST)
    block_ends = jnp.einsum("mgs,bsgr->bmgr", reversed_pow, product_blocks, precision=HIGHEST)
    local_entry = jnp.einsum("mgab,bmgr->amgr", carry_table, block_ends, precision=HIGHEST)
    summary = span_pow[:, :, None] * local_entry[-1] + block_ends[-1]
    identity = (jnp.ones_like(shard_pow), jnp.zeros_like(summary))
    entering = prefix((shard_pow, summary), "seq", combine, identity, False)[1]
    entry_state = (
        local_entry
        + jnp.exp(decay_log[None] * block_len * block_index[:, None, None])[..., None]
        * entering[None]
    )
    out_weights = weights[:, :, None] * powers * decay_base[:, :, None]
    carried_in = jnp.einsum("mgt,bmgr->btgr", out_weights, entry_state, precision=HIGHEST)
    modal_out = (inside + carried_in).reshape(row_count, channels) + skip_row * product
    block_out = (inputs.astype(jnp.float32) + query_rows * modal_out).astype(jnp.bfloat16)
    grad_query = arrived * modal_out
    grad_modal = arrived * query_rows
    grad_blocks = grad_modal.reshape(blocks, block_len, groups, group_size)
    back_inside = jnp.einsum("gst,bsgr->btgr", toeplitz, grad_blocks, precision=HIGHEST)
    block_starts = jnp.einsum(
        "mgt,btgr->bmgr", weights[:, :, None] * powers, grad_blocks, precision=HIGHEST
    )
    local_exit = jnp.einsum("mgba,bmgr->amgr", carry_table, block_starts, precision=HIGHEST)
    first_adjoint = block_starts[0] + span_pow[:, :, None] * local_exit[0]
    leaving = prefix((shard_pow, first_adjoint), "seq", combine, identity, True)[1]
    exiting = (
        local_exit
        + jnp.exp(decay_log[None] * block_len * (blocks - 1 - block_index)[:, None, None])[
            ..., None
        ]
        * leaving[None]
    )
    back_carry = jnp.einsum(
        "mgt,bmgr->btgr", reversed_pow * decay_base[:, :, None], exiting, precision=HIGHEST
    )
    grad_product = (back_inside + back_carry).reshape(row_count, channels) + skip_row * grad_modal
    grad_key = grad_product * value_rows
    grad_value = grad_product * key_rows
    crossed = jnp.einsum("btgr,bsgr->gts", grad_blocks, product_blocks, precision=HIGHEST)
    by_lag = jnp.einsum("gts,tsj->gj", crossed, lag_table, precision=HIGHEST)
    carried_out = jnp.einsum(
        "mgt,btgr->bmgr", powers * decay_base[:, :, None], grad_blocks, precision=HIGHEST
    )
    grad_residue = jnp.einsum("mgj,gj->mg", powers, by_lag, precision=HIGHEST) + jnp.sum(
        carried_out * entry_state, axis=(0, 3)
    )
    slopes = lag_values * jnp.exp(decay_log[:, :, None] * (lag_values - 1.0))
    term_one = weights * jnp.einsum("mgj,gj->mg", slopes, by_lag, precision=HIGHEST)
    ramp_out = weights[:, :, None] * (lag_values + 1.0) * powers
    term_two = jnp.sum(
        jnp.einsum("mgt,btgr->bmgr", ramp_out, grad_blocks, precision=HIGHEST) * entry_state,
        axis=(0, 3),
    )
    ramp_in = (block_len - 1.0 - lag_values) * reversed_pow
    third_term = jnp.sum(
        jnp.einsum("mgs,bsgr->bmgr", ramp_in, product_blocks, precision=HIGHEST) * exiting,
        axis=(0, 3),
    )
    fourth_term = block_len * span_pow * jnp.sum(exiting * entry_state, axis=(0, 3))
    grad_decay = term_one + term_two + third_term + fourth_term
    grad_rate = grad_decay * (decay_base * decay_log)
    streams = [grad_query, grad_key, grad_value]
    heads = jnp.stack([item[:border_rows] for item in streams], 0)
    following = shifted_2(heads, "seq", -1)
    normalized_gradient = sum(
        (
            depthwise(jnp.concatenate([streams[stream], following[stream]], 0), filters[stream])
            for stream in range(3)
        )
    )
    filter_rows = jnp.stack([depthwise(normed, streams[stream])[::-1] for stream in range(3)], 0)
    local_normalized_input = unscaled_normalized[border_rows:]
    inverse_own = inverse[border_rows:]
    gain_gradient = jnp.sum(normalized_gradient * local_normalized_input, 0)
    grad_skip = jnp.sum(grad_modal * product, 0)
    channel_grads = jnp.concatenate(
        [filter_rows.reshape(3 * tap_count, channels), gain_gradient[None], grad_skip[None]], 0
    )[None, None]
    scaled_result = normalized_gradient * gain_row
    input_grad = arrived + inverse_own * (
        scaled_result
        - local_normalized_input
        * jnp.mean(scaled_result * local_normalized_input, axis=-1, keepdims=True)
    )
    return (
        block_out[None],
        input_grad.astype(jnp.bfloat16)[None],
        channel_grads,
        grad_residue[None, None],
        grad_rate[None, None],
    )


def solution(mesh):
    placed = (
        P("section", "seq", None),
        P("section", "seq", None),
        P("section", None),
        P("section", None, None),
        P("section", None, None),
        P("section", None, None),
        P("section", None),
    )
    return jax.shard_map(
        on_device,
        mesh=mesh,
        in_specs=placed,
        out_specs=(
            P("section", "seq", None),
            P("section", "seq", None),
            P("section", "seq", None, None),
            P("section", "seq", None, None),
            P("section", "seq", None, None),
        ),
        check_vma=False,
    )
```

profile of v0, /device:TPU:25, one launch (start us, length us, event | category | flops | bytes accessed | tf_op | source)
XLA Modules:
  0.0 1019.2 jit_solution(15819333634693884801)
XLA Ops:
  36.4 5.6 mul.492
  42.0 7.4 fusion.53
  49.4 7.0 copy.168
  56.4 40.5 %fusion.16 = f32[16,256,16,2]{2,3,1,0:T(2,128)} fusion(f32[2,16,256,16]{3,0,2,1:T(2,128)} %copy.168, pred[2,2]{0,1:T(4,128)(4,1)S(1)} %copy-done.66, f32[2,2]{0,1:T(2,128)S(1)} %copy-done.61, f32[16,256]{1,0:T(8,128)S(1)} %copy-done.54), kind=kOutput, calls=%fused_computation.35 | convolution fusion | flops 3178496 | bytes 1064980 | tf_op jit(solution)/shard_map/mgab,bmgr->amgr/dot_general | solution.py:108
  97.0 16.0 %copy.170 = f32[16,256,16,2]{0,2,3,1:T(8,128)} copy(f32[16,256,16,2]{2,3,1,0:T(2,128)} %fusion.16) | data formatting | bytes 1048576 | tf_op jit(solution)/shard_map/mgab,bmgr->amgr/dot_general | solution.py:108
  129.3 9.5 copy.221
  140.3 24.0 %all_gather.6 = f32[32,16,256]{2,1,0:T(8,128)S(1)} all-gather(f32[1,16,256]{2,1,0:T(8,128)S(1)} %get-tuple-element.366), channel_id=1, replica_groups=mesh['section'=4,'seq'=32] {'seq'}, dimensions={0}, use_global_device_ids=true | all-gather | bytes 540672 | tf_op jit(solution)/shard_map/all_gather | solution.py:23
  165.4 4.6 copy.177
  182.3 19.5 %fusion.13 = f32[256,2,16,64]{3,2,1,0:T(8,128)} fusion(f32[256,64,64,1]{2,1,3,0:T(8,128)} %copy.221, f32[2,64,256,16]{1,0,3,2:T(2,128)} %mul.492), kind=kOutput, calls=%fused_computation.32 | convolution fusion | flops 402653184 | bytes 8388608 | tf_op jit(solution)/shard_map/gts,bsgr->btgr/dot_general | solution.py:106
  201.9 133.1 %all-gather.3.cloned.1.call-done = f32[32,16,256,16]{1,3,0,2:T(8,128)} async-done(((f32[1,16,256,16]{1,3,0,2:T(8,128)}), f32[32,16,256,16]{1,3,0,2:T(8,128)}) %all-gather.3.cloned.1.call-update) | async-done | bytes 8388624 | tf_op jit(solution)/shard_map/all_gather | solution.py:23
  335.0 38.8 %copy.173 = f32[32,16,256,16]{2,3,1,0:T(8,128)} copy(f32[32,16,256,16]{1,3,0,2:T(8,128)} %all-gather.3.cloned.1.call-done) | data formatting | bytes 16777216
  373.8 38.6 %while.30 = (s32[]{:T(128)}, f32[16,256,16]{1,2,0:T(8,128)S(1)}, s32[]{:T(128)}, f32[32,16,256]{2,1,0:T(8,128)S(1)}, f32[32,16,256,16]{2,3,1,0:T(8,128)}, /*index=5*/s32[]{:T(128)}, s32[]{:T(128)}) while((s32[]{:T(128)}, f32[16,256,16]{1,2,0:T(8,128)S(1)}, s32[]{:T(128)}, f32[32,16,256]{2,1,0:T(8,128)S(1)}, ...), condition=%wide.region_3.4_spmd.clone, body=%wide.region_2.3_spmd.clone.sunk | while | flops 262148 | bytes 835689 | solution.py:36
  414.6 7.3 add_bitcast_fusion.1
  426.2 5.8 reshape.351
  434.9 5.5 convert_multiply_fusion
  443.4 5.7 mul.530
  449.1 7.4 fusion.50
  456.6 7.0 copy.187
  463.5 32.4 %fusion.15 = f32[16,256,16,2]{2,3,1,0:T(2,128)} fusion(f32[2,16,256,16]{3,0,2,1:T(2,128)} %copy.187, pred[2,2]{0,1:T(4,128)(4,1)S(1)} %copy-done.67, f32[2,2]{0,1:T(2,128)S(1)} %copy-done.62, f32[16,256]{1,0:T(8,128)S(1)} %copy-done.55), kind=kOutput, calls=%fused_computation.34 | convolution fusion | flops 3178496 | bytes 1064980 | tf_op jit(solution)/shard_map/mgba,bmgr->amgr/dot_general | solution.py:128
  496.0 7.0 copy.188
  506.9 4.8 copy.181
  522.9 5.9 reshape.354
  528.7 5.4 reshape.352
  534.2 8.3 fusion.5
  544.1 18.4 %fusion.17 = f32[256,64,64]{2,1,0:T(8,128)} fusion(f32[2,64,256,16]{1,0,3,2:T(2,128)} %mul.492, f32[2,64,256,16]{1,0,3,2:T(2,128)} %mul.530), kind=kOutput, calls=%fused_computation.36 | convolution fusion | flops 402653184 | bytes 8388608 | tf_op jit(solution)/shard_map/btgr,bsgr->gts/dot_general | solution.py:144
  562.4 8.6 copy.212
  571.1 4.7 fusion.174
  583.6 4.4 fusion.96
  588.0 7.8 fusion.6
  603.9 121.3 %all-gather.5.cloned.1.call-done = f32[32,16,256,16]{1,3,0,2:T(8,128)} async-done(((f32[1,16,256,16]{1,3,0,2:T(8,128)}), f32[32,16,256,16]{1,3,0,2:T(8,128)}) %all-gather.5.cloned.1.call-update) | async-done | bytes 8388624 | tf_op jit(solution)/shard_map/all_gather | solution.py:23
  725.2 38.8 %copy.189 = f32[32,16,256,16]{2,3,1,0:T(8,128)} copy(f32[32,16,256,16]{1,3,0,2:T(8,128)} %all-gather.5.cloned.1.call-done) | data formatting | bytes 16777216
  764.1 61.1 %while.31 = (s32[]{:T(128)}, f32[16,256,16]{1,2,0:T(8,128)S(1)}, s32[]{:T(128)}, f32[32,16,256]{2,1,0:T(8,128)}, f32[32,16,256,16]{2,3,1,0:T(8,128)}, /*index=5*/s32[]{:T(128)}, s32[]{:T(128)}, s32[]{:T(128)}, s32[]{:T(128)}) while((s32[]{:T(128)}, f32[16,256,16]{1,2,0:T(8,128)S(1)}, s32[]{:T(128)}, f32[32,16,256]{2,1,0:T(8,128)}, ...), condition=%wide.region_5.6_spmd.clone, body=%wide.region_4.5_spmd.clone.sunk | while | flops 262152 | bytes 835751 | solution.py:36
  827.7 6.5 multiply_reduce_fusion
  835.0 5.6 fusion.4
  840.6 5.1 fusion.20
  845.7 10.6 %add_bitcast_fusion = f32[2,64,256,16]{1,3,0,2:T(8,128)S(1)} fusion(f32[256,2,16,64]{3,2,1,0:T(8,128)S(1)} %fusion.20, f32[256,64,64,1]{2,1,3,0:T(8,128)} %copy.221, f32[2,64,256,16]{1,0,3,2:T(2,128)S(1)} %copy-done), kind=kOutput, calls=%fused_computation.21 | convolution fusion | flops 403177472 | bytes 10485760 | tf_op jit(solution)/shard_map/gst,bsgr->btgr/dot_general | solution.py:124
  860.6 5.5 reshape.355
  866.0 5.4 reshape.353
  874.5 6.8 bitcast_multiply_fusion.3
  881.3 4.7 fusion.78
  886.8 14.2 %rev.12 = f32[7,4096]{1,0:T(8,128)} reverse(f32[7,4096]{1,0:T(8,128)} %bitcast.337), dimensions={0} | reverse | bytes 229376 | tf_op jit(solution)/shard_map/rev | solution.py:176
  900.9 5.8 fusion.76
  907.5 14.2 %rev.13 = f32[7,4096]{1,0:T(8,128)} reverse(f32[7,4096]{1,0:T(8,128)} %bitcast.338), dimensions={0} | reverse | bytes 229376 | tf_op jit(solution)/shard_map/rev | solution.py:176
  921.7 5.8 fusion.74
  928.2 14.2 %rev.14 = f32[7,4096]{1,0:T(8,128)} reverse(f32[7,4096]{1,0:T(8,128)} %bitcast.339), dimensions={0} | reverse | bytes 229376 | tf_op jit(solution)/shard_map/rev | solution.py:176
  945.5 5.4 multiply_reduce_fusion.2
  959.3 6.1 collective-permute-done.2
  978.1 5.0 reshape.382
  (379 shorter events, 268.5 us)
Async XLA Ops:
  7.2 11.3 %copy-start.7 = (bf16[1,128,4096]{2,1,0:T(8,128)(2,1)S(1)}, bf16[1,128,4096]{2,1,0:T(8,128)(2,1)}, u32[]{:S(2)}) copy-start(bf16[1,128,4096]{2,1,0:T(8,128)(2,1)} %param.11) | copy-start | bytes 3145732
  7.2 11.9 %copy-start.41 = (f32[1,4096]{1,0:T(1,128)S(1)}, f32[1,4096]{1,0:T(1,128)}, u32[]{:S(2)}) copy-start(f32[1,4096]{1,0:T(1,128)} %param.13) | copy-start | bytes 49156
  7.2 327.8 %all-gather.3.cloned.1.call-start = ((), (), s32[]{:S(2)}) async-start(), calls=%async_computation | async-start | bytes 69206016 | tf_op jit(solution)/shard_map/all_gather | solution.py:23
  8.2 10.3 %collective-permute-start = (bf16[6,4096]{1,0:T(8,128)(2,1)S(1)}, bf16[6,4096]{1,0:T(8,128)(2,1)S(1)}, u32[]{:S(2)}, u32[]{:S(2)}) collective-permute-start(bf16[6,4096]{1,0:T(8,128)(2,1)S(1)} %slice_bitcast_fusion.7), channel_id=1, source_target_pairs={{0,1},{1,2},{2,3},{3,4},{4,5},{5,6},{6,7},{7,8},{8,9},{9,10},{10,1... | collective-permute-start | bytes 147464 | tf_op jit(solution)/shard_map/ppermute | solution.py:18
  18.4 23.7 %copy-start.14 = (f32[16,256]{0,1:T(8,128)}, f32[16,256]{0,1:T(8,128)S(1)}, u32[]{:S(2)}) copy-start(f32[16,256]{0,1:T(8,128)S(1)} %copy.162) | copy-start | bytes 49156
  18.5 94.5 %copy-start.29 = (f32[16,256]{0,1:T(8,128)}, f32[16,256]{0,1:T(8,128)S(1)}, u32[]{:S(2)}) copy-start(f32[16,256]{0,1:T(8,128)S(1)} %copy.172) | copy-start | bytes 49156
  36.4 5.6 copy-start.56
  49.4 7.0 copy-start.54
  49.4 7.0 copy-start.61
  49.4 7.0 copy-start.66
  113.0 7.8 copy-start.45
  116.9 6.8 copy-start.15
  116.9 608.3 %all-gather.5.cloned.1.call-start = ((), (), s32[]{:S(2)}) async-start(), calls=%async_computation.1 | async-start | bytes 69206016 | tf_op jit(solution)/shard_map/all_gather | solution.py:23
  117.0 318.0 %collective-permute-start.1 = (bf16[1,128,4096]{2,1,0:T(8,128)(2,1)}, bf16[1,128,4096]{2,1,0:T(8,128)(2,1)S(1)}, u32[]{:S(2)}, u32[]{:S(2)}) collective-permute-start(bf16[1,128,4096]{2,1,0:T(8,128)(2,1)} %param.12), channel_id=1, source_target_pairs={{0,96},{32,0},{64,32},{96,64},{1,97},{33,1},{65,33},{97,65},{2,98}... | collective-permute-start | bytes 3145736 | tf_op jit(solution)/shard_map/ppermute | solution.py:12
  120.9 8.4 copy-start.24
  129.3 9.5 copy-start.49
  129.3 9.6 copy-start.50
  129.3 10.3 %copy-start.36 = (f32[1,7,4096]{2,0,1:T(1,128)S(1)}, f32[1,7,4096]{2,0,1:T(1,128)}, u32[]{:S(2)}) copy-start(f32[1,7,4096]{2,0,1:T(1,128)} %get-tuple-element.357) | copy-start | bytes 344068
  170.1 3.7 copy-start.38
  170.1 3.7 copy-start.64
  443.4 5.8 copy-start.25
  456.6 7.0 copy-start.55
  456.6 7.0 copy-start.62
  456.6 7.0 copy-start.67
  496.0 7.0 copy-start.30
  506.9 4.8 copy-start.59
  506.9 5.5 copy-start.22
  827.7 6.6 copy-start.1
  827.7 6.7 copy-start.2
  827.7 7.3 copy-start.3
  827.7 7.3 copy-start.18
  827.7 7.3 copy-start.57
  835.0 5.6 copy-start.23
  840.6 5.2 copy-start
  874.5 6.8 copy-start.17
  945.5 10.4 %copy-start.33 = (f32[7,4096]{1,0:T(8,128)S(1)}, f32[7,4096]{1,0:T(8,128)}, u32[]{:S(2)}) copy-start(f32[7,4096]{1,0:T(8,128)} %rev.12) | copy-start | bytes 344068
  945.5 10.4 %copy-start.34 = (f32[7,4096]{1,0:T(8,128)S(1)}, f32[7,4096]{1,0:T(8,128)}, u32[]{:S(2)}) copy-start(f32[7,4096]{1,0:T(8,128)} %rev.13) | copy-start | bytes 344068
  945.5 10.4 %copy-start.35 = (f32[7,4096]{1,0:T(8,128)S(1)}, f32[7,4096]{1,0:T(8,128)}, u32[]{:S(2)}) copy-start(f32[7,4096]{1,0:T(8,128)} %rev.14) | copy-start | bytes 344068
  950.9 7.7 copy-start.43
  950.9 7.7 copy-start.46
  951.0 7.7 copy-start.47
  951.0 7.7 copy-start.48
  953.7 11.7 %collective-permute-start.2 = (f32[3,6,4096]{2,1,0:T(8,128)}, f32[3,6,4096]{2,1,0:T(8,128)}, u32[]{:S(2)}, u32[]{:S(2)}) collective-permute-start(f32[3,6,4096]{2,1,0:T(8,128)} %pad_maximum_fusion.1), channel_id=1, source_target_pairs={{1,0},{2,1},{3,2},{4,3},{5,4},{6,5},{7,6},{8,7},{9,8},{10,9},{11,1... | collective-permute-start | bytes 884744 | tf_op jit(solution)/shard_map/ppermute | solution.py:18
  955.9 10.6 %copy-start.13 = (f32[128,4096]{1,0:T(8,128)S(1)}, f32[128,4096]{1,0:T(8,128)}, u32[]{:S(2)}) copy-start(f32[128,4096]{1,0:T(8,128)} %copy-done.12) | copy-start | bytes 6291460
  970.9 5.2 copy-start.9
  970.9 5.2 copy-start.11
  1003.2 3.7 copy-start.5
  1003.2 3.7 copy-start.42
  (27 other events, 54.7 us)
Sparse Core Ops, SparseCore 0:
  117.0 217.8 all-gather.2
  507.0 218.2 all-gather.4
where the time goes:
time: 1030 us; the launch traced here: 1020 us
  local copies, waits for them, and re-layouts  370 us (36%)
  waiting for transfers between devices  261 us (25%)
  matrix products  212 us (21%)
  other arithmetic  127 us (12%)
  blocking collectives  24 us (2%)
  between operations  15.1 us (1%)
    all_gather x2, waiting for transfers between devices, prefix(): everything = jax.tree.map(lambda part: lax.all_gather(part, axis), shard)  254 us
    unnamed x145, local copies, waits for them, and re-layouts  89.6 us
    select_n x64, other arithmetic, hop(): return jax.tree.map(lambda a, b: jnp.where(reached, a, b), new, before)  74.6 us
    conv_general_dilated x18, local copies, waits for them, and re-layouts, depthwise(): lax.conv_general_dilated(rows[None], kernel[:, None, :], (1,), 'VALID', d...  47.5 us
    rev x3, local copies, waits for them, and re-layouts, on_device(): depthwise(normed, streams[stream])[::-1]  42.5 us
    dot_general x1, matrix products, on_device(): jnp.einsum('mgab,bmgr->amgr', carry_table, block_ends, precision=HIGHEST)  40.5 us
    dot_general x1, matrix products, on_device(): jnp.einsum('mgba,bmgr->amgr', carry_table, block_starts, precision=HIGHEST)  32.4 us
    conv_general_dilated x9, matrix products, depthwise(): lax.conv_general_dilated(rows[None], kernel[:, None, :], (1,), 'VALID', d...  27.9 us
  transfers between devices with their start and end apart: 5, of which 3 were waited for; matrix products, arithmetic and copies ran while one was open for 26% of the time, Pallas kernels for 0%

commit v1 on v0

v1 whole, which is shorter than its diff:
```python
import jax
import jax.numpy as jnp
from jax import lax
from jax.experimental import pallas as pl
from jax.experimental.pallas import tpu as pltpu
from jax.sharding import PartitionSpec as P

EPSILON = 1e-06
F32 = jnp.float32
BF16 = jnp.bfloat16
LANES = 128
STEP = 8
WIDE = STEP * LANES
BLOCK = 64
TABLE_STEP = 16
VMEM_LIMIT = 60 * 1024 * 1024


def iota(shape, axis):
    return lax.broadcasted_iota(jnp.int32, shape, axis)


def dot(a, b):
    return jnp.dot(a, b, preferred_element_type=F32)


def call(kernel, grid, ins, outs, scratch=(), micros=1.0, name=None):
    total = sum(a.size * a.dtype.itemsize for a, _, _ in ins)
    for shape, dtype, _, _ in outs:
        size = jnp.dtype(dtype).itemsize
        for n in shape:
            size *= n
        total += size
    return pl.pallas_call(
        kernel,
        grid=grid,
        in_specs=[pl.BlockSpec(b, m) for _, b, m in ins],
        out_specs=[pl.BlockSpec(b, m) for _, _, b, m in outs],
        out_shape=[jax.ShapeDtypeStruct(s, d) for s, d, _, _ in outs],
        scratch_shapes=list(scratch),
        compiler_params=pltpu.CompilerParams(
            dimension_semantics=("arbitrary",) * len(grid), vmem_limit_bytes=VMEM_LIMIT
        ),
        cost_estimate=pl.CostEstimate(
            flops=int(micros * 1.0e9),
            bytes_accessed=int(total) if micros else 0,
            transcendentals=0,
        ),
        name=name,
    )(*[a for a, _, _ in ins])


def lane_group(shape):
    return (iota(shape, 1) % LANES) // 16


def by_group(rows):
    own = lane_group(rows.shape)
    zero = jnp.zeros_like(rows)
    return jnp.concatenate([jnp.where(own == g, rows, zero) for g in range(8)], 0)


def own_group(rows):
    own = lane_group((16, rows.shape[1]))
    kept = rows[:16]
    for g in range(1, 8):
        kept = jnp.where(own == g, rows[16 * g : 16 * g + 16], kept)
    return kept


def side_by_side(rows):
    return jnp.concatenate([rows[:BLOCK], rows[BLOCK:]], 1)


def joined(first, rest, lanes):
    return jnp.concatenate([first[:, lanes], rest[:, lanes]], 0).astype(F32)


def stacked(rows):
    return jnp.concatenate([rows[:, :LANES], rows[:, LANES:]], 0)


def table_kernel(lr, w, lc, lrw, kk, r_e, w_e):
    shape = (16, LANES)
    first = iota(shape, 1) < BLOCK
    token = (iota(shape, 1) % BLOCK).astype(F32)
    own = lane_group(shape)

    def split(value):
        high = value.astype(BF16).astype(F32)
        return jnp.where(first, high, value - high)

    for c in range(lc.shape[0]):
        parts = [[] for _ in range(5)]
        rate_lanes = weight_lanes = None
        for g in range(8):
            at = c * 8 + g
            rate = jnp.broadcast_to(jnp.exp(lr[:, at : at + 1]), shape)
            weight = jnp.broadcast_to(w[:, at : at + 1], shape)
            end = jnp.exp(-rate * (BLOCK - 1.0 - token))
            start = jnp.exp(-rate * token)
            decay = jnp.exp(-rate)
            parts[0].append(split(end))
            parts[1].append(split((BLOCK - 1.0 - token) * end))
            parts[2].append(split(start))
            parts[3].append(split((token + 1.0) * start))
            parts[4].append(decay * jnp.where(first, weight * start, end))
            for i, value in enumerate((end, start)):
                row = jnp.sum(weight * value, axis=0, keepdims=True)
                kk[i, at : at + 1, :] = jnp.where(first[:1], row, 0.0)
            if g == 0:
                rate_lanes, weight_lanes = rate, weight
            else:
                rate_lanes = jnp.where(own == g, rate, rate_lanes)
                weight_lanes = jnp.where(own == g, weight, weight_lanes)
        for i in range(4):
            lc[c, i] = jnp.concatenate(parts[i], 0).astype(BF16)
        turned = jnp.concatenate(parts[4], 0).T.astype(BF16)
        lrw[c, 0] = turned[:BLOCK]
        lrw[c, 1] = turned[BLOCK:]
        lanes = slice(c * LANES, (c + 1) * LANES)
        r_e[:, lanes] = rate_lanes
        w_e[:, lanes] = weight_lanes


def features_kernel(
    x, xh, gain, filt, lc, kk, r_e, nrm, q, k, v, p, inside, inv_out, s, f, inv
):
    channels = x.shape[1]
    step = pl.program_id(0)

    @pl.when(step == 0)
    def _():
        def add(i, carry):
            own, halo = carry
            lanes = pl.ds(pl.multiple_of(i * LANES, LANES), LANES)
            a = x[:, lanes].astype(F32)
            b = xh[:, lanes].astype(F32)
            return own + a * a, halo + b * b

        own, halo = lax.fori_loop(
            0,
            channels // LANES,
            add,
            (jnp.zeros((LANES, LANES), F32), jnp.zeros((8, LANES), F32)),
            unroll=4,
        )
        for rows, total in ((slice(0, 8), halo), (slice(8, 136), own)):
            mean = jnp.sum(total, axis=1, keepdims=True) * (1.0 / channels)
            inverse = lax.rsqrt(mean + EPSILON)
            inv[rows, :] = jnp.broadcast_to(inverse, total.shape)
        inv_out[...] = inv[...]

    for c in range(STEP):
        local = slice(c * LANES, (c + 1) * LANES)
        lanes = pl.ds(pl.multiple_of((step * STEP + c) * LANES, LANES), LANES)
        gains = gain[:, local]
        own = x[:, lanes].astype(F32) * inv[8:136, :]
        nrm[c, 8:136, :] = (own * gains).astype(BF16).astype(F32)
        halo = xh[:, lanes].astype(F32) * inv[0:8, :]
        nrm[c, 0:8, :] = (halo * gains).astype(BF16).astype(F32)
        taps = [filt[j, 0:1, local] for j in range(21)]
        for r in range(0, LANES, 32):
            total = [jnp.zeros((32, LANES), F32) for _ in range(3)]
            for j in range(7):
                rows = nrm[c, 8 + r - j : 40 + r - j, :]
                for i in range(3):
                    total[i] = total[i] + taps[i * 7 + j] * rows
            q[c, r : r + 32, :] = total[0]
            k[c, r : r + 32, :] = total[1]
            v[c, r : r + 32, :] = total[2]
            product = total[1] * total[2]
            high = product.astype(BF16)
            p[0, c, r : r + 32, :] = high
            p[1, c, r : r + 32, :] = (product - high.astype(F32)).astype(BF16)
    for c in range(STEP):
        local = slice(c * LANES, (c + 1) * LANES)
        high, low = side_by_side(p[0, c]), side_by_side(p[1, c])
        table = lc[c].reshape(2 * LANES, LANES)
        sums = dot(
            jnp.concatenate([table, table], 1), jnp.concatenate([high, high, low, low], 0)
        )
        ends, ramps = own_group(sums[:LANES]), own_group(sums[LANES:])
        span = jnp.exp(-float(BLOCK) * r_e[:, local])
        s[:, local] = span * ends[:, :LANES] + ends[:, LANES:]
        f[0:32, local] = stacked(ends)
        f[32:64, local] = stacked(ramps)
        inside[c] = forward_blocks(p[0, c], kk[0, c * 8 : c * 8 + 8, :])


def forward_blocks(p, kernel):
    first = iota((BLOCK, LANES), 1) < BLOCK
    tiles = []
    for g in range(0, 8, 2):
        even, odd = (jnp.broadcast_to(kernel[i : i + 1], (BLOCK, LANES)) for i in (g, g + 1))
        even = pltpu.roll(even, BLOCK + 1, 1, stride=1, stride_axis=0)
        odd = pltpu.roll(odd, 1, 1, stride=1, stride_axis=0)
        tiles.append(jnp.where(first, even, odd).astype(BF16))
    return stacked(dot(jnp.concatenate(tiles, 1), by_group(side_by_side(p))))


def taken(grads, c, streams, taps, first, rows):
    total = None
    for i, stream in enumerate(streams):
        for j in range(7):
            term = taps[stream * 7 + j] * grads[c, i, first + j : first + j + rows, :]
            total = term if total is None else total + term
    return total


def tap_gradients(grads, nrm, c, count):
    sums = [jnp.zeros((8, LANES), F32) for _ in range(7 * count)]
    for r in range(0, LANES, 32):
        items = [grads[c, i, 8 + r : 40 + r, :] for i in range(count)]
        for j in range(7):
            rows = nrm[c, 8 + r - j : 40 + r - j, :]
            for i in range(count):
                term = (items[i] * rows).reshape(4, 8, LANES)
                sums[i * 7 + j] = sums[i * 7 + j] + jnp.sum(term, axis=0)
    return [jnp.sum(item, axis=0, keepdims=True) for item in sums]


def clear_ends(grads, count):
    @pl.when(pl.program_id(0) == 0)
    def _():
        for i in range(count):
            grads[:, i, 0:8, :] = jnp.zeros((STEP, 8, LANES), F32)
            grads[:, i, 136:144, :] = jnp.zeros((STEP, 8, LANES), F32)


def output_kernel(
    inside, lrw, e, f, r_e, q, k, v, x, skip, g, g_rest, nrm, filt, out, gn, fg, grads
):
    clear_ends(grads, 1)
    for c in range(STEP):
        local = slice(c * LANES, (c + 1) * LANES)
        state = e[:, local]
        second = f[:, local] + jnp.exp(-float(BLOCK) * r_e[:, local]) * state
        states = jnp.concatenate([state, second], 1).astype(BF16)
        carried = stacked(dot(lrw[c, 0], by_group(states)))
        product = k[c] * v[c]
        modal = inside[c] + carried + skip[:, local] * product
        query = q[c]
        arrived = joined(g, g_rest, local)
        out[:, local] = (x[:, local].astype(F32) + query * modal).astype(BF16)
        grads[c, 0, 8:136, :] = arrived * modal
        skip_grad = jnp.sum(arrived * query * product, axis=0, keepdims=True)
        taps = [filt[j, 0:1, local] for j in range(7)]
        gn[c, 0:8, :] = taken(grads, c, (0,), taps, 0, 8)
        for r in range(8, 136, 32):
            gn[c, r : r + 32, :] = taken(grads, c, (0,), taps, r, 32)
        fg[:, local] = jnp.concatenate(tap_gradients(grads, nrm, c, 1) + [skip_grad], 0)


def adjoint_kernel(g, g_rest, q, lc, w_e, r_e, gm, a, b):
    for c in range(STEP):
        local = slice(c * LANES, (c + 1) * LANES)
        grad = (joined(g, g_rest, local) * q[c]).astype(BF16)
        gm[c] = grad
        sides = side_by_side(grad)
        sums = dot(lc[c].reshape(2 * LANES, LANES), jnp.concatenate([sides, sides], 0))
        starts, ramps = own_group(sums[:LANES]), own_group(sums[LANES:])
        span = jnp.exp(-float(BLOCK) * r_e[:, local])
        first = w_e[:, local] * (starts[:, :LANES] + span * starts[:, LANES:])
        a[:, local] = first.astype(BF16)
        b[0:32, local] = stacked(starts)
        b[32:64, local] = stacked(ramps)


def backward_kernel(p, gm, kk, back, by_lag):
    first = iota((BLOCK, LANES), 1) < BLOCK
    both = iota((LANES, LANES), 0) + iota((LANES, LANES), 1)
    same = iota((LANES, LANES), 0) // BLOCK == iota((LANES, LANES), 1) // BLOCK
    flip = (same & (both % BLOCK == BLOCK - 1)).astype(BF16)
    for c in range(STEP):
        grads = by_group(side_by_side(gm[c]))
        tiles = []
        for g in range(0, 8, 2):
            even, odd = (
                jnp.broadcast_to(kk[0, c * 8 + i : c * 8 + i + 1, :], (BLOCK, LANES))
                for i in (g, g + 1)
            )
            even = pltpu.roll(even, 0, 1, stride=1, stride_axis=0)
            odd = pltpu.roll(odd, BLOCK, 1, stride=1, stride_axis=0)
            tiles.append(jnp.where(first, even, odd).astype(BF16))
        back[c] = stacked(dot(jnp.concatenate(tiles, 1), grads))
        sides = jnp.concatenate([side_by_side(p[0, c]), side_by_side(p[1, c])], 0)
        sides = dot(flip, sides).astype(BF16)
        crossed = lax.dot_general(
            sides, grads, (((1,), (1,)), ((), ())), preferred_element_type=F32
        )
        crossed = crossed[:BLOCK] + crossed[BLOCK:]
        for g in range(8):
            tile = crossed[:, g // 2 * LANES : (g // 2 + 1) * LANES]
            tile = jnp.where(first if g % 2 == 0 else ~first, tile, 0.0)
            tile = pltpu.roll(tile, g % 2 * BLOCK, 1, stride=1, stride_axis=0)
            by_lag[c * 8 + g : c * 8 + g + 1, :] = jnp.sum(tile, axis=0, keepdims=True)


def mixer_kernel(
    back, lrw, a, b, w_e, r_e, g, g_rest, q, k, v, gn0, nrm, filt, skip, gain, x, inv,
    gn, fg, hx, part, grads,
):
    clear_ends(grads, 2)

    @pl.when(pl.program_id(0) == 0)
    def _():
        hx[...] = jnp.zeros_like(hx)

    for c in range(STEP):
        local = slice(c * LANES, (c + 1) * LANES)
        second = a[:, local].astype(F32)
        span = jnp.exp(-float(BLOCK) * r_e[:, local])
        first = w_e[:, local] * b[:, local] + span * second
        states = jnp.concatenate([first, second], 1).astype(BF16)
        carried = stacked(dot(lrw[c, 0], by_group(states)))
        modal = joined(g, g_rest, local) * q[c]
        product = back[c] + carried + skip[:, local] * modal
        grads[c, 0, 8:136, :] = product * v[c]
        grads[c, 1, 8:136, :] = product * k[c]
        gains = gain[:, local]
        taps = [filt[j, 0:1, local] for j in range(21)]
        part[:, local] = (gn0[c, 0:8, :] + taken(grads, c, (1, 2), taps, 0, 8)).astype(BF16)
        gain_grad = jnp.zeros((8, LANES), F32)
        for r in range(0, LANES, 32):
            total = gn0[c, 8 + r : 40 + r, :] + taken(grads, c, (1, 2), taps, 8 + r, 32)
            gn[c, r : r + 32, :] = total
            xhat = x[r : r + 32, local].astype(F32) * inv[8 + r : 40 + r, :]
            both = total * xhat
            gain_grad = gain_grad + jnp.sum(both.reshape(4, 8, LANES), axis=0)
            hx[r : r + 32, :] += both * gains
        gain_grad = jnp.sum(gain_grad, axis=0, keepdims=True)
        rows = tap_gradients(grads, nrm, c, 2) + [gain_grad, jnp.zeros((1, LANES), F32)]
        fg[:, local] = jnp.concatenate(rows, 0)


def final_kernel(
    gn, g, g_rest, fg0, fg, hx, part, x, x_last, inv, gain, gain_all, out, cg, mean
):
    channels = x_last.shape[1]
    step = pl.program_id(0)

    @pl.when(step == 0)
    def _():
        def add(i, total):
            lanes = pl.ds(pl.multiple_of(i * LANES, LANES), LANES)
            xhat = x_last[8:16, lanes].astype(F32) * inv[128:136, :]
            return total + part[:, lanes].astype(F32) * gain_all[:, lanes] * xhat

        extra = lax.fori_loop(
            0, channels // LANES, add, jnp.zeros((8, LANES), F32), unroll=4
        )
        total = jnp.concatenate([hx[:120], hx[120:] + extra], 0)
        total = jnp.sum(total, axis=1, keepdims=True) * (1.0 / channels)
        mean[...] = jnp.broadcast_to(total, mean.shape)

    for c in range(STEP):
        local = slice(c * LANES, (c + 1) * LANES)
        lanes = pl.ds(pl.multiple_of((step * STEP + c) * LANES, LANES), LANES)
        arrived = joined(g, g_rest, local)
        extra = part[:, lanes].astype(F32)
        own = gn[c]
        own = jnp.concatenate([own[:120], own[120:] + extra], 0)
        xhat = x[:, local].astype(F32) * inv[8:136, :]
        result = arrived + inv[8:136, :] * (own * gain[:, local] - xhat * mean[...])
        out[:, local] = result.astype(BF16)
        fixed = jnp.sum(extra * xhat[120:], axis=0, keepdims=True)
        sources = [fg0[i : i + 1, local] for i in range(7)]
        sources += [fg[i : i + 1, local] for i in range(14)]
        sources += [fg[14:15, local] + fixed, fg0[7:8, local]]
        for i, source in enumerate(sources):
            cg[i, 0:1, local] = source


def modes_kernel(a, b, e, f, r_e, w_e, by_lag, lr, w, residue_out, rate_out):
    groups = lr.shape[1]
    chunks = e.shape[1] // LANES

    def chunk(i, total):
        lanes = pl.ds(pl.multiple_of(i * LANES, LANES), LANES)
        rate = r_e[:, lanes]
        weight = w_e[:, lanes]
        span = jnp.exp(-float(BLOCK) * rate)
        state0 = e[:, lanes]
        state1 = f[0:16, lanes] + span * state0
        adjoint1 = a[:, lanes].astype(F32)
        adjoint0 = weight * b[16:32, lanes] + span * adjoint1
        one = (state0 * b[0:16, lanes] + state1 * b[16:32, lanes]) * jnp.exp(-rate)
        two = weight * (state0 * b[32:48, lanes] + state1 * b[48:64, lanes])
        two = two + adjoint0 * f[32:48, lanes] + adjoint1 * f[48:64, lanes]
        two = two + BLOCK * span * (adjoint0 * state0 + adjoint1 * state1)
        both = jnp.concatenate([one, two], 0)
        high = both.astype(BF16)
        low = (both - high.astype(F32)).astype(BF16)
        shape = (LANES, groups)
        hot = (iota(shape, 1) == i * 8 + iota(shape, 0) // 16).astype(BF16)
        return total + dot(jnp.concatenate([high, low], 0), hot)

    totals = lax.fori_loop(0, chunks, chunk, jnp.zeros((64, groups), F32), unroll=8)
    totals = totals[:32] + totals[32:]
    lag = (iota((LANES, groups), 0) - (BLOCK - 1)).astype(F32)
    lags = jnp.where(lag >= 0.0, by_lag[...].T, 0.0)
    lag = jnp.maximum(lag, 0.0)
    for m in range(16):
        rate = jnp.exp(lr[m : m + 1, :])
        terms = jnp.exp(-rate * lag) * lags
        first = jnp.sum(terms, axis=0, keepdims=True)
        second = jnp.sum(terms * lag, axis=0, keepdims=True) * jnp.exp(rate)
        residue_out[m : m + 1, :] = first + totals[m : m + 1, :]
        decay = w[m : m + 1, :] * second + totals[16 + m : 17 + m, :]
        rate_out[m : m + 1, :] = decay * (-jnp.exp(-rate) * rate)


def levels_of(count):
    levels = []
    stride = 1
    while stride < count:
        size = 2 if stride == 1 else min(4, count // stride)
        levels.append((stride, size))
        stride *= size
    return levels


def after(value, *others):
    return lax.optimization_barrier((value, *others))[0]


class Prefix:
    def __init__(self, local, rate, rows, reverse):
        self.count = lax.axis_size("seq")
        self.mine = lax.axis_index("seq")
        self.local, self.rate, self.rows, self.reverse = local, rate, rows, reverse
        half = local.shape[1] // 2
        self.even = self.mine % 2 == 0
        self.half_rate = jnp.where(self.even, rate[:, :half], rate[:, half:])
        self.value = local
        self.levels = levels_of(self.count)
        self.above = 0.0
        self.low = 0.0

    def send(self, number):
        stride, size = self.levels[number]
        last = stride * size == self.count
        sign = -1 if self.reverse else 1
        self.got = []
        for h in range(1, size):
            pairs = []
            for i in range(self.count):
                there = (i // stride) % size + sign * h
                if last and not 0 <= there < size:
                    continue
                pairs.append((i, i + (there % size - (i // stride) % size) * stride))
            self.got.append(lax.ppermute(self.value, "seq", pairs))

    def join(self, number, *others):
        stride, size = self.levels[number]
        last = stride * size == self.count
        rate = self.rate if number == 0 else self.half_rate
        span = float(self.rows * stride)
        digit = (self.mine // stride) % size
        place = size - 1 - digit if self.reverse else digit
        got = self.got
        if others:
            got = [after(item, *others) for item in got]
        own = self.value.astype(F32)
        group = own * jnp.exp(-rate * (span * (size - 1 - place).astype(F32)))
        before = jnp.zeros_like(own)
        for h in range(1, size):
            item = got[h - 1].astype(F32)
            earlier = jnp.where(h <= place, 1.0, 0.0)
            before = before + item * (earlier * jnp.exp(-rate * (span * (h - 1))))
            if not last:
                away = (h - 1 - place) % size
                group = group + item * jnp.exp(-rate * (span * away.astype(F32)))
        if number == 0:
            self.near, self.place = before, place
            half = group.shape[1] // 2
            group = jnp.where(self.even, group[:, :half], group[:, half:])
        else:
            self.above = self.above + before * jnp.exp(-rate * (self.rows * self.low))
            self.low = self.low + (place * stride).astype(F32)
        self.value = group.astype(self.local.dtype)

    def swap(self):
        mine = self.above.astype(self.local.dtype)
        other = lax.ppermute(mine, "seq", [(i, i ^ 1) for i in range(self.count)])
        low = jnp.where(self.even, mine, other)
        high = jnp.where(self.even, other, mine)
        above = jnp.concatenate([low, high], 1).astype(F32)
        result = self.near + above * jnp.exp(
            -self.rate * (self.rows * self.place.astype(F32))
        )
        return result.astype(self.local.dtype)


def on_device(section_input, sent_grad, norm_gain, short_filter, log_rate, residue, skip_gain):
    x = section_input[0]
    rows, channels = x.shape
    groups = log_rate.shape[2]
    chunks = channels // LANES
    sections = lax.axis_size("section")
    count = lax.axis_size("seq")
    filt, gain, skip = short_filter.reshape(-1, 1, channels), norm_gain, skip_gain
    lr, w = log_rate[0], residue[0]

    ring = [(i, (i - 1) % sections) for i in range(sections)]
    cut = rows * 5 // 8
    g = lax.ppermute(sent_grad[0, :cut], "section", ring)
    g_rest = lax.ppermute(sent_grad[0, cut:], "section", ring)
    halo = lax.ppermute(x[rows - 8 :], "seq", [(i, i + 1) for i in range(count - 1)])

    full = lambda i: (0, 0)
    lane = lambda i: (0, i)
    block = lambda i: (i, 0, 0)
    cube = (STEP, LANES, LANES)
    tall = (STEP, LANES + 8, LANES)
    grid = (chunks // STEP,)
    table_step = min(TABLE_STEP, chunks)
    table_groups = 8 * table_step
    lc, lrw, kk, r_e, w_e = call(
        table_kernel,
        (chunks // table_step,),
        [(lr, (16, table_groups), lane), (w, (16, table_groups), lane)],
        [
            (
                (chunks, 4, LANES, LANES),
                BF16,
                (table_step, 4, LANES, LANES),
                lambda i: (i, 0, 0, 0),
            ),
            (
                (chunks, 2, BLOCK, LANES),
                BF16,
                (table_step, 2, BLOCK, LANES),
                lambda i: (i, 0, 0, 0),
            ),
            ((2, groups, LANES), F32, (2, table_groups, LANES), lambda i: (0, i, 0)),
            ((16, channels), F32, (16, table_step * LANES), lane),
            ((16, channels), F32, (16, table_step * LANES), lane),
        ],
        micros=0,
        name="tables",
    )
    wide16 = (16, WIDE)
    nrm, q, k, v, p, inside, inv, s, f = call(
        features_kernel,
        grid,
        [
            (x, (rows, channels), full),
            (halo, (8, channels), full),
            (gain, (1, WIDE), lane),
            (filt, (21, 1, WIDE), lambda i: (0, 0, i)),
            (lc, (STEP, 2, LANES, LANES), lambda i: (i, 0, 0, 0)),
            (kk, (1, 8 * STEP, LANES), lambda i: (0, i, 0)),
            (r_e, wide16, lane),
        ],
        [
            ((chunks, LANES + 8, LANES), F32, tall, block),
            ((chunks, LANES, LANES), F32, cube, block),
            ((chunks, LANES, LANES), F32, cube, block),
            ((chunks, LANES, LANES), F32, cube, block),
            ((2, chunks, LANES, LANES), BF16, (2,) + cube, lambda i: (0, i, 0, 0)),
            ((chunks, LANES, LANES), F32, cube, block),
            ((LANES + 8, LANES), F32, (LANES + 8, LANES), full),
            ((16, channels), F32, wide16, lane),
            ((64, channels), F32, (64, WIDE), lane),
        ],
        scratch=[pltpu.VMEM((LANES + 8, LANES), F32)],
        micros=0,
        name="features",
    )
    ahead = Prefix(after(s, g), r_e, rows, False)
    ahead.send(0)
    ahead.join(0)
    ahead.send(1)
    q_late = after(q, ahead.value)
    gm, a_local, b = call(
        adjoint_kernel,
        grid,
        [
            (g, (cut, WIDE), lane),
            (g_rest, (rows - cut, WIDE), lane),
            (q_late, cube, block),
            (lc, (STEP, 2, LANES, LANES), lambda i: (i, 1, 0, 0)),
            (w_e, wide16, lane),
            (r_e, wide16, lane),
        ],
        [
            ((chunks, LANES, LANES), BF16, cube, block),
            ((16, channels), BF16, wide16, lane),
            ((64, channels), F32, (64, WIDE), lane),
        ],
        micros=3,
        name="adjoint",
    )
    behind = Prefix(a_local, r_e, rows, True)
    behind.send(0)
    ahead.join(1, a_local)
    ahead.send(2)
    behind.join(0)
    behind.send(1)
    gm_late = after(gm, behind.value, ahead.value)
    back, by_lag = call(
        backward_kernel,
        grid,
        [
            (p, (2,) + cube, lambda i: (0, i, 0, 0)),
            (gm_late, cube, block),
            (kk, (1, 8 * STEP, LANES), lambda i: (1, i, 0)),
        ],
        [
            ((chunks, LANES, LANES), F32, cube, block),
            ((groups, LANES), F32, (8 * STEP, LANES), lambda i: (i, 0)),
        ],
        micros=6,
        name="backward",
    )
    behind.join(1, by_lag)
    behind.send(2)
    ahead.join(2, by_lag)
    e = after(ahead.swap(), behind.value)
    block_out, gn0, fg0 = call(
        output_kernel,
        grid,
        [
            (inside, cube, block),
            (lrw, (STEP, 1, BLOCK, LANES), lambda i: (i, 0, 0, 0)),
            (e, wide16, lane),
            (f, wide16, lane),
            (r_e, wide16, lane),
            (q, cube, block),
            (k, cube, block),
            (v, cube, block),
            (x, (rows, WIDE), lane),
            (skip, (1, WIDE), lane),
            (g, (cut, WIDE), lane),
            (g_rest, (rows - cut, WIDE), lane),
            (nrm, tall, block),
            (filt, (21, 1, WIDE), lambda i: (0, 0, i)),
        ],
        [
            ((rows, channels), BF16, (rows, WIDE), lane),
            ((chunks, LANES + 8, LANES), F32, tall, block),
            ((8, channels), F32, (8, WIDE), lane),
        ],
        scratch=[pltpu.VMEM((STEP, 1, LANES + 16, LANES), F32)],
        micros=8,
        name="output",
    )
    behind.join(2, fg0)
    a = behind.swap()
    gn, fg, hx, part = call(
        mixer_kernel,
        grid,
        [
            (back, cube, block),
            (lrw, (STEP, 1, BLOCK, LANES), lambda i: (i, 1, 0, 0)),
            (a, wide16, lane),
            (b, wide16, lambda i: (1, i)),
            (w_e, wide16, lane),
            (r_e, wide16, lane),
            (g, (cut, WIDE), lane),
            (g_rest, (rows - cut, WIDE), lane),
            (q, cube, block),
            (k, cube, block),
            (v, cube, block),
            (gn0, tall, block),
            (nrm, tall, block),
            (filt, (21, 1, WIDE), lambda i: (0, 0, i)),
            (skip, (1, WIDE), lane),
            (gain, (1, WIDE), lane),
            (x, (rows, WIDE), lane),
            (inv, (LANES + 8, LANES), full),
        ],
        [
            ((chunks, LANES, LANES), F32, cube, block),
            ((16, channels), F32, wide16, lane),
            ((LANES, LANES), F32, (LANES, LANES), full),
            ((8, channels), BF16, (8, WIDE), lane),
        ],
        scratch=[pltpu.VMEM((STEP, 2, LANES + 16, LANES), F32)],
        micros=10,
        name="mixer",
    )
    part = lax.ppermute(part, "seq", [(i + 1, i) for i in range(count - 1)])
    whole = lambda value: (value, value.shape, lambda i: (0,) * value.ndim)
    residue_grads, rate_grads = call(
        modes_kernel,
        (1,),
        [whole(value) for value in (a, b, e, f, r_e, w_e, by_lag, lr, w)],
        [((16, groups), F32, (16, groups), full)] * 2,
        micros=3,
        name="modes",
    )
    input_grad, channel_grads = call(
        final_kernel,
        grid,
        [
            (gn, cube, block),
            (g, (cut, WIDE), lane),
            (g_rest, (rows - cut, WIDE), lane),
            (fg0, (8, WIDE), lane),
            (fg, wide16, lane),
            (hx, (LANES, LANES), full),
            (part, (8, channels), full),
            (x, (rows, WIDE), lane),
            (x, (16, channels), lambda i: (rows // 16 - 1, 0)),
            (inv, (LANES + 8, LANES), full),
            (gain, (1, WIDE), lane),
            (gain, (1, channels), full),
        ],
        [
            ((rows, channels), BF16, (rows, WIDE), lane),
            ((23, 1, channels), F32, (23, 1, WIDE), lambda i: (0, 0, i)),
        ],
        scratch=[pltpu.VMEM((LANES, LANES), F32)],
        micros=4,
        name="final",
    )
    return (
        block_out[None],
        input_grad[None],
        channel_grads.reshape(1, 1, 23, channels),
        residue_grads[None, None],
        rate_grads[None, None],
    )


def solution(mesh):
    placed = (
        P("section", "seq", None),
        P("section", "seq", None),
        P("section", None),
        P("section", None, None),
        P("section", None, None),
        P("section", None, None),
        P("section", None),
    )
    return jax.shard_map(
        on_device,
        mesh=mesh,
        in_specs=placed,
        out_specs=(
            P("section", "seq", None),
            P("section", "seq", None),
            P("section", "seq", None, None),
            P("section", "seq", None, None),
            P("section", "seq", None, None),
        ),
        check_vma=False,
    )
```

time: 1030 us -> 119 us (0.12)
  the two profiles are of different devices: /device:TPU:25 before, /device:TPU:23 now
where the time goes in v1:
time: 119 us; the launch traced here: 118 us
  Pallas kernels  59.2 us (50%)
  starting transfers between devices  37.5 us (32%)
  waiting for transfers between devices  11.2 us (9%)
  local copies, waits for them, and re-layouts  5.16 us (4%)
  other arithmetic  4.31 us (4%)
    pallas_call x8, Pallas kernels, call(): pl.pallas_call(kernel, grid=grid, in_specs=[pl.BlockSpec(b, m) for _, b,...  59.2 us
    ppermute x14, starting transfers between devices, send(): self.got.append(lax.ppermute(self.value, 'seq', pairs))  24.2 us
    ppermute x1, waiting for transfers between devices, on_device(): g_rest = lax.ppermute(sent_grad[0, cut:], 'section', ring)  8.79 us
    ppermute x1, starting transfers between devices, on_device(): g = lax.ppermute(sent_grad[0, :cut], 'section', ring)  3.83 us
    ppermute x1, starting transfers between devices, on_device(): lax.ppermute(x[rows - 8:], 'seq', [(i, i + 1) for i in range(count - 1)])  3.74 us
    ppermute x2, starting transfers between devices, swap(): other = lax.ppermute(mine, 'seq', [(i, i ^ 1) for i in range(self.count)])  3.29 us
  transfers between devices with their start and end apart: 20, of which 5 were waited for; matrix products, arithmetic and copies ran while one was open for 4% of the time, Pallas kernels for 32%

profile of v1, /device:TPU:23, one launch (start us, length us, event | category | flops | bytes accessed | tf_op | source)
XLA Modules:
  0.0 118.4 jit_solution(11994907250583267136)
XLA Ops:
  0.6 1.1 slice_bitcast_fusion
  1.8 3.8 %collective-permute-start.1 = (bf16[80,4096]{1,0:T(8,128)(2,1)S(1)}, bf16[80,4096]{1,0:T(8,128)(2,1)S(1)}, u32[]{:S(2)}, u32[]{:S(2)}) collective-permute-start(bf16[80,4096]{1,0:T(8,128)(2,1)S(1)} %slice_bitcast_fusion), channel_id=1, source_target_pairs={{0,96},{32,0},{64,32},{96,64},{1,97},{33,1},{65,33},{97,65},{2,98}... | collective-permute-start | bytes 1966088 | tf_op jit(solution)/shard_map/ppermute | solution.py:508
  5.6 0.8 slice_bitcast_fusion.2
  6.4 3.7 %collective-permute-start = (bf16[8,4096]{1,0:T(8,128)(2,1)S(1)}, bf16[8,4096]{1,0:T(8,128)(2,1)S(1)}, u32[]{:S(2)}, u32[]{:S(2)}) collective-permute-start(bf16[8,4096]{1,0:T(8,128)(2,1)S(1)} %slice_bitcast_fusion.2), channel_id=1, source_target_pairs={{0,1},{1,2},{2,3},{3,4},{4,5},{5,6},{6,7},{7,8},{8,9},{9,10},{10,1... | collective-permute-start | bytes 196616 | tf_op jit(solution)/shard_map/ppermute | solution.py:510
  10.2 6.0 %tables.1 = (bf16[32,4,128,128]{3,2,1,0:T(8,128)(2,1)}, bf16[32,2,64,128]{3,2,1,0:T(8,128)(2,1)}, f32[2,256,128]{2,1,0:T(8,128)}, f32[16,4096]{1,0:T(8,128)}, f32[16,4096]{1,0:T(8,128)}) custom-call(f32[16,256]{1,0:T(8,128)} %bitcast.25, f32[16,256]{1,0:T(8,128)} %bitcast.27), custom_call_target="tpu_custom_call" | custom-call | tf_op jit(solution)/shard_map/tables/pallas_call | solution.py:34
  16.2 0.0 collective-permute-done.xh
  16.2 0.6 copy-done.3
  16.8 9.9 %features.1 = (f32[32,136,128]{2,1,0:T(8,128)}, f32[32,128,128]{2,1,0:T(8,128)}, f32[32,128,128]{2,1,0:T(8,128)}, f32[32,128,128]{2,1,0:T(8,128)}, bf16[2,32,128...) custom-call(bf16[128,4096]{1,0:T(8,128)(2,1)} %bitcast.17, ...), custom_call_target="tpu_custom_call" | custom-call | tf_op jit(solution)/shard_map/features/pallas_call | solution.py:34
  26.7 0.0 collective-permute-done.1.g
  26.8 0.1 collective-permute-start.2
  26.9 1.2 slice_bitcast_fusion.1
  28.0 0.2 collective-permute-start.4
  28.2 0.4 collective-permute-done.2
  28.6 1.0 multiply_add_fusion
  29.7 8.8 %collective-permute-done.4.g_rest = bf16[48,4096]{1,0:T(8,128)(2,1)S(1)} collective-permute-done((bf16[48,4096]{1,0:T(8,128)(2,1)S(1)}, bf16[48,4096]{1,0:T(8,128)(2,1)S(1)}, u32[]{:S(2)}, u32[]{:S(2)}) %collective-permute-start.4) | collective-permute-done | bytes 393248 | tf_op jit(solution)/shard_map/ppermute | solution.py:509
  38.5 0.8 copy-done.5
  39.2 5.2 %adjoint.1 = (bf16[32,128,128]{2,1,0:T(8,128)(2,1)}, bf16[16,4096]{1,0:T(8,128)(2,1)}, f32[64,4096]{1,0:T(8,128)}) custom-call(bf16[80,4096]{1,0:T(8,128)(2,1)} %copy-done.4, bf16[48,4096]{1,0:T(8,128)(2,1)} %copy-done.5, f32[32,128,128]{2,1,0:T(8,128)} %get-tuple-element.59.q, bf16[32,4,128,128]{3,2,1,0:T(8,128)(2,1)} %get-tuple-element.51.lc, ...), custom_call_target="tpu_custom_call" | custom-call | flops 3000000000 | bytes 10092544 | tf_op jit(solution)/shard_map/adjoint/pallas_call | solution.py:34
  44.4 1.2 collective-permute-start.8
  45.6 1.6 %collective-permute-start.5 = (f32[16,2048]{1,0:T(8,128)S(1)}, f32[16,2048]{1,0:T(8,128)S(1)}, u32[]{:S(2)}, u32[]{:S(2)}) collective-permute-start(f32[16,2048]{1,0:T(8,128)S(1)} %slice_select_fusion.1), channel_id=1, source_target_pairs={{0,4},{1,5},{2,6},{3,7},{4,0},{5,1},{6,2},{7,3},{8,12},{9,13},{10,... | collective-permute-start | bytes 393224 | tf_op jit(solution)/shard_map/ppermute | solution.py:453
  47.2 0.8 collective-permute-start.6
  48.0 1.0 fusion
  49.0 0.9 collective-permute-start.14
  49.9 1.9 %collective-permute-start.13 = (bf16[16,2048]{1,0:T(8,128)(2,1)S(1)}, bf16[16,2048]{1,0:T(8,128)(2,1)S(1)}, u32[]{:S(2)}, u32[]{:S(2)}) collective-permute-start(bf16[16,2048]{1,0:T(8,128)(2,1)S(1)} %fusion.13), channel_id=1, source_target_pairs={{0,4},{1,5},{2,6},{3,7},{4,0},{5,1},{6,2},{7,3},{8,12},{9,13},{10,... | collective-permute-start | bytes 196616 | tf_op jit(solution)/shard_map/ppermute | solution.py:453
  51.8 2.0 %collective-permute-start.12 = (bf16[16,2048]{1,0:T(8,128)(2,1)S(1)}, bf16[16,2048]{1,0:T(8,128)(2,1)S(1)}, u32[]{:S(2)}, u32[]{:S(2)}) collective-permute-start(bf16[16,2048]{1,0:T(8,128)(2,1)S(1)} %fusion.13), channel_id=1, source_target_pairs={{0,6},{1,7},{2,0},{3,1},{4,2},{5,3},{6,4},{7,5},{8,14},{9,15},{10,... | collective-permute-start | bytes 196616 | tf_op jit(solution)/shard_map/ppermute | solution.py:453
  53.8 0.9 collective-permute-done.6
  54.6 0.1 multiply_add_fusion.2
  54.7 1.3 %collective-permute-start.7 = (f32[16,2048]{1,0:T(8,128)S(1)}, f32[16,2048]{1,0:T(8,128)S(1)}, u32[]{:S(2)}, u32[]{:S(2)}) collective-permute-start(f32[16,2048]{1,0:T(8,128)S(1)} %get-tuple-element.102), channel_id=1, source_target_pairs={{0,8},{1,9},{2,10},{3,11},{4,12},{5,13},{6,14},{7,15},{8,16},{9,17... | collective-permute-start | bytes 393224 | tf_op jit(solution)/shard_map/ppermute | solution.py:453
  56.0 1.3 %collective-permute-start.9 = (f32[16,2048]{1,0:T(8,128)S(1)}, f32[16,2048]{1,0:T(8,128)S(1)}, u32[]{:S(2)}, u32[]{:S(2)}) collective-permute-start(f32[16,2048]{1,0:T(8,128)S(1)} %get-tuple-element.102), channel_id=1, source_target_pairs={{0,16},{1,17},{2,18},{3,19},{4,20},{5,21},{6,22},{7,23},{8,24},{9,... | collective-permute-start | bytes 393224 | tf_op jit(solution)/shard_map/ppermute | solution.py:453
  57.4 1.3 %collective-permute-start.10 = (f32[16,2048]{1,0:T(8,128)S(1)}, f32[16,2048]{1,0:T(8,128)S(1)}, u32[]{:S(2)}, u32[]{:S(2)}) collective-permute-start(f32[16,2048]{1,0:T(8,128)S(1)} %get-tuple-element.102), channel_id=1, source_target_pairs={{0,24},{1,25},{2,26},{3,27},{4,28},{5,29},{6,30},{7,31},{32,56},{3... | collective-permute-start | bytes 393224 | tf_op jit(solution)/shard_map/ppermute | solution.py:453
  58.7 8.6 %backward.1 = (f32[32,128,128]{2,1,0:T(8,128)}, f32[256,128]{1,0:T(8,128)}) custom-call(bf16[2,32,128,128]{3,2,1,0:T(8,128)(2,1)} %get-tuple-element.65.p, bf16[32,128,128]{2,1,0:T(8,128)(2,1)} %get-tuple-element.67.gm, f32[2,256,128]{2,1,0:T(8,128)} %get-tuple-element.52.kk), custom_call_target="tpu_custom_call" | custom-call | flops 6000000000 | bytes 5636096 | tf_op jit(solution)/shard_map/backward/pallas_call | solution.py:34
  67.2 0.2 collective-permute-done.10
  67.5 0.2 multiply_add_fusion.1
  67.7 2.6 %collective-permute-start.11 = (f32[16,2048]{1,0:T(8,128)S(1)}, f32[16,2048]{1,0:T(8,128)S(1)}, u32[]{:S(2)}, u32[]{:S(2)}) collective-permute-start(f32[16,2048]{1,0:T(8,128)S(1)} %multiply_add_fusion.1), channel_id=1, source_target_pairs={{0,1},{1,0},{2,3},{3,2},{4,5},{5,4},{6,7},{7,6},{8,9},{9,8},{10,11... | collective-permute-start | bytes 393224 | tf_op jit(solution)/shard_map/ppermute | solution.py:486
  70.3 0.1 fusion.7
  70.4 3.4 %collective-permute-start.15 = (bf16[16,2048]{1,0:T(8,128)(2,1)S(1)}, bf16[16,2048]{1,0:T(8,128)(2,1)S(1)}, u32[]{:S(2)}, u32[]{:S(2)}) collective-permute-start(bf16[16,2048]{1,0:T(8,128)(2,1)S(1)} %fusion.7), channel_id=1, source_target_pairs={{8,0},{9,1},{10,2},{11,3},{12,4},{13,5},{14,6},{15,7},{16,8},{17,9... | collective-permute-start | bytes 196616 | tf_op jit(solution)/shard_map/ppermute | solution.py:453
  73.8 7.0 %collective-permute-start.16 = (bf16[16,2048]{1,0:T(8,128)(2,1)S(1)}, bf16[16,2048]{1,0:T(8,128)(2,1)S(1)}, u32[]{:S(2)}, u32[]{:S(2)}) collective-permute-start(bf16[16,2048]{1,0:T(8,128)(2,1)S(1)} %fusion.7), channel_id=1, source_target_pairs={{16,0},{17,1},{18,2},{19,3},{20,4},{21,5},{22,6},{23,7},{24,8},{25... | collective-permute-start | bytes 196616 | tf_op jit(solution)/shard_map/ppermute | solution.py:453
  80.8 1.5 %collective-permute-start.17 = (bf16[16,2048]{1,0:T(8,128)(2,1)S(1)}, bf16[16,2048]{1,0:T(8,128)(2,1)S(1)}, u32[]{:S(2)}, u32[]{:S(2)}) collective-permute-start(bf16[16,2048]{1,0:T(8,128)(2,1)S(1)} %fusion.7), channel_id=1, source_target_pairs={{24,0},{25,1},{26,2},{27,3},{28,4},{29,5},{30,6},{31,7},{56,32},{5... | collective-permute-start | bytes 196616 | tf_op jit(solution)/shard_map/ppermute | solution.py:453
  82.4 0.8 fusion.3.e
  83.2 8.9 %output.1 = (bf16[128,4096]{1,0:T(8,128)(2,1)}, f32[32,136,128]{2,1,0:T(8,128)}, f32[8,4096]{1,0:T(8,128)}) custom-call(f32[32,128,128]{2,1,0:T(8,128)} %get-tuple-element.54.inside, bf16[32,2,64,128]{3,2,1,0:T(8,128)(2,1)} %get-tuple-element.55.lrw, f32[16,4096]{1,0:T(8,128)} %fusion.3.e, f32[64,4096]{1,0:T(8,128)} %get-tuple-element.76.f, ...), custom_call_target="tpu_custom_call" | custom-call | flops 8000000000 | bytes 19103744 | tf_op jit(solution)/shard_map/output/pallas_call | solution.py:34
  92.1 0.2 fusion.12
  92.3 0.7 collective-permute-start.18
  93.0 0.9 collective-permute-done.18
  93.9 0.8 fusion.2.a
  94.7 11.5 %mixer.1 = (f32[32,128,128]{2,1,0:T(8,128)}, f32[16,4096]{1,0:T(8,128)}, f32[128,128]{1,0:T(8,128)}, bf16[8,4096]{1,0:T(8,128)(2,1)}) custom-call(f32[32,128,128]{2,1,0:T(8,128)} %get-tuple-element.81.back, bf16[32,2,64,128]{3,2,1,0:T(8,128)(2,1)} %get-tuple-element.55.lrw, bf16[16,4096]{1,0:T(8,128)(2,1)} %fusion.2.a, f32[64,4096]{1,0:T(8,128)} %get-tuple-element.86.b, ...), custom_call_target="tpu_custom_call" | custom-call | flops 10000000000 | bytes 20631552 | tf_op jit(solution)/shard_map/mixer/pallas_call | solution.py:34
  106.2 2.3 %collective-permute-start.19 = (bf16[8,4096]{1,0:T(8,128)(2,1)}, bf16[8,4096]{1,0:T(8,128)(2,1)S(1)}, u32[]{:S(2)}, u32[]{:S(2)}) collective-permute-start(bf16[8,4096]{1,0:T(8,128)(2,1)} %get-tuple-element.92), channel_id=1, source_target_pairs={{1,0},{2,1},{3,2},{4,3},{5,4},{6,5},{7,6},{8,7},{9,8},{10,9},{11,1... | collective-permute-start | bytes 196616 | tf_op jit(solution)/shard_map/ppermute | solution.py:685
  108.5 4.2 %modes.1 = (f32[16,256]{1,0:T(8,128)}, f32[16,256]{1,0:T(8,128)}) custom-call(bf16[16,4096]{1,0:T(8,128)(2,1)} %fusion.2.a, f32[64,4096]{1,0:T(8,128)} %get-tuple-element.86.b, f32[16,4096]{1,0:T(8,128)} %fusion.3.e, f32[64,4096]{1,0:T(8,128)} %get-tuple-element.76.f, f32[16,4096]{1,0:T(8,128)} %get-tuple-element.53.r_e, f32[16,4096]{1,0:T(8,128)} %get-tuple-element.60.w_e, ...), custom_call_target="tpu_custom_call" | custom-call | flops 3000000000 | bytes 3211264 | tf_op jit(solution)/shard_map/modes/pallas_call | solution.py:34
  112.8 0.6 copy-done.6
  113.4 4.9 %final.1 = (bf16[128,4096]{1,0:T(8,128)(2,1)}, f32[23,1,4096]{2,1,0:T(1,128)}) custom-call(f32[32,128,128]{2,1,0:T(8,128)} %get-tuple-element.89.gn, bf16[80,4096]{1,0:T(8,128)(2,1)} %copy-done.4, bf16[48,4096]{1,0:T(8,128)(2,1)} %copy-done.5, f32[8,4096]{1,0:T(8,128)} %get-tuple-element.82.fg0, f32[16,4096]{1,0:T(8,128)} %get-tuple-element.90.fg, ...), custom_call_target="tpu_custom_call" | custom-call | flops 4000000000 | bytes 7294976 | tf_op jit(solution)/shard_map/final/pallas_call | solution.py:34
  (29 shorter events, 0.1 us)
Async XLA Ops:
  1.8 25.0 %collective-permute-start.1 = (bf16[80,4096]{1,0:T(8,128)(2,1)S(1)}, bf16[80,4096]{1,0:T(8,128)(2,1)S(1)}, u32[]{:S(2)}, u32[]{:S(2)}) collective-permute-start(bf16[80,4096]{1,0:T(8,128)(2,1)S(1)} %slice_bitcast_fusion), channel_id=1, source_target_pairs={{0,96},{32,0},{64,32},{96,64},{1,97},{33,1},{65,33},{97,65},{2,98}... | collective-permute-start | bytes 1966088 | tf_op jit(solution)/shard_map/ppermute | solution.py:508
  6.4 9.7 %collective-permute-start = (bf16[8,4096]{1,0:T(8,128)(2,1)S(1)}, bf16[8,4096]{1,0:T(8,128)(2,1)S(1)}, u32[]{:S(2)}, u32[]{:S(2)}) collective-permute-start(bf16[8,4096]{1,0:T(8,128)(2,1)S(1)} %slice_bitcast_fusion.2), channel_id=1, source_target_pairs={{0,1},{1,2},{2,3},{3,4},{4,5},{5,6},{6,7},{7,8},{8,9},{9,10},{10,1... | collective-permute-start | bytes 196616 | tf_op jit(solution)/shard_map/ppermute | solution.py:510
  16.2 0.6 copy-start.3
  16.8 11.8 %copy-start = (f32[16,4096]{1,0:T(8,128)S(1)}, f32[16,4096]{1,0:T(8,128)}, u32[]{:S(2)}) copy-start(f32[16,4096]{1,0:T(8,128)} %get-tuple-element.53.r_e) | copy-start | bytes 786436
  26.8 11.7 %copy-start.4 = (bf16[80,4096]{1,0:T(8,128)(2,1)}, bf16[80,4096]{1,0:T(8,128)(2,1)S(1)}, u32[]{:S(2)}) copy-start(bf16[80,4096]{1,0:T(8,128)(2,1)S(1)} %collective-permute-done.1.g) | copy-start | bytes 1966084
  26.8 1.8 %collective-permute-start.2 = (f32[16,4096]{1,0:T(8,128)}, f32[16,4096]{1,0:T(8,128)S(1)}, u32[]{:S(2)}, u32[]{:S(2)}) collective-permute-start(f32[16,4096]{1,0:T(8,128)} %get-tuple-element.57), channel_id=1, source_target_pairs={{0,1},{1,0},{2,3},{3,2},{4,5},{5,4},{6,7},{7,6},{8,9},{9,8},{10,11... | collective-permute-start | bytes 786440 | tf_op jit(solution)/shard_map/ppermute | solution.py:453
  28.0 10.4 %collective-permute-start.4 = (bf16[48,4096]{1,0:T(8,128)(2,1)S(1)}, bf16[48,4096]{1,0:T(8,128)(2,1)S(1)}, u32[]{:S(2)}, u32[]{:S(2)}) collective-permute-start(bf16[48,4096]{1,0:T(8,128)(2,1)S(1)} %slice_bitcast_fusion.1), channel_id=1, source_target_pairs={{0,96},{32,0},{64,32},{96,64},{1,97},{33,1},{65,33},{97,65},{2,98}... | collective-permute-start | bytes 1179656 | tf_op jit(solution)/shard_map/ppermute | solution.py:509
  38.4 0.8 copy-start.5
  39.2 8.8 %copy-start.1 = (f32[16,4096]{1,0:T(8,128)S(1)}, f32[16,4096]{1,0:T(8,128)}, u32[]{:S(2)}) copy-start(f32[16,4096]{1,0:T(8,128)} %get-tuple-element.53.r_e) | copy-start | bytes 786436
  44.4 3.6 %collective-permute-start.8 = (bf16[16,4096]{1,0:T(8,128)(2,1)}, bf16[16,4096]{1,0:T(8,128)(2,1)S(1)}, u32[]{:S(2)}, u32[]{:S(2)}) collective-permute-start(bf16[16,4096]{1,0:T(8,128)(2,1)} %get-tuple-element.61), channel_id=1, source_target_pairs={{0,1},{1,0},{2,3},{3,2},{4,5},{5,4},{6,7},{7,6},{8,9},{9,8},{10,11... | collective-permute-start | bytes 393224 | tf_op jit(solution)/shard_map/ppermute | solution.py:453
  45.5 6.3 %collective-permute-start.3 = (f32[16,2048]{1,0:T(8,128)S(1)}, f32[16,2048]{1,0:T(8,128)S(1)}, u32[]{:S(2)}, u32[]{:S(2)}) collective-permute-start(f32[16,2048]{1,0:T(8,128)S(1)} %slice_select_fusion.1), channel_id=1, source_target_pairs={{0,2},{1,3},{2,4},{3,5},{4,6},{5,7},{6,0},{7,1},{8,10},{9,11},{10,... | collective-permute-start | bytes 393224 | tf_op jit(solution)/shard_map/ppermute | solution.py:453
  45.6 8.2 %collective-permute-start.5 = (f32[16,2048]{1,0:T(8,128)S(1)}, f32[16,2048]{1,0:T(8,128)S(1)}, u32[]{:S(2)}, u32[]{:S(2)}) collective-permute-start(f32[16,2048]{1,0:T(8,128)S(1)} %slice_select_fusion.1), channel_id=1, source_target_pairs={{0,4},{1,5},{2,6},{3,7},{4,0},{5,1},{6,2},{7,3},{8,12},{9,13},{10,... | collective-permute-start | bytes 393224 | tf_op jit(solution)/shard_map/ppermute | solution.py:453
  47.2 7.4 %collective-permute-start.6 = (f32[16,2048]{1,0:T(8,128)S(1)}, f32[16,2048]{1,0:T(8,128)S(1)}, u32[]{:S(2)}, u32[]{:S(2)}) collective-permute-start(f32[16,2048]{1,0:T(8,128)S(1)} %slice_select_fusion.1), channel_id=1, source_target_pairs={{0,6},{1,7},{2,0},{3,1},{4,2},{5,3},{6,4},{7,5},{8,14},{9,15},{10,... | collective-permute-start | bytes 393224 | tf_op jit(solution)/shard_map/ppermute | solution.py:453
  49.0 8.3 %collective-permute-start.14 = (bf16[16,2048]{1,0:T(8,128)(2,1)S(1)}, bf16[16,2048]{1,0:T(8,128)(2,1)S(1)}, u32[]{:S(2)}, u32[]{:S(2)}) collective-permute-start(bf16[16,2048]{1,0:T(8,128)(2,1)S(1)} %fusion.13), channel_id=1, source_target_pairs={{0,2},{1,3},{2,4},{3,5},{4,6},{5,7},{6,0},{7,1},{8,10},{9,11},{10,... | collective-permute-start | bytes 196616 | tf_op jit(solution)/shard_map/ppermute | solution.py:453
  49.9 17.3 %collective-permute-start.13 = (bf16[16,2048]{1,0:T(8,128)(2,1)S(1)}, bf16[16,2048]{1,0:T(8,128)(2,1)S(1)}, u32[]{:S(2)}, u32[]{:S(2)}) collective-permute-start(bf16[16,2048]{1,0:T(8,128)(2,1)S(1)} %fusion.13), channel_id=1, source_target_pairs={{0,4},{1,5},{2,6},{3,7},{4,0},{5,1},{6,2},{7,3},{8,12},{9,13},{10,... | collective-permute-start | bytes 196616 | tf_op jit(solution)/shard_map/ppermute | solution.py:453
  51.8 15.4 %collective-permute-start.12 = (bf16[16,2048]{1,0:T(8,128)(2,1)S(1)}, bf16[16,2048]{1,0:T(8,128)(2,1)S(1)}, u32[]{:S(2)}, u32[]{:S(2)}) collective-permute-start(bf16[16,2048]{1,0:T(8,128)(2,1)S(1)} %fusion.13), channel_id=1, source_target_pairs={{0,6},{1,7},{2,0},{3,1},{4,2},{5,3},{6,4},{7,5},{8,14},{9,15},{10,... | collective-permute-start | bytes 196616 | tf_op jit(solution)/shard_map/ppermute | solution.py:453
  54.7 12.5 %collective-permute-start.7 = (f32[16,2048]{1,0:T(8,128)S(1)}, f32[16,2048]{1,0:T(8,128)S(1)}, u32[]{:S(2)}, u32[]{:S(2)}) collective-permute-start(f32[16,2048]{1,0:T(8,128)S(1)} %get-tuple-element.102), channel_id=1, source_target_pairs={{0,8},{1,9},{2,10},{3,11},{4,12},{5,13},{6,14},{7,15},{8,16},{9,17... | collective-permute-start | bytes 393224 | tf_op jit(solution)/shard_map/ppermute | solution.py:453
  56.0 11.2 %collective-permute-start.9 = (f32[16,2048]{1,0:T(8,128)S(1)}, f32[16,2048]{1,0:T(8,128)S(1)}, u32[]{:S(2)}, u32[]{:S(2)}) collective-permute-start(f32[16,2048]{1,0:T(8,128)S(1)} %get-tuple-element.102), channel_id=1, source_target_pairs={{0,16},{1,17},{2,18},{3,19},{4,20},{5,21},{6,22},{7,23},{8,24},{9,... | collective-permute-start | bytes 393224 | tf_op jit(solution)/shard_map/ppermute | solution.py:453
  57.4 10.1 %collective-permute-start.10 = (f32[16,2048]{1,0:T(8,128)S(1)}, f32[16,2048]{1,0:T(8,128)S(1)}, u32[]{:S(2)}, u32[]{:S(2)}) collective-permute-start(f32[16,2048]{1,0:T(8,128)S(1)} %get-tuple-element.102), channel_id=1, source_target_pairs={{0,24},{1,25},{2,26},{3,27},{4,28},{5,29},{6,30},{7,31},{32,56},{3... | collective-permute-start | bytes 393224 | tf_op jit(solution)/shard_map/ppermute | solution.py:453
  67.7 14.7 %collective-permute-start.11 = (f32[16,2048]{1,0:T(8,128)S(1)}, f32[16,2048]{1,0:T(8,128)S(1)}, u32[]{:S(2)}, u32[]{:S(2)}) collective-permute-start(f32[16,2048]{1,0:T(8,128)S(1)} %multiply_add_fusion.1), channel_id=1, source_target_pairs={{0,1},{1,0},{2,3},{3,2},{4,5},{5,4},{6,7},{7,6},{8,9},{9,8},{10,11... | collective-permute-start | bytes 393224 | tf_op jit(solution)/shard_map/ppermute | solution.py:486
  70.4 21.7 %collective-permute-start.15 = (bf16[16,2048]{1,0:T(8,128)(2,1)S(1)}, bf16[16,2048]{1,0:T(8,128)(2,1)S(1)}, u32[]{:S(2)}, u32[]{:S(2)}) collective-permute-start(bf16[16,2048]{1,0:T(8,128)(2,1)S(1)} %fusion.7), channel_id=1, source_target_pairs={{8,0},{9,1},{10,2},{11,3},{12,4},{13,5},{14,6},{15,7},{16,8},{17,9... | collective-permute-start | bytes 196616 | tf_op jit(solution)/shard_map/ppermute | solution.py:453
  73.8 18.3 %collective-permute-start.16 = (bf16[16,2048]{1,0:T(8,128)(2,1)S(1)}, bf16[16,2048]{1,0:T(8,128)(2,1)S(1)}, u32[]{:S(2)}, u32[]{:S(2)}) collective-permute-start(bf16[16,2048]{1,0:T(8,128)(2,1)S(1)} %fusion.7), channel_id=1, source_target_pairs={{16,0},{17,1},{18,2},{19,3},{20,4},{21,5},{22,6},{23,7},{24,8},{25... | collective-permute-start | bytes 196616 | tf_op jit(solution)/shard_map/ppermute | solution.py:453
  80.8 11.3 %collective-permute-start.17 = (bf16[16,2048]{1,0:T(8,128)(2,1)S(1)}, bf16[16,2048]{1,0:T(8,128)(2,1)S(1)}, u32[]{:S(2)}, u32[]{:S(2)}) collective-permute-start(bf16[16,2048]{1,0:T(8,128)(2,1)S(1)} %fusion.7), channel_id=1, source_target_pairs={{24,0},{25,1},{26,2},{27,3},{28,4},{29,5},{30,6},{31,7},{56,32},{5... | collective-permute-start | bytes 196616 | tf_op jit(solution)/shard_map/ppermute | solution.py:453
  83.2 10.7 %copy-start.2 = (f32[16,4096]{1,0:T(8,128)S(1)}, f32[16,4096]{1,0:T(8,128)}, u32[]{:S(2)}) copy-start(f32[16,4096]{1,0:T(8,128)} %get-tuple-element.53.r_e) | copy-start | bytes 786436
  92.3 1.6 %collective-permute-start.18 = (bf16[16,2048]{1,0:T(8,128)(2,1)S(1)}, bf16[16,2048]{1,0:T(8,128)(2,1)S(1)}, u32[]{:S(2)}, u32[]{:S(2)}) collective-permute-start(bf16[16,2048]{1,0:T(8,128)(2,1)S(1)} %fusion.12), channel_id=1, source_target_pairs={{0,1},{1,0},{2,3},{3,2},{4,5},{5,4},{6,7},{7,6},{8,9},{9,8},{10,11... | collective-permute-start | bytes 196616 | tf_op jit(solution)/shard_map/ppermute | solution.py:486
  106.2 6.5 %collective-permute-start.19 = (bf16[8,4096]{1,0:T(8,128)(2,1)}, bf16[8,4096]{1,0:T(8,128)(2,1)S(1)}, u32[]{:S(2)}, u32[]{:S(2)}) collective-permute-start(bf16[8,4096]{1,0:T(8,128)(2,1)} %get-tuple-element.92), channel_id=1, source_target_pairs={{1,0},{2,1},{3,2},{4,3},{5,4},{6,5},{7,6},{8,7},{9,8},{10,9},{11,1... | collective-permute-start | bytes 196616 | tf_op jit(solution)/shard_map/ppermute | solution.py:685
  112.8 0.6 copy-start.6

commit v2 on v1

--- a/solution.py
+++ b/solution.py
@@ -13,7 +13,7 @@
 WIDE = STEP * LANES
 BLOCK = 64
 TABLE_STEP = 16
-VMEM_LIMIT = 60 * 1024 * 1024
+VMEM_LIMIT = 20 * 1024 * 1024
 
 
 def iota(shape, axis):
@@ -72,8 +72,8 @@
     return jnp.concatenate([rows[:BLOCK], rows[BLOCK:]], 1)
 
 
-def joined(first, rest, lanes):
-    return jnp.concatenate([first[:, lanes], rest[:, lanes]], 0).astype(F32)
+def joined(parts, lanes):
+    return jnp.concatenate([part[:, lanes] for part in parts], 0).astype(F32)
 
 
 def stacked(rows):
@@ -91,7 +91,7 @@
         return jnp.where(first, high, value - high)
 
     for c in range(lc.shape[0]):
-        parts = [[] for _ in range(5)]
+        parts = [[] for _ in range(4)]
         rate_lanes = weight_lanes = None
         for g in range(8):
             at = c * 8 + g
@@ -102,9 +102,8 @@
             decay = jnp.exp(-rate)
             parts[0].append(split(end))
             parts[1].append(split((BLOCK - 1.0 - token) * end))
-            parts[2].append(split(start))
-            parts[3].append(split((token + 1.0) * start))
-            parts[4].append(decay * jnp.where(first, weight * start, end))
+            parts[2].append(jnp.where(first, 1.0, token + 1.0) * start)
+            parts[3].append(decay * jnp.where(first, weight * start, end))
             for i, value in enumerate((end, start)):
                 row = jnp.sum(weight * value, axis=0, keepdims=True)
                 kk[i, at : at + 1, :] = jnp.where(first[:1], row, 0.0)
@@ -113,9 +112,9 @@
             else:
                 rate_lanes = jnp.where(own == g, rate, rate_lanes)
                 weight_lanes = jnp.where(own == g, weight, weight_lanes)
-        for i in range(4):
+        for i in range(3):
             lc[c, i] = jnp.concatenate(parts[i], 0).astype(BF16)
-        turned = jnp.concatenate(parts[4], 0).T.astype(BF16)
+        turned = jnp.concatenate(parts[3], 0).T.astype(BF16)
         lrw[c, 0] = turned[:BLOCK]
         lrw[c, 1] = turned[BLOCK:]
         lanes = slice(c * LANES, (c + 1) * LANES)
@@ -124,7 +123,7 @@
 
 
 def features_kernel(
-    x, xh, gain, filt, lc, kk, r_e, nrm, q, k, v, p, inside, inv_out, s, f, inv
+    x, xh, gain, filt, lc, kk, r_e, nrm_out, q, k, v, p, inside, inv_out, s, f, inv, nrm
 ):
     channels = x.shape[1]
     step = pl.program_id(0)
@@ -156,9 +155,13 @@
         lanes = pl.ds(pl.multiple_of((step * STEP + c) * LANES, LANES), LANES)
         gains = gain[:, local]
         own = x[:, lanes].astype(F32) * inv[8:136, :]
-        nrm[c, 8:136, :] = (own * gains).astype(BF16).astype(F32)
+        own = (own * gains).astype(BF16)
+        nrm_out[c, 16:144, :] = own
+        nrm[c, 8:136, :] = own.astype(F32)
         halo = xh[:, lanes].astype(F32) * inv[0:8, :]
-        nrm[c, 0:8, :] = (halo * gains).astype(BF16).astype(F32)
+        halo = (halo * gains).astype(BF16).astype(F32)
+        nrm_out[c, 0:16, :] = jnp.concatenate([jnp.zeros_like(halo), halo], 0).astype(BF16)
+        nrm[c, 0:8, :] = halo
         taps = [filt[j, 0:1, local] for j in range(21)]
         for r in range(0, LANES, 32):
             total = [jnp.zeros((32, LANES), F32) for _ in range(3)]
@@ -213,7 +216,7 @@
     for r in range(0, LANES, 32):
         items = [grads[c, i, 8 + r : 40 + r, :] for i in range(count)]
         for j in range(7):
-            rows = nrm[c, 8 + r - j : 40 + r - j, :]
+            rows = nrm[c, 16 + r - j : 48 + r - j, :]
             for i in range(count):
                 term = (items[i] * rows).reshape(4, 8, LANES)
                 sums[i * 7 + j] = sums[i * 7 + j] + jnp.sum(term, axis=0)
@@ -229,19 +232,20 @@
 
 
 def output_kernel(
-    inside, lrw, e, f, r_e, q, k, v, x, skip, g, g_rest, nrm, filt, out, gn, fg, grads
+    inside, lrw, e, f, r_e, q, p, x, skip, g0, g1, g2, nrm_in, filt, out, gn, fg, grads, nrm
 ):
     clear_ends(grads, 1)
     for c in range(STEP):
+        nrm[c] = nrm_in[c].astype(F32)
         local = slice(c * LANES, (c + 1) * LANES)
         state = e[:, local]
         second = f[:, local] + jnp.exp(-float(BLOCK) * r_e[:, local]) * state
         states = jnp.concatenate([state, second], 1).astype(BF16)
         carried = stacked(dot(lrw[c, 0], by_group(states)))
-        product = k[c] * v[c]
+        product = p[0, c].astype(F32) + p[1, c].astype(F32)
         modal = inside[c] + carried + skip[:, local] * product
         query = q[c]
-        arrived = joined(g, g_rest, local)
+        arrived = joined((g0, g1, g2), local)
         out[:, local] = (x[:, local].astype(F32) + query * modal).astype(BF16)
         grads[c, 0, 8:136, :] = arrived * modal
         skip_grad = jnp.sum(arrived * query * product, axis=0, keepdims=True)
@@ -252,14 +256,18 @@
         fg[:, local] = jnp.concatenate(tap_gradients(grads, nrm, c, 1) + [skip_grad], 0)
 
 
-def adjoint_kernel(g, g_rest, q, lc, w_e, r_e, gm, a, b):
+def adjoint_kernel(g0, g1, g2, q, lc, w_e, r_e, gm, a, b):
     for c in range(STEP):
         local = slice(c * LANES, (c + 1) * LANES)
-        grad = (joined(g, g_rest, local) * q[c]).astype(BF16)
+        grad = (joined((g0, g1, g2), local) * q[c]).astype(BF16)
         gm[c] = grad
         sides = side_by_side(grad)
-        sums = dot(lc[c].reshape(2 * LANES, LANES), jnp.concatenate([sides, sides], 0))
-        starts, ramps = own_group(sums[:LANES]), own_group(sums[LANES:])
+        none = jnp.zeros_like(sides)
+        sides = jnp.concatenate(
+            [jnp.concatenate([sides, none], 1), jnp.concatenate([none, sides], 1)], 0
+        )
+        sums = own_group(dot(lc[c, 0], sides))
+        starts, ramps = sums[:, : 2 * LANES], sums[:, 2 * LANES :]
         span = jnp.exp(-float(BLOCK) * r_e[:, local])
         first = w_e[:, local] * (starts[:, :LANES] + span * starts[:, LANES:])
         a[:, local] = first.astype(BF16)
@@ -298,8 +306,8 @@
 
 
 def mixer_kernel(
-    back, lrw, a, b, w_e, r_e, g, g_rest, q, k, v, gn0, nrm, filt, skip, gain, x, inv,
-    gn, fg, hx, part, grads,
+    back, lrw, a, b, w_e, r_e, gm, k, v, gn0, nrm_in, filt, skip, gain, x, inv,
+    gn, fg, hx, part, grads, nrm,
 ):
     clear_ends(grads, 2)
 
@@ -308,13 +316,14 @@
         hx[...] = jnp.zeros_like(hx)
 
     for c in range(STEP):
+        nrm[c] = nrm_in[c].astype(F32)
         local = slice(c * LANES, (c + 1) * LANES)
         second = a[:, local].astype(F32)
         span = jnp.exp(-float(BLOCK) * r_e[:, local])
         first = w_e[:, local] * b[:, local] + span * second
         states = jnp.concatenate([first, second], 1).astype(BF16)
         carried = stacked(dot(lrw[c, 0], by_group(states)))
-        modal = joined(g, g_rest, local) * q[c]
+        modal = gm[c].astype(F32)
         product = back[c] + carried + skip[:, local] * modal
         grads[c, 0, 8:136, :] = product * v[c]
         grads[c, 1, 8:136, :] = product * k[c]
@@ -335,7 +344,7 @@
 
 
 def final_kernel(
-    gn, g, g_rest, fg0, fg, hx, part, x, x_last, inv, gain, gain_all, out, cg, mean
+    gn, g0, g1, g2, fg0, fg, hx, part, x, x_last, inv, gain, gain_all, out, cg, mean
 ):
     channels = x_last.shape[1]
     step = pl.program_id(0)
@@ -357,7 +366,7 @@
     for c in range(STEP):
         local = slice(c * LANES, (c + 1) * LANES)
         lanes = pl.ds(pl.multiple_of((step * STEP + c) * LANES, LANES), LANES)
-        arrived = joined(g, g_rest, local)
+        arrived = joined((g0, g1, g2), local)
         extra = part[:, lanes].astype(F32)
         own = gn[c]
         own = jnp.concatenate([own[:120], own[120:] + extra], 0)
@@ -425,18 +434,43 @@
     return lax.optimization_barrier((value, *others))[0]
 
 
+def shard_numbers(rows):
+    count = lax.axis_size("seq")
+    shard = lax.axis_index("seq")
+    found = {"even": shard % 2 == 0}
+    for reverse in (False, True):
+        low = 0
+        for number, (stride, size) in enumerate(levels_of(count)):
+            digit = (shard // stride) % size
+            place = size - 1 - digit if reverse else digit
+            found[reverse, number, "own"] = (rows * stride * (size - 1 - place)).astype(F32)
+            if number > 1:
+                found[reverse, number, "low"] = (rows * low).astype(F32)
+            found[reverse, number, "place"] = (rows * stride * place).astype(F32)
+            for h in range(1, size):
+                found[reverse, number, "earlier", h] = jnp.where(h <= place, 1.0, 0.0)
+                away = rows * stride * ((h - 1 - place) % size)
+                found[reverse, number, "away", h] = away.astype(F32)
+            if number:
+                low = low + place * stride
+    return found
+
+
 class Prefix:
-    def __init__(self, local, rate, rows, reverse):
+    def __init__(self, local, rate, rows, reverse, column):
         self.count = lax.axis_size("seq")
-        self.mine = lax.axis_index("seq")
         self.local, self.rate, self.rows, self.reverse = local, rate, rows, reverse
-        half = local.shape[1] // 2
-        self.even = self.mine % 2 == 0
-        self.half_rate = jnp.where(self.even, rate[:, :half], rate[:, half:])
+        self.column = column
         self.value = local
         self.levels = levels_of(self.count)
         self.above = 0.0
-        self.low = 0.0
+
+    def get(self, *name):
+        return self.column((self.reverse,) + name)
+
+    def mine(self, value):
+        half = value.shape[1] // 2
+        return jnp.where(self.column("even"), value[:, :half], value[:, half:])
 
     def send(self, number):
         stride, size = self.levels[number]
@@ -455,41 +489,37 @@
     def join(self, number, *others):
         stride, size = self.levels[number]
         last = stride * size == self.count
-        rate = self.rate if number == 0 else self.half_rate
+        rate = self.rate if number == 0 else self.mine(self.rate)
         span = float(self.rows * stride)
-        digit = (self.mine // stride) % size
-        place = size - 1 - digit if self.reverse else digit
         got = self.got
         if others:
             got = [after(item, *others) for item in got]
         own = self.value.astype(F32)
-        group = own * jnp.exp(-rate * (span * (size - 1 - place).astype(F32)))
+        group = own * jnp.exp(-rate * self.get(number, "own"))
         before = jnp.zeros_like(own)
         for h in range(1, size):
             item = got[h - 1].astype(F32)
-            earlier = jnp.where(h <= place, 1.0, 0.0)
+            earlier = self.get(number, "earlier", h)
             before = before + item * (earlier * jnp.exp(-rate * (span * (h - 1))))
             if not last:
-                away = (h - 1 - place) % size
-                group = group + item * jnp.exp(-rate * (span * away.astype(F32)))
+                group = group + item * jnp.exp(-rate * self.get(number, "away", h))
         if number == 0:
-            self.near, self.place = before, place
-            half = group.shape[1] // 2
-            group = jnp.where(self.even, group[:, :half], group[:, half:])
+            self.near = before
+            group = self.mine(group)
         else:
-            self.above = self.above + before * jnp.exp(-rate * (self.rows * self.low))
-            self.low = self.low + (place * stride).astype(F32)
+            if number > 1:
+                before = before * jnp.exp(-rate * self.get(number, "low"))
+            self.above = self.above + before
         self.value = group.astype(self.local.dtype)
 
     def swap(self):
         mine = self.above.astype(self.local.dtype)
         other = lax.ppermute(mine, "seq", [(i, i ^ 1) for i in range(self.count)])
-        low = jnp.where(self.even, mine, other)
-        high = jnp.where(self.even, other, mine)
+        even = self.column("even")
+        low = jnp.where(even, mine, other)
+        high = jnp.where(even, other, mine)
         above = jnp.concatenate([low, high], 1).astype(F32)
-        result = self.near + above * jnp.exp(
-            -self.rate * (self.rows * self.place.astype(F32))
-        )
+        result = self.near + above * jnp.exp(-self.rate * self.get(0, "place"))
         return result.astype(self.local.dtype)
 
 
@@ -501,12 +531,17 @@
     sections = lax.axis_size("section")
     count = lax.axis_size("seq")
     filt, gain, skip = short_filter.reshape(-1, 1, channels), norm_gain, skip_gain
-    lr, w = log_rate[0], residue[0]
+    names, numbers = zip(*shard_numbers(rows).items())
+    lr, w, *numbers = lax.optimization_barrier((log_rate[0], residue[0], *numbers))
+    column = dict(zip(names, numbers)).__getitem__
 
     ring = [(i, (i - 1) % sections) for i in range(sections)]
-    cut = rows * 5 // 8
-    g = lax.ppermute(sent_grad[0, :cut], "section", ring)
-    g_rest = lax.ppermute(sent_grad[0, cut:], "section", ring)
+    cuts = (0, rows * 3 // 8, rows * 7 // 8, rows)
+    g = [
+        lax.ppermute(sent_grad[0, low:high], "section", ring)
+        for low, high in zip(cuts[:-1], cuts[1:])
+    ]
+    arrived = [(item, (item.shape[0], WIDE), lambda i: (0, i)) for item in g]
     halo = lax.ppermute(x[rows - 8 :], "seq", [(i, i + 1) for i in range(count - 1)])
 
     full = lambda i: (0, 0)
@@ -514,6 +549,7 @@
     block = lambda i: (i, 0, 0)
     cube = (STEP, LANES, LANES)
     tall = (STEP, LANES + 8, LANES)
+    normal = (STEP, LANES + 16, LANES)
     grid = (chunks // STEP,)
     table_step = min(TABLE_STEP, chunks)
     table_groups = 8 * table_step
@@ -523,9 +559,9 @@
         [(lr, (16, table_groups), lane), (w, (16, table_groups), lane)],
         [
             (
-                (chunks, 4, LANES, LANES),
+                (chunks, 3, LANES, LANES),
                 BF16,
-                (table_step, 4, LANES, LANES),
+                (table_step, 3, LANES, LANES),
                 lambda i: (i, 0, 0, 0),
             ),
             (
@@ -547,7 +583,7 @@
         grid,
         [
             (x, (rows, channels), full),
-            (halo, (8, channels), full),
+            (after(halo, g[0]), (8, channels), full),
             (gain, (1, WIDE), lane),
             (filt, (21, 1, WIDE), lambda i: (0, 0, i)),
             (lc, (STEP, 2, LANES, LANES), lambda i: (i, 0, 0, 0)),
@@ -555,7 +591,7 @@
             (r_e, wide16, lane),
         ],
         [
-            ((chunks, LANES + 8, LANES), F32, tall, block),
+            ((chunks, LANES + 16, LANES), BF16, normal, block),
             ((chunks, LANES, LANES), F32, cube, block),
             ((chunks, LANES, LANES), F32, cube, block),
             ((chunks, LANES, LANES), F32, cube, block),
@@ -565,11 +601,11 @@
             ((16, channels), F32, wide16, lane),
             ((64, channels), F32, (64, WIDE), lane),
         ],
-        scratch=[pltpu.VMEM((LANES + 8, LANES), F32)],
+        scratch=[pltpu.VMEM((LANES + 8, LANES), F32), pltpu.VMEM(tall, F32)],
         micros=0,
         name="features",
     )
-    ahead = Prefix(after(s, g), r_e, rows, False)
+    ahead = Prefix(after(s, g[1]), r_e, rows, False, column)
     ahead.send(0)
     ahead.join(0)
     ahead.send(1)
@@ -578,10 +614,9 @@
         adjoint_kernel,
         grid,
         [
-            (g, (cut, WIDE), lane),
-            (g_rest, (rows - cut, WIDE), lane),
+            *arrived,
             (q_late, cube, block),
-            (lc, (STEP, 2, LANES, LANES), lambda i: (i, 1, 0, 0)),
+            (lc, (STEP, 1, LANES, LANES), lambda i: (i, 2, 0, 0)),
             (w_e, wide16, lane),
             (r_e, wide16, lane),
         ],
@@ -590,10 +625,10 @@
             ((16, channels), BF16, wide16, lane),
             ((64, channels), F32, (64, WIDE), lane),
         ],
-        micros=3,
+        micros=0,
         name="adjoint",
     )
-    behind = Prefix(a_local, r_e, rows, True)
+    behind = Prefix(after(a_local, *ahead.got), r_e, rows, True, column)
     behind.send(0)
     ahead.join(1, a_local)
     ahead.send(2)
@@ -629,13 +664,11 @@
             (f, wide16, lane),
             (r_e, wide16, lane),
             (q, cube, block),
-            (k, cube, block),
-            (v, cube, block),
+            (p, (2,) + cube, lambda i: (0, i, 0, 0)),
             (x, (rows, WIDE), lane),
             (skip, (1, WIDE), lane),
-            (g, (cut, WIDE), lane),
-            (g_rest, (rows - cut, WIDE), lane),
-            (nrm, tall, block),
+            *arrived,
+            (nrm, normal, block),
             (filt, (21, 1, WIDE), lambda i: (0, 0, i)),
         ],
         [
@@ -643,7 +676,7 @@
             ((chunks, LANES + 8, LANES), F32, tall, block),
             ((8, channels), F32, (8, WIDE), lane),
         ],
-        scratch=[pltpu.VMEM((STEP, 1, LANES + 16, LANES), F32)],
+        scratch=[pltpu.VMEM((STEP, 1, LANES + 16, LANES), F32), pltpu.VMEM(normal, F32)],
         micros=8,
         name="output",
     )
@@ -659,13 +692,11 @@
             (b, wide16, lambda i: (1, i)),
             (w_e, wide16, lane),
             (r_e, wide16, lane),
-            (g, (cut, WIDE), lane),
-            (g_rest, (rows - cut, WIDE), lane),
-            (q, cube, block),
+            (gm, cube, block),
             (k, cube, block),
             (v, cube, block),
             (gn0, tall, block),
-            (nrm, tall, block),
+            (nrm, normal, block),
             (filt, (21, 1, WIDE), lambda i: (0, 0, i)),
             (skip, (1, WIDE), lane),
             (gain, (1, WIDE), lane),
@@ -678,7 +709,7 @@
             ((LANES, LANES), F32, (LANES, LANES), full),
             ((8, channels), BF16, (8, WIDE), lane),
         ],
-        scratch=[pltpu.VMEM((STEP, 2, LANES + 16, LANES), F32)],
+        scratch=[pltpu.VMEM((STEP, 2, LANES + 16, LANES), F32), pltpu.VMEM(normal, F32)],
         micros=10,
         name="mixer",
     )
@@ -697,8 +728,7 @@
         grid,
         [
             (gn, cube, block),
-            (g, (cut, WIDE), lane),
-            (g_rest, (rows - cut, WIDE), lane),
+            *arrived,
             (fg0, (8, WIDE), lane),
             (fg, wide16, lane),
             (hx, (LANES, LANES), full),

time: 119 us -> 99.4 us (0.84)
  the two profiles are of different devices: /device:TPU:23 before, /device:TPU:25 now
where the time goes in v2:
time: 99.4 us; the launch traced here: 99.1 us
  Pallas kernels  39.8 us (40%)
  starting transfers between devices  38.4 us (39%)
  waiting for transfers between devices  14.5 us (15%)
  local copies, waits for them, and re-layouts  3.98 us (4%)
  between operations  1.31 us (1%)
  other arithmetic  1.1 us (1%)
    pallas_call x8, Pallas kernels, call(): pl.pallas_call(kernel, grid=grid, in_specs=[pl.BlockSpec(b, m) for _, b,...  39.8 us
    ppermute x14, starting transfers between devices, send(): self.got.append(lax.ppermute(self.value, 'seq', pairs))  20.4 us
    ppermute x14, waiting for transfers between devices, send(): self.got.append(lax.ppermute(self.value, 'seq', pairs))  8.03 us
    ppermute x3, starting transfers between devices, on_device(): lax.ppermute(sent_grad[0, low:high], 'section', ring)  7.5 us
    ppermute x2, starting transfers between devices, swap(): other = lax.ppermute(mine, 'seq', [(i, i ^ 1) for i in range(self.count)])  4.43 us
    ppermute x1, starting transfers between devices, on_device(): lax.ppermute(x[rows - 8:], 'seq', [(i, i + 1) for i in range(count - 1)])  3.89 us
    squeeze x3, local copies, waits for them, and re-layouts, on_device(): sent_grad[0, low:high]  3.11 us
    ppermute x1, waiting for transfers between devices, on_device(): part = lax.ppermute(part, 'seq', [(i + 1, i) for i in range(count - 1)])  3 us
  transfers between devices with their start and end apart: 21, of which 8 were waited for; matrix products, arithmetic and copies ran while one was open for 4% of the time, Pallas kernels for 28%

profile of v2, /device:TPU:25, one launch (start us, length us, event | category | flops | bytes accessed | tf_op | source)
XLA Modules:
  0.0 99.1 jit_solution(4324229776473164980)
XLA Ops:
  0.7 1.1 %slice_bitcast_fusion.1 = bf16[48,4096]{1,0:T(8,128)(2,1)S(1)} fusion(bf16[1,128,4096]{2,1,0:T(8,128)(2,1)} %param.8), kind=kLoop, calls=%fused_computation.1 | loop fusion | bytes 786432 | tf_op jit(solution)/shard_map/squeeze | solution.py:541
  1.8 3.8 %collective-permute-start.1 = (bf16[48,4096]{1,0:T(8,128)(2,1)S(1)}, bf16[48,4096]{1,0:T(8,128)(2,1)S(1)}, u32[]{:S(2)}, u32[]{:S(2)}) collective-permute-start(bf16[48,4096]{1,0:T(8,128)(2,1)S(1)} %slice_bitcast_fusion.1), channel_id=1, source_target_pairs={{0,96},{32,0},{64,32},{96,64},{1,97},{33,1},{65,33},{97,65},{2,98}... | collective-permute-start | bytes 1179656 | tf_op jit(solution)/shard_map/ppermute | solution.py:541
  5.6 1.1 %slice_bitcast_fusion = bf16[64,4096]{1,0:T(8,128)(2,1)S(1)} fusion(bf16[1,128,4096]{2,1,0:T(8,128)(2,1)} %param.8), kind=kLoop, calls=%fused_computation | loop fusion | bytes 1048576 | tf_op jit(solution)/shard_map/squeeze | solution.py:541
  6.7 0.2 collective-permute-start.2
  6.9 0.8 slice_bitcast_fusion.3
  7.8 3.9 %collective-permute-start = (bf16[8,4096]{1,0:T(8,128)(2,1)S(1)}, bf16[8,4096]{1,0:T(8,128)(2,1)S(1)}, u32[]{:S(2)}, u32[]{:S(2)}) collective-permute-start(bf16[8,4096]{1,0:T(8,128)(2,1)S(1)} %slice_bitcast_fusion.3), channel_id=1, source_target_pairs={{0,1},{1,2},{2,3},{3,4},{4,5},{5,6},{6,7},{7,8},{8,9},{9,10},{10,1... | collective-permute-start | bytes 196616 | tf_op jit(solution)/shard_map/ppermute | solution.py:545
  12.0 3.3 %tables.1 = (bf16[32,3,128,128]{3,2,1,0:T(8,128)(2,1)S(1)}, bf16[32,2,64,128]{3,2,1,0:T(8,128)(2,1)S(1)}, f32[2,256,128]{2,1,0:T(8,128)S(1)}, f32[16,4096]{1,0:T(8,128)S(1)}, f32[16,4096]{1,0:T(8,128)S(1)}) custom-call(f32[16,256]{1,0:T(8,128)S(1)} %bitcast.27, f32[16,256]{1,0:T(8,128)S(1)} %bitcast.29), custom_call_target="tpu_custom_call" | custom-call | tf_op jit(solution)/shard_map/tables/pallas_call | solution.py:34
  15.3 7.3 %features.1 = (bf16[32,144,128]{2,1,0:T(8,128)(2,1)S(1)}, f32[32,128,128]{2,1,0:T(8,128)S(1)}, f32[32,128,128]{2,1,0:T(8,128)S(1)}, f32[32,128,128]{2,1,0:T(8,12...) custom-call(bf16[128,4096]{1,0:T(8,128)(2,1)S(1)} %bitcast.19, ...), custom_call_target="tpu_custom_call" | custom-call | tf_op jit(solution)/shard_map/features/pallas_call | solution.py:34
  22.6 2.1 %collective-permute-done.2.g1 = bf16[64,4096]{1,0:T(8,128)(2,1)S(1)} collective-permute-done((bf16[64,4096]{1,0:T(8,128)(2,1)S(1)}, bf16[64,4096]{1,0:T(8,128)(2,1)S(1)}, u32[]{:S(2)}, u32[]{:S(2)}) %collective-permute-start.2) | collective-permute-done | bytes 524320 | tf_op jit(solution)/shard_map/ppermute | solution.py:541
  24.7 1.5 %collective-permute-start.3 = (f32[16,4096]{1,0:T(8,128)S(1)}, f32[16,4096]{1,0:T(8,128)S(1)}, u32[]{:S(2)}, u32[]{:S(2)}) collective-permute-start(f32[16,4096]{1,0:T(8,128)S(1)} %get-tuple-element.95), channel_id=1, source_target_pairs={{0,1},{1,0},{2,3},{3,2},{4,5},{5,4},{6,7},{7,6},{8,9},{9,8},{10,11... | collective-permute-start | bytes 786440 | tf_op jit(solution)/shard_map/ppermute | solution.py:487
  26.2 0.9 slice_bitcast_fusion.2
  27.1 3.5 %collective-permute-start.5 = (bf16[16,4096]{1,0:T(8,128)(2,1)S(1)}, bf16[16,4096]{1,0:T(8,128)(2,1)S(1)}, u32[]{:S(2)}, u32[]{:S(2)}) collective-permute-start(bf16[16,4096]{1,0:T(8,128)(2,1)S(1)} %slice_bitcast_fusion.2), channel_id=1, source_target_pairs={{0,96},{32,0},{64,32},{96,64},{1,97},{33,1},{65,33},{97,65},{2,98}... | collective-permute-start | bytes 393224 | tf_op jit(solution)/shard_map/ppermute | solution.py:541
  30.6 0.1 multiply_add_fusion
  30.7 0.1 collective-permute-start.4
  30.8 2.2 %collective-permute-start.6 = (f32[16,2048]{1,0:T(8,128)S(1)}, f32[16,2048]{1,0:T(8,128)S(1)}, u32[]{:S(2)}, u32[]{:S(2)}) collective-permute-start(f32[16,2048]{1,0:T(8,128)S(1)} %slice_select_fusion.1), channel_id=1, source_target_pairs={{0,4},{1,5},{2,6},{3,7},{4,0},{5,1},{6,2},{7,3},{8,12},{9,13},{10,... | collective-permute-start | bytes 393224 | tf_op jit(solution)/shard_map/ppermute | solution.py:487
  33.1 0.5 collective-permute-done.5.g2
  33.5 2.1 %adjoint.1 = (bf16[32,128,128]{2,1,0:T(8,128)(2,1)S(1)}, bf16[16,4096]{1,0:T(8,128)(2,1)S(1)}, f32[64,4096]{1,0:T(8,128)S(1)}) custom-call(bf16[48,4096]{1,0:T(8,128)(2,1)S(1)} %collective-permute-done.1.g0, bf16[64,4096]{1,0:T(8,128)(2,1)S(1)} %collective-permute-done.2.g1, bf16[16,4096]{1,0:T(8,128)(2,1)S(1)} %collective-permute-done.5.g2, ...), custom_call_target="tpu_custom_call" | custom-call | tf_op jit(solution)/shard_map/adjoint/pallas_call | solution.py:34
  35.7 1.4 %collective-permute-done.6 = f32[16,2048]{1,0:T(8,128)S(1)} collective-permute-done((f32[16,2048]{1,0:T(8,128)S(1)}, f32[16,2048]{1,0:T(8,128)S(1)}, u32[]{:S(2)}, u32[]{:S(2)}) %collective-permute-start.6) | collective-permute-done | bytes 131104 | tf_op jit(solution)/shard_map/ppermute | solution.py:487
  37.1 3.0 %collective-permute-done.7 = f32[16,2048]{1,0:T(8,128)S(1)} collective-permute-done((f32[16,2048]{1,0:T(8,128)S(1)}, f32[16,2048]{1,0:T(8,128)S(1)}, u32[]{:S(2)}, u32[]{:S(2)}) %collective-permute-start.7) | collective-permute-done | bytes 131104 | tf_op jit(solution)/shard_map/ppermute | solution.py:487
  40.1 1.0 %collective-permute-start.9 = (bf16[16,4096]{1,0:T(8,128)(2,1)S(1)}, bf16[16,4096]{1,0:T(8,128)(2,1)S(1)}, u32[]{:S(2)}, u32[]{:S(2)}) collective-permute-start(bf16[16,4096]{1,0:T(8,128)(2,1)S(1)} %get-tuple-element.116), channel_id=1, source_target_pairs={{0,1},{1,0},{2,3},{3,2},{4,5},{5,4},{6,7},{7,6},{8,9},{9,8},{10,11... | collective-permute-start | bytes 393224 | tf_op jit(solution)/shard_map/ppermute | solution.py:487
  41.1 0.1 multiply_add_fusion.2
  41.2 3.1 %collective-permute-start.8 = (f32[16,2048]{1,0:T(8,128)S(1)}, f32[16,2048]{1,0:T(8,128)S(1)}, u32[]{:S(2)}, u32[]{:S(2)}) collective-permute-start(f32[16,2048]{1,0:T(8,128)S(1)} %get-tuple-element.172), channel_id=1, source_target_pairs={{0,8},{1,9},{2,10},{3,11},{4,12},{5,13},{6,14},{7,15},{8,16},{9,17... | collective-permute-start | bytes 393224 | tf_op jit(solution)/shard_map/ppermute | solution.py:487
  44.4 4.4 %collective-permute-start.10 = (f32[16,2048]{1,0:T(8,128)S(1)}, f32[16,2048]{1,0:T(8,128)S(1)}, u32[]{:S(2)}, u32[]{:S(2)}) collective-permute-start(f32[16,2048]{1,0:T(8,128)S(1)} %get-tuple-element.172), channel_id=1, source_target_pairs={{0,16},{1,17},{2,18},{3,19},{4,20},{5,21},{6,22},{7,23},{8,24},{9,... | collective-permute-start | bytes 393224 | tf_op jit(solution)/shard_map/ppermute | solution.py:487
  48.7 1.3 %collective-permute-start.11 = (f32[16,2048]{1,0:T(8,128)S(1)}, f32[16,2048]{1,0:T(8,128)S(1)}, u32[]{:S(2)}, u32[]{:S(2)}) collective-permute-start(f32[16,2048]{1,0:T(8,128)S(1)} %get-tuple-element.172), channel_id=1, source_target_pairs={{0,24},{1,25},{2,26},{3,27},{4,28},{5,29},{6,30},{7,31},{32,56},{3... | collective-permute-start | bytes 393224 | tf_op jit(solution)/shard_map/ppermute | solution.py:487
  50.0 0.1 fusion
  50.2 0.9 collective-permute-start.15
  51.0 1.7 %collective-permute-start.14 = (bf16[16,2048]{1,0:T(8,128)(2,1)S(1)}, bf16[16,2048]{1,0:T(8,128)(2,1)S(1)}, u32[]{:S(2)}, u32[]{:S(2)}) collective-permute-start(bf16[16,2048]{1,0:T(8,128)(2,1)S(1)} %fusion.12), channel_id=1, source_target_pairs={{0,4},{1,5},{2,6},{3,7},{4,0},{5,1},{6,2},{7,3},{8,12},{9,13},{10,... | collective-permute-start | bytes 196616 | tf_op jit(solution)/shard_map/ppermute | solution.py:487
  52.7 6.8 %backward.1 = (f32[32,128,128]{2,1,0:T(8,128)S(1)}, f32[256,128]{1,0:T(8,128)S(1)}) custom-call(bf16[2,32,128,128]{3,2,1,0:T(8,128)(2,1)S(1)} %get-tuple-element.114.p, bf16[32,128,128]{2,1,0:T(8,128)(2,1)S(1)} %get-tuple-element.119.gm, f32[2,256,128]{2,1,0:T(8,128)S(1)} %get-tuple-element.90.kk), custom_call_target="tpu_custom_call" | custom-call | flops 6000000000 | bytes 5636096 | tf_op jit(solution)/shard_map/backward/pallas_call | solution.py:34
  59.6 0.1 collective-permute-start.13
  59.7 0.2 multiply_add_fusion.1
  59.9 1.3 %collective-permute-start.12 = (f32[16,2048]{1,0:T(8,128)S(1)}, f32[16,2048]{1,0:T(8,128)S(1)}, u32[]{:S(2)}, u32[]{:S(2)}) collective-permute-start(f32[16,2048]{1,0:T(8,128)S(1)} %multiply_add_fusion.1), channel_id=1, source_target_pairs={{0,1},{1,0},{2,3},{3,2},{4,5},{5,4},{6,7},{7,6},{8,9},{9,8},{10,11... | collective-permute-start | bytes 393224 | tf_op jit(solution)/shard_map/ppermute | solution.py:517
  61.2 2.8 %collective-permute-done.13 = bf16[16,2048]{1,0:T(8,128)(2,1)S(1)} collective-permute-done((bf16[16,2048]{1,0:T(8,128)(2,1)S(1)}, bf16[16,2048]{1,0:T(8,128)(2,1)S(1)}, u32[]{:S(2)}, u32[]{:S(2)}) %collective-permute-start.13) | collective-permute-done | bytes 65568 | tf_op jit(solution)/shard_map/ppermute | solution.py:487
  64.0 0.1 fusion.7
  64.1 1.3 %collective-permute-start.16 = (bf16[16,2048]{1,0:T(8,128)(2,1)S(1)}, bf16[16,2048]{1,0:T(8,128)(2,1)S(1)}, u32[]{:S(2)}, u32[]{:S(2)}) collective-permute-start(bf16[16,2048]{1,0:T(8,128)(2,1)S(1)} %fusion.7), channel_id=1, source_target_pairs={{8,0},{9,1},{10,2},{11,3},{12,4},{13,5},{14,6},{15,7},{16,8},{17,9... | collective-permute-start | bytes 196616 | tf_op jit(solution)/shard_map/ppermute | solution.py:487
  65.4 1.3 %collective-permute-start.17 = (bf16[16,2048]{1,0:T(8,128)(2,1)S(1)}, bf16[16,2048]{1,0:T(8,128)(2,1)S(1)}, u32[]{:S(2)}, u32[]{:S(2)}) collective-permute-start(bf16[16,2048]{1,0:T(8,128)(2,1)S(1)} %fusion.7), channel_id=1, source_target_pairs={{16,0},{17,1},{18,2},{19,3},{20,4},{21,5},{22,6},{23,7},{24,8},{25... | collective-permute-start | bytes 196616 | tf_op jit(solution)/shard_map/ppermute | solution.py:487
  66.7 1.5 %collective-permute-start.18 = (bf16[16,2048]{1,0:T(8,128)(2,1)S(1)}, bf16[16,2048]{1,0:T(8,128)(2,1)S(1)}, u32[]{:S(2)}, u32[]{:S(2)}) collective-permute-start(bf16[16,2048]{1,0:T(8,128)(2,1)S(1)} %fusion.7), channel_id=1, source_target_pairs={{24,0},{25,1},{26,2},{27,3},{28,4},{29,5},{30,6},{31,7},{56,32},{5... | collective-permute-start | bytes 196616 | tf_op jit(solution)/shard_map/ppermute | solution.py:487
  68.2 0.1 fusion.3.e
  68.4 6.3 %output.1 = (bf16[128,4096]{1,0:T(8,128)(2,1)}, f32[32,136,128]{2,1,0:T(8,128)S(1)}, f32[8,4096]{1,0:T(8,128)S(1)}) custom-call(f32[32,128,128]{2,1,0:T(8,128)S(1)} %get-tuple-element.92.inside, bf16[32,2,64,128]{3,2,1,0:T(8,128)(2,1)S(1)} %get-tuple-element.93.lrw, f32[16,4096]{1,0:T(8,128)S(1)} %fusion.3.e, f32[64,4096]{1,0:T(8,128)S(1)} %get-tuple-element.137.f, ...), custom_call_target="tpu_custom_call" | custom-call | flops 8000000000 | bytes 15958016 | tf_op jit(solution)/shard_map/output/pallas_call | solution.py:34
  74.6 0.7 collective-permute-done.18
  75.4 0.2 fusion.11
  75.5 3.2 %collective-permute-start.19 = (bf16[16,2048]{1,0:T(8,128)(2,1)S(1)}, bf16[16,2048]{1,0:T(8,128)(2,1)S(1)}, u32[]{:S(2)}, u32[]{:S(2)}) collective-permute-start(bf16[16,2048]{1,0:T(8,128)(2,1)S(1)} %fusion.11), channel_id=1, source_target_pairs={{0,1},{1,0},{2,3},{3,2},{4,5},{5,4},{6,7},{7,6},{8,9},{9,8},{10,11... | collective-permute-start | bytes 196616 | tf_op jit(solution)/shard_map/ppermute | solution.py:517
  78.7 0.9 collective-permute-done.19
  79.6 0.1 fusion.2.a
  79.8 9.0 %mixer.1 = (f32[32,128,128]{2,1,0:T(8,128)S(1)}, f32[16,4096]{1,0:T(8,128)S(1)}, f32[128,128]{1,0:T(8,128)S(1)}, bf16[8,4096]{1,0:T(8,128)(2,1)S(1)}) custom-call(f32[32,128,128]{2,1,0:T(8,128)S(1)} %get-tuple-element.140.back, bf16[32,2,64,128]{3,2,1,0:T(8,128)(2,1)S(1)} %get-tuple-element.93.lrw, bf16[16,4096]{1,0:T(8,128)(2,1)S(1)} %fusion.2.a, ...), custom_call_target="tpu_custom_call" | custom-call | flops 10000000000 | bytes 17485824 | tf_op jit(solution)/shard_map/mixer/pallas_call | solution.py:34
  88.7 2.3 %collective-permute-start.20 = (bf16[8,4096]{1,0:T(8,128)(2,1)S(1)}, bf16[8,4096]{1,0:T(8,128)(2,1)S(1)}, u32[]{:S(2)}, u32[]{:S(2)}) collective-permute-start(bf16[8,4096]{1,0:T(8,128)(2,1)S(1)} %get-tuple-element.162), channel_id=1, source_target_pairs={{1,0},{2,1},{3,2},{4,3},{5,4},{6,5},{7,6},{8,7},{9,8},{10,9},{11,1... | collective-permute-start | bytes 196616 | tf_op jit(solution)/shard_map/ppermute | solution.py:716
  91.0 2.4 %modes.1 = (f32[16,256]{1,0:T(8,128)}, f32[16,256]{1,0:T(8,128)}) custom-call(bf16[16,4096]{1,0:T(8,128)(2,1)S(1)} %fusion.2.a, f32[64,4096]{1,0:T(8,128)S(1)} %get-tuple-element.154.b, f32[16,4096]{1,0:T(8,128)S(1)} %fusion.3.e, f32[64,4096]{1,0:T(8,128)S(1)} %get-tuple-element.137.f, f32[16,4096]{1,0:T(8,128)S(1)} %get-tuple-element.91.r_e, ...), custom_call_target="tpu_custom_call" | custom-call | flops 3000000000 | bytes 3211264 | tf_op jit(solution)/shard_map/modes/pallas_call | solution.py:34
  93.4 3.0 %collective-permute-done.20.part = bf16[8,4096]{1,0:T(8,128)(2,1)S(1)} collective-permute-done((bf16[8,4096]{1,0:T(8,128)(2,1)S(1)}, bf16[8,4096]{1,0:T(8,128)(2,1)S(1)}, u32[]{:S(2)}, u32[]{:S(2)}) %collective-permute-start.20) | collective-permute-done | bytes 65568 | tf_op jit(solution)/shard_map/ppermute | solution.py:716
  96.4 2.6 %final.1 = (bf16[128,4096]{1,0:T(8,128)(2,1)}, f32[23,1,4096]{2,1,0:T(1,128)}) custom-call(f32[32,128,128]{2,1,0:T(8,128)S(1)} %get-tuple-element.159.gn, bf16[48,4096]{1,0:T(8,128)(2,1)S(1)} %collective-permute-done.1.g0, bf16[64,4096]{1,0:T(8,128)(2,1)S(1)} %collective-permute-done.2.g1, bf16[16,4096]{1,0:T(8,128)(2,1)S(1)} %collective-permute-done.5.g2, ...), custom_call_target="tpu_custom_call" | custom-call | flops 4000000000 | bytes 7294976 | tf_op jit(solution)/shard_map/final/pallas_call | solution.py:34
  (30 shorter events, 0.1 us)
Async XLA Ops:
  0.6 14.6 %copy-start = (bf16[1,128,4096]{2,1,0:T(8,128)(2,1)S(1)}, bf16[1,128,4096]{2,1,0:T(8,128)(2,1)}, u32[]{:S(2)}) copy-start(bf16[1,128,4096]{2,1,0:T(8,128)(2,1)} %param.7) | copy-start | bytes 3145732
  0.6 11.3 %copy-start.3 = (f32[1,16,256]{2,1,0:T(8,128)S(1)}, f32[1,16,256]{2,1,0:T(8,128)}, u32[]{:S(2)}) copy-start(f32[1,16,256]{2,1,0:T(8,128)} %param.11) | copy-start | bytes 49156
  0.7 11.3 %copy-start.4 = (f32[1,16,256]{2,1,0:T(8,128)S(1)}, f32[1,16,256]{2,1,0:T(8,128)}, u32[]{:S(2)}) copy-start(f32[1,16,256]{2,1,0:T(8,128)} %param.12) | copy-start | bytes 49156
  0.7 14.6 %copy-start.1 = (f32[1,21,4096]{2,0,1:T(1,128)S(1)}, f32[1,21,4096]{2,0,1:T(1,128)}, u32[]{:S(2)}) copy-start(f32[1,21,4096]{2,0,1:T(1,128)} %param.10) | copy-start | bytes 1032196
  0.7 14.6 %copy-start.2 = (f32[1,4096]{1,0:T(1,128)S(1)}, f32[1,4096]{1,0:T(1,128)}, u32[]{:S(2)}) copy-start(f32[1,4096]{1,0:T(1,128)} %gain_all.1) | copy-start | bytes 49156
  1.8 13.5 %collective-permute-start.1 = (bf16[48,4096]{1,0:T(8,128)(2,1)S(1)}, bf16[48,4096]{1,0:T(8,128)(2,1)S(1)}, u32[]{:S(2)}, u32[]{:S(2)}) collective-permute-start(bf16[48,4096]{1,0:T(8,128)(2,1)S(1)} %slice_bitcast_fusion.1), channel_id=1, source_target_pairs={{0,96},{32,0},{64,32},{96,64},{1,97},{33,1},{65,33},{97,65},{2,98}... | collective-permute-start | bytes 1179656 | tf_op jit(solution)/shard_map/ppermute | solution.py:541
  6.7 17.9 %collective-permute-start.2 = (bf16[64,4096]{1,0:T(8,128)(2,1)S(1)}, bf16[64,4096]{1,0:T(8,128)(2,1)S(1)}, u32[]{:S(2)}, u32[]{:S(2)}) collective-permute-start(bf16[64,4096]{1,0:T(8,128)(2,1)S(1)} %slice_bitcast_fusion), channel_id=1, source_target_pairs={{0,96},{32,0},{64,32},{96,64},{1,97},{33,1},{65,33},{97,65},{2,98}... | collective-permute-start | bytes 1572872 | tf_op jit(solution)/shard_map/ppermute | solution.py:541
  7.8 7.5 %collective-permute-start = (bf16[8,4096]{1,0:T(8,128)(2,1)S(1)}, bf16[8,4096]{1,0:T(8,128)(2,1)S(1)}, u32[]{:S(2)}, u32[]{:S(2)}) collective-permute-start(bf16[8,4096]{1,0:T(8,128)(2,1)S(1)} %slice_bitcast_fusion.3), channel_id=1, source_target_pairs={{0,1},{1,2},{2,3},{3,4},{4,5},{5,6},{6,7},{7,8},{8,9},{9,10},{10,1... | collective-permute-start | bytes 196616 | tf_op jit(solution)/shard_map/ppermute | solution.py:545
  24.7 5.9 %collective-permute-start.3 = (f32[16,4096]{1,0:T(8,128)S(1)}, f32[16,4096]{1,0:T(8,128)S(1)}, u32[]{:S(2)}, u32[]{:S(2)}) collective-permute-start(f32[16,4096]{1,0:T(8,128)S(1)} %get-tuple-element.95), channel_id=1, source_target_pairs={{0,1},{1,0},{2,3},{3,2},{4,5},{5,4},{6,7},{7,6},{8,9},{9,8},{10,11... | collective-permute-start | bytes 786440 | tf_op jit(solution)/shard_map/ppermute | solution.py:487
  27.1 6.4 %collective-permute-start.5 = (bf16[16,4096]{1,0:T(8,128)(2,1)S(1)}, bf16[16,4096]{1,0:T(8,128)(2,1)S(1)}, u32[]{:S(2)}, u32[]{:S(2)}) collective-permute-start(bf16[16,4096]{1,0:T(8,128)(2,1)S(1)} %slice_bitcast_fusion.2), channel_id=1, source_target_pairs={{0,96},{32,0},{64,32},{96,64},{1,97},{33,1},{65,33},{97,65},{2,98}... | collective-permute-start | bytes 393224 | tf_op jit(solution)/shard_map/ppermute | solution.py:541
  30.7 4.9 %collective-permute-start.4 = (f32[16,2048]{1,0:T(8,128)S(1)}, f32[16,2048]{1,0:T(8,128)S(1)}, u32[]{:S(2)}, u32[]{:S(2)}) collective-permute-start(f32[16,2048]{1,0:T(8,128)S(1)} %slice_select_fusion.1), channel_id=1, source_target_pairs={{0,2},{1,3},{2,4},{3,5},{4,6},{5,7},{6,0},{7,1},{8,10},{9,11},{10,... | collective-permute-start | bytes 393224 | tf_op jit(solution)/shard_map/ppermute | solution.py:487
  30.8 6.2 %collective-permute-start.6 = (f32[16,2048]{1,0:T(8,128)S(1)}, f32[16,2048]{1,0:T(8,128)S(1)}, u32[]{:S(2)}, u32[]{:S(2)}) collective-permute-start(f32[16,2048]{1,0:T(8,128)S(1)} %slice_select_fusion.1), channel_id=1, source_target_pairs={{0,4},{1,5},{2,6},{3,7},{4,0},{5,1},{6,2},{7,3},{8,12},{9,13},{10,... | collective-permute-start | bytes 393224 | tf_op jit(solution)/shard_map/ppermute | solution.py:487
  33.0 7.0 %collective-permute-start.7 = (f32[16,2048]{1,0:T(8,128)S(1)}, f32[16,2048]{1,0:T(8,128)S(1)}, u32[]{:S(2)}, u32[]{:S(2)}) collective-permute-start(f32[16,2048]{1,0:T(8,128)S(1)} %slice_select_fusion.1), channel_id=1, source_target_pairs={{0,6},{1,7},{2,0},{3,1},{4,2},{5,3},{6,4},{7,5},{8,14},{9,15},{10,... | collective-permute-start | bytes 393224 | tf_op jit(solution)/shard_map/ppermute | solution.py:487
  40.1 9.9 %collective-permute-start.9 = (bf16[16,4096]{1,0:T(8,128)(2,1)S(1)}, bf16[16,4096]{1,0:T(8,128)(2,1)S(1)}, u32[]{:S(2)}, u32[]{:S(2)}) collective-permute-start(bf16[16,4096]{1,0:T(8,128)(2,1)S(1)} %get-tuple-element.116), channel_id=1, source_target_pairs={{0,1},{1,0},{2,3},{3,2},{4,5},{5,4},{6,7},{7,6},{8,9},{9,8},{10,11... | collective-permute-start | bytes 393224 | tf_op jit(solution)/shard_map/ppermute | solution.py:487
  41.2 18.4 %collective-permute-start.8 = (f32[16,2048]{1,0:T(8,128)S(1)}, f32[16,2048]{1,0:T(8,128)S(1)}, u32[]{:S(2)}, u32[]{:S(2)}) collective-permute-start(f32[16,2048]{1,0:T(8,128)S(1)} %get-tuple-element.172), channel_id=1, source_target_pairs={{0,8},{1,9},{2,10},{3,11},{4,12},{5,13},{6,14},{7,15},{8,16},{9,17... | collective-permute-start | bytes 393224 | tf_op jit(solution)/shard_map/ppermute | solution.py:487
  44.4 15.3 %collective-permute-start.10 = (f32[16,2048]{1,0:T(8,128)S(1)}, f32[16,2048]{1,0:T(8,128)S(1)}, u32[]{:S(2)}, u32[]{:S(2)}) collective-permute-start(f32[16,2048]{1,0:T(8,128)S(1)} %get-tuple-element.172), channel_id=1, source_target_pairs={{0,16},{1,17},{2,18},{3,19},{4,20},{5,21},{6,22},{7,23},{8,24},{9,... | collective-permute-start | bytes 393224 | tf_op jit(solution)/shard_map/ppermute | solution.py:487
  48.7 11.0 %collective-permute-start.11 = (f32[16,2048]{1,0:T(8,128)S(1)}, f32[16,2048]{1,0:T(8,128)S(1)}, u32[]{:S(2)}, u32[]{:S(2)}) collective-permute-start(f32[16,2048]{1,0:T(8,128)S(1)} %get-tuple-element.172), channel_id=1, source_target_pairs={{0,24},{1,25},{2,26},{3,27},{4,28},{5,29},{6,30},{7,31},{32,56},{3... | collective-permute-start | bytes 393224 | tf_op jit(solution)/shard_map/ppermute | solution.py:487
  50.2 11.0 %collective-permute-start.15 = (bf16[16,2048]{1,0:T(8,128)(2,1)S(1)}, bf16[16,2048]{1,0:T(8,128)(2,1)S(1)}, u32[]{:S(2)}, u32[]{:S(2)}) collective-permute-start(bf16[16,2048]{1,0:T(8,128)(2,1)S(1)} %fusion.12), channel_id=1, source_target_pairs={{0,2},{1,3},{2,4},{3,5},{4,6},{5,7},{6,0},{7,1},{8,10},{9,11},{10,... | collective-permute-start | bytes 196616 | tf_op jit(solution)/shard_map/ppermute | solution.py:487
  51.0 10.1 %collective-permute-start.14 = (bf16[16,2048]{1,0:T(8,128)(2,1)S(1)}, bf16[16,2048]{1,0:T(8,128)(2,1)S(1)}, u32[]{:S(2)}, u32[]{:S(2)}) collective-permute-start(bf16[16,2048]{1,0:T(8,128)(2,1)S(1)} %fusion.12), channel_id=1, source_target_pairs={{0,4},{1,5},{2,6},{3,7},{4,0},{5,1},{6,2},{7,3},{8,12},{9,13},{10,... | collective-permute-start | bytes 196616 | tf_op jit(solution)/shard_map/ppermute | solution.py:487
  59.6 8.8 %copy-start.5 = (f32[1,4096]{1,0:T(1,128)S(1)}, f32[1,4096]{1,0:T(1,128)}, u32[]{:S(2)}) copy-start(f32[1,4096]{1,0:T(1,128)} %skip.3) | copy-start | bytes 49156
  59.6 4.4 %collective-permute-start.13 = (bf16[16,2048]{1,0:T(8,128)(2,1)S(1)}, bf16[16,2048]{1,0:T(8,128)(2,1)S(1)}, u32[]{:S(2)}, u32[]{:S(2)}) collective-permute-start(bf16[16,2048]{1,0:T(8,128)(2,1)S(1)} %fusion.12), channel_id=1, source_target_pairs={{0,6},{1,7},{2,0},{3,1},{4,2},{5,3},{6,4},{7,5},{8,14},{9,15},{10,... | collective-permute-start | bytes 196616 | tf_op jit(solution)/shard_map/ppermute | solution.py:487
  59.9 8.3 %collective-permute-start.12 = (f32[16,2048]{1,0:T(8,128)S(1)}, f32[16,2048]{1,0:T(8,128)S(1)}, u32[]{:S(2)}, u32[]{:S(2)}) collective-permute-start(f32[16,2048]{1,0:T(8,128)S(1)} %multiply_add_fusion.1), channel_id=1, source_target_pairs={{0,1},{1,0},{2,3},{3,2},{4,5},{5,4},{6,7},{7,6},{8,9},{9,8},{10,11... | collective-permute-start | bytes 393224 | tf_op jit(solution)/shard_map/ppermute | solution.py:517
  64.1 10.5 %collective-permute-start.16 = (bf16[16,2048]{1,0:T(8,128)(2,1)S(1)}, bf16[16,2048]{1,0:T(8,128)(2,1)S(1)}, u32[]{:S(2)}, u32[]{:S(2)}) collective-permute-start(bf16[16,2048]{1,0:T(8,128)(2,1)S(1)} %fusion.7), channel_id=1, source_target_pairs={{8,0},{9,1},{10,2},{11,3},{12,4},{13,5},{14,6},{15,7},{16,8},{17,9... | collective-permute-start | bytes 196616 | tf_op jit(solution)/shard_map/ppermute | solution.py:487
  65.4 9.2 %collective-permute-start.17 = (bf16[16,2048]{1,0:T(8,128)(2,1)S(1)}, bf16[16,2048]{1,0:T(8,128)(2,1)S(1)}, u32[]{:S(2)}, u32[]{:S(2)}) collective-permute-start(bf16[16,2048]{1,0:T(8,128)(2,1)S(1)} %fusion.7), channel_id=1, source_target_pairs={{16,0},{17,1},{18,2},{19,3},{20,4},{21,5},{22,6},{23,7},{24,8},{25... | collective-permute-start | bytes 196616 | tf_op jit(solution)/shard_map/ppermute | solution.py:487
  66.7 8.7 %collective-permute-start.18 = (bf16[16,2048]{1,0:T(8,128)(2,1)S(1)}, bf16[16,2048]{1,0:T(8,128)(2,1)S(1)}, u32[]{:S(2)}, u32[]{:S(2)}) collective-permute-start(bf16[16,2048]{1,0:T(8,128)(2,1)S(1)} %fusion.7), channel_id=1, source_target_pairs={{24,0},{25,1},{26,2},{27,3},{28,4},{29,5},{30,6},{31,7},{56,32},{5... | collective-permute-start | bytes 196616 | tf_op jit(solution)/shard_map/ppermute | solution.py:487
  75.5 4.1 %collective-permute-start.19 = (bf16[16,2048]{1,0:T(8,128)(2,1)S(1)}, bf16[16,2048]{1,0:T(8,128)(2,1)S(1)}, u32[]{:S(2)}, u32[]{:S(2)}) collective-permute-start(bf16[16,2048]{1,0:T(8,128)(2,1)S(1)} %fusion.11), channel_id=1, source_target_pairs={{0,1},{1,0},{2,3},{3,2},{4,5},{5,4},{6,7},{7,6},{8,9},{9,8},{10,11... | collective-permute-start | bytes 196616 | tf_op jit(solution)/shard_map/ppermute | solution.py:517
  88.7 7.7 %collective-permute-start.20 = (bf16[8,4096]{1,0:T(8,128)(2,1)S(1)}, bf16[8,4096]{1,0:T(8,128)(2,1)S(1)}, u32[]{:S(2)}, u32[]{:S(2)}) collective-permute-start(bf16[8,4096]{1,0:T(8,128)(2,1)S(1)} %get-tuple-element.162), channel_id=1, source_target_pairs={{1,0},{2,1},{3,2},{4,3},{5,4},{6,5},{7,6},{8,7},{9,8},{10,9},{11,1... | collective-permute-start | bytes 196616 | tf_op jit(solution)/shard_map/ppermute | solution.py:716

commit v3 on v2

--- a/solution.py
+++ b/solution.py
@@ -275,13 +275,33 @@
         b[32:64, local] = stacked(ramps)
 
 
-def backward_kernel(p, gm, kk, back, by_lag):
-    first = iota((BLOCK, LANES), 1) < BLOCK
+def lags_kernel(p, gm, by_lag):
+    first = iota((1, LANES), 1) < BLOCK
+    shape = (BLOCK, LANES)
+    causal = iota(shape, 1) % BLOCK + iota(shape, 0) >= BLOCK - 1
     both = iota((LANES, LANES), 0) + iota((LANES, LANES), 1)
     same = iota((LANES, LANES), 0) // BLOCK == iota((LANES, LANES), 1) // BLOCK
     flip = (same & (both % BLOCK == BLOCK - 1)).astype(BF16)
     for c in range(STEP):
         grads = by_group(side_by_side(gm[c]))
+        sides = jnp.concatenate([side_by_side(p[0, c]), side_by_side(p[1, c])], 0)
+        sides = dot(flip, sides).astype(BF16)
+        crossed = lax.dot_general(
+            sides, grads, (((1,), (1,)), ((), ())), preferred_element_type=F32
+        )
+        crossed = crossed[:BLOCK] + crossed[BLOCK:]
+        for g in range(0, 8, 2):
+            tile = jnp.where(causal, crossed[:, g * BLOCK : (g + 2) * BLOCK], 0.0)
+            tile = pltpu.roll(tile, BLOCK + 1, 1, stride=1, stride_axis=0)
+            tile = jnp.sum(tile, axis=0, keepdims=True)
+            at = c * 8 + g
+            by_lag[at : at + 1, :] = jnp.where(first, tile, 0.0)
+            by_lag[at + 1 : at + 2, :] = jnp.where(first, pltpu.roll(tile, BLOCK, 1), 0.0)
+
+
+def backward_kernel(gm, kk, back):
+    first = iota((BLOCK, LANES), 1) < BLOCK
+    for c in range(STEP):
         tiles = []
         for g in range(0, 8, 2):
             even, odd = (
@@ -291,18 +311,7 @@
             even = pltpu.roll(even, 0, 1, stride=1, stride_axis=0)
             odd = pltpu.roll(odd, BLOCK, 1, stride=1, stride_axis=0)
             tiles.append(jnp.where(first, even, odd).astype(BF16))
-        back[c] = stacked(dot(jnp.concatenate(tiles, 1), grads))
-        sides = jnp.concatenate([side_by_side(p[0, c]), side_by_side(p[1, c])], 0)
-        sides = dot(flip, sides).astype(BF16)
-        crossed = lax.dot_general(
-            sides, grads, (((1,), (1,)), ((), ())), preferred_element_type=F32
-        )
-        crossed = crossed[:BLOCK] + crossed[BLOCK:]
-        for g in range(8):
-            tile = crossed[:, g // 2 * LANES : (g // 2 + 1) * LANES]
-            tile = jnp.where(first if g % 2 == 0 else ~first, tile, 0.0)
-            tile = pltpu.roll(tile, g % 2 * BLOCK, 1, stride=1, stride_axis=0)
-            by_lag[c * 8 + g : c * 8 + g + 1, :] = jnp.sum(tile, axis=0, keepdims=True)
+        back[c] = stacked(dot(jnp.concatenate(tiles, 1), by_group(side_by_side(gm[c]))))
 
 
 def mixer_kernel(
@@ -407,9 +416,8 @@
 
     totals = lax.fori_loop(0, chunks, chunk, jnp.zeros((64, groups), F32), unroll=8)
     totals = totals[:32] + totals[32:]
-    lag = (iota((LANES, groups), 0) - (BLOCK - 1)).astype(F32)
-    lags = jnp.where(lag >= 0.0, by_lag[...].T, 0.0)
-    lag = jnp.maximum(lag, 0.0)
+    lag = iota((LANES, groups), 0).astype(F32)
+    lags = by_lag[...].T
     for m in range(16):
         rate = jnp.exp(lr[m : m + 1, :])
         terms = jnp.exp(-rate * lag) * lags
@@ -438,6 +446,11 @@
     count = lax.axis_size("seq")
     shard = lax.axis_index("seq")
     found = {"even": shard % 2 == 0}
+    stride, size = levels_of(count)[-1]
+    digit = (shard // stride) % size
+    for h in range(1, size):
+        found["onward", h] = digit + h < size
+        found["later", h] = jnp.where(h <= digit, 0.0, 1.0)
     for reverse in (False, True):
         low = 0
         for number, (stride, size) in enumerate(levels_of(count)):
@@ -512,15 +525,42 @@
             self.above = self.above + before
         self.value = group.astype(self.local.dtype)
 
-    def swap(self):
-        mine = self.above.astype(self.local.dtype)
-        other = lax.ppermute(mine, "seq", [(i, i ^ 1) for i in range(self.count)])
-        even = self.column("even")
-        low = jnp.where(even, mine, other)
-        high = jnp.where(even, other, mine)
-        above = jnp.concatenate([low, high], 1).astype(F32)
-        result = self.near + above * jnp.exp(-self.rate * self.get(0, "place"))
-        return result.astype(self.local.dtype)
+
+def send_both(ahead, behind):
+    stride, size = ahead.levels[-1]
+    got = []
+    for h in range(1, size):
+        pairs = []
+        for i in range(ahead.count):
+            digit = (i // stride) % size
+            pairs.append((i, i + ((digit + h) % size - digit) * stride))
+        value = jnp.where(ahead.column(("onward", h)), ahead.value, behind.value.astype(F32))
+        got.append(lax.ppermute(value, "seq", pairs))
+    return got
+
+
+def join_both(ahead, behind, got):
+    number = len(ahead.levels) - 1
+    stride, size = ahead.levels[-1]
+    rate = ahead.mine(ahead.rate)
+    span = float(ahead.rows * stride)
+    states = adjoints = 0.0
+    for h in range(1, size):
+        item = got[h - 1]
+        near = jnp.exp(-rate * (span * (h - 1)))
+        states = states + item * (ahead.get(number, "earlier", h) * near)
+        near = jnp.exp(-rate * (span * (size - h - 1)))
+        adjoints = adjoints + item * (ahead.column(("later", h)) * near)
+    states = ahead.above + states * jnp.exp(-rate * ahead.get(number, "low"))
+    adjoints = behind.above + adjoints * jnp.exp(-rate * behind.get(number, "low"))
+    mine = jnp.concatenate([states, adjoints], 0)
+    other = lax.ppermute(mine, "seq", [(i, i ^ 1) for i in range(ahead.count)])
+    even = ahead.column("even")
+    low, high = jnp.where(even, mine, other), jnp.where(even, other, mine)
+    above = jnp.concatenate([low, high], 1)
+    states = ahead.near + above[:16] * jnp.exp(-ahead.rate * ahead.get(0, "place"))
+    adjoints = behind.near + above[16:] * jnp.exp(-ahead.rate * behind.get(0, "place"))
+    return states, adjoints.astype(BF16)
 
 
 def on_device(section_input, sent_grad, norm_gain, short_filter, log_rate, residue, skip_gain):
@@ -536,7 +576,7 @@
     column = dict(zip(names, numbers)).__getitem__
 
     ring = [(i, (i - 1) % sections) for i in range(sections)]
-    cuts = (0, rows * 3 // 8, rows * 7 // 8, rows)
+    cuts = (0, rows * 2 // 8, rows * 5 // 8, rows)
     g = [
         lax.ppermute(sent_grad[0, low:high], "section", ring)
         for low, high in zip(cuts[:-1], cuts[1:])
@@ -628,32 +668,37 @@
         micros=0,
         name="adjoint",
     )
+    (back,) = call(
+        backward_kernel,
+        grid,
+        [
+            (after(gm, a_local), cube, block),
+            (kk, (1, 8 * STEP, LANES), lambda i: (1, i, 0)),
+        ],
+        [((chunks, LANES, LANES), F32, cube, block)],
+        micros=0,
+        name="backward",
+    )
+    ahead.got = [after(item, back) for item in ahead.got]
     behind = Prefix(after(a_local, *ahead.got), r_e, rows, True, column)
     behind.send(0)
-    ahead.join(1, a_local)
-    ahead.send(2)
+    ahead.join(1)
     behind.join(0)
     behind.send(1)
-    gm_late = after(gm, behind.value, ahead.value)
-    back, by_lag = call(
-        backward_kernel,
+    behind.join(1)
+    got = send_both(ahead, behind)
+    (by_lag,) = call(
+        lags_kernel,
         grid,
         [
-            (p, (2,) + cube, lambda i: (0, i, 0, 0)),
-            (gm_late, cube, block),
-            (kk, (1, 8 * STEP, LANES), lambda i: (1, i, 0)),
-        ],
-        [
-            ((chunks, LANES, LANES), F32, cube, block),
-            ((groups, LANES), F32, (8 * STEP, LANES), lambda i: (i, 0)),
-        ],
+            (after(p, behind.value, ahead.value), (2,) + cube, lambda i: (0, i, 0, 0)),
+            (gm, cube, block),
+        ],
+        [((groups, LANES), F32, (8 * STEP, LANES), lambda i: (i, 0))],
         micros=6,
-        name="backward",
-    )
-    behind.join(1, by_lag)
-    behind.send(2)
-    ahead.join(2, by_lag)
-    e = after(ahead.swap(), behind.value)
+        name="lags",
+    )
+    e, a = join_both(ahead, behind, [after(item, by_lag) for item in got])
     block_out, gn0, fg0 = call(
         output_kernel,
         grid,
@@ -680,8 +725,6 @@
         micros=8,
         name="output",
     )
-    behind.join(2, fg0)
-    a = behind.swap()
     gn, fg, hx, part = call(
         mixer_kernel,
         grid,

time: 99.4 us -> 89 us (0.90)
  starting transfers between devices: 38.4 us -> 27.8 us
  Pallas kernels: 39.8 us -> 41.7 us
  local copies, waits for them, and re-layouts: 3.98 us -> 2.27 us
    ppermute x14 -> x8, starting transfers between devices: 20.4 us -> 7.32 us  [send(): self.got.append(lax.ppermute(self.value, 'seq', pairs))]
    ppermute x2 -> x4, starting transfers between devices: 4.43 us -> 8.14 us  [the longest x3 4.97 us: send_both(): got.append(lax.ppermute(value, 'seq', pairs))]
    ppermute x3, waiting for transfers between devices: 2.55 us -> 5.25 us  [on_device(): lax.ppermute(sent_grad[0, low:high], 'section', ring)]
    ppermute x14 -> x8, waiting for transfers between devices: 8.03 us -> 5.32 us  [send(): self.got.append(lax.ppermute(self.value, 'seq', pairs))]
    pallas_call x8 -> x9, Pallas kernels: 39.8 us -> 41.7 us  [call(): pl.pallas_call(kernel, grid=grid, in_specs=[pl.BlockSpec(b, m) for _, b,...]
    ppermute x3, starting transfers between devices: 7.5 us -> 6.16 us  [on_device(): lax.ppermute(sent_grad[0, low:high], 'section', ring)]
    squeeze x3 -> x2, local copies, waits for them, and re-layouts: 3.11 us -> 2.23 us  [on_device(): sent_grad[0, low:high]]
  transfers between devices with their start and end apart: 21 -> 17, of which waited for: 8 -> 7; matrix products, arithmetic and copies ran while one was open for 4% -> 1% of each run, Pallas kernels for 28% -> 27%
where the time goes in v3:
time: 89 us; the launch traced here: 88.8 us
  Pallas kernels  41.7 us (47%)
  starting transfers between devices  27.8 us (31%)
  waiting for transfers between devices  14.7 us (17%)
  local copies, waits for them, and re-layouts  2.27 us (3%)
  between operations  1.24 us (1%)
  other arithmetic  1.07 us (1%)
    pallas_call x9, Pallas kernels, call(): pl.pallas_call(kernel, grid=grid, in_specs=[pl.BlockSpec(b, m) for _, b,...  41.7 us
    ppermute x8, starting transfers between devices, send(): self.got.append(lax.ppermute(self.value, 'seq', pairs))  7.32 us
    ppermute x3, starting transfers between devices, on_device(): lax.ppermute(sent_grad[0, low:high], 'section', ring)  6.16 us
    ppermute x8, waiting for transfers between devices, send(): self.got.append(lax.ppermute(self.value, 'seq', pairs))  5.32 us
    ppermute x3, waiting for transfers between devices, on_device(): lax.ppermute(sent_grad[0, low:high], 'section', ring)  5.25 us
    ppermute x3, starting transfers between devices, send_both(): got.append(lax.ppermute(value, 'seq', pairs))  4.97 us
    ppermute x1, starting transfers between devices, on_device(): lax.ppermute(x[rows - 8:], 'seq', [(i, i + 1) for i in range(count - 1)])  3.9 us
    ppermute x1, starting transfers between devices, join_both(): other = lax.ppermute(mine, 'seq', [(i, i ^ 1) for i in range(ahead.count)])  3.17 us
  transfers between devices with their start and end apart: 17, of which 7 were waited for; matrix products, arithmetic and copies ran while one was open for 1% of the time, Pallas kernels for 27%

profile of v3, /device:TPU:25, one launch (start us, length us, event | category | flops | bytes accessed | tf_op | source)
XLA Modules:
  0.0 88.8 jit_solution(10675937111084948038)
XLA Ops:
  0.7 1.1 %slice_bitcast_fusion.2 = bf16[32,4096]{1,0:T(8,128)(2,1)S(1)} fusion(bf16[1,128,4096]{2,1,0:T(8,128)(2,1)} %param.8), kind=kLoop, calls=%fused_computation.17 | loop fusion | bytes 524288 | tf_op jit(solution)/shard_map/squeeze | solution.py:581
  1.8 3.8 %collective-permute-start.1 = (bf16[32,4096]{1,0:T(8,128)(2,1)S(1)}, bf16[32,4096]{1,0:T(8,128)(2,1)S(1)}, u32[]{:S(2)}, u32[]{:S(2)}) collective-permute-start(bf16[32,4096]{1,0:T(8,128)(2,1)S(1)} %slice_bitcast_fusion.2), channel_id=1, source_target_pairs={{0,96},{32,0},{64,32},{96,64},{1,97},{33,1},{65,33},{97,65},{2,98}... | collective-permute-start | bytes 786440 | tf_op jit(solution)/shard_map/ppermute | solution.py:581
  5.6 1.2 %slice_bitcast_fusion = (bf16[48,4096]{1,0:T(8,128)(2,1)S(1)}, bf16[48,4096]{1,0:T(8,128)(2,1)S(1)}) fusion(bf16[1,128,4096]{2,1,0:T(8,128)(2,1)} %param.8), kind=kLoop, calls=%fused_computation.2 | loop fusion | bytes 1572864 | tf_op jit(solution)/shard_map/squeeze | solution.py:581
  6.7 0.2 collective-permute-start.2
  7.0 3.9 %collective-permute-start = (bf16[8,4096]{1,0:T(8,128)(2,1)S(1)}, bf16[8,4096]{1,0:T(8,128)(2,1)S(1)}, u32[]{:S(2)}, u32[]{:S(2)}) collective-permute-start(bf16[8,4096]{1,0:T(8,128)(2,1)S(1)} %slice_bitcast_fusion.3), channel_id=1, source_target_pairs={{0,1},{1,2},{2,3},{3,4},{4,5},{5,6},{6,7},{7,8},{8,9},{9,10},{10,1... | collective-permute-start | bytes 196616 | tf_op jit(solution)/shard_map/ppermute | solution.py:585
  11.2 3.3 %tables.1 = (bf16[32,3,128,128]{3,2,1,0:T(8,128)(2,1)S(1)}, bf16[32,2,64,128]{3,2,1,0:T(8,128)(2,1)S(1)}, f32[2,256,128]{2,1,0:T(8,128)S(1)}, f32[16,4096]{1,0:T(8,128)S(1)}, f32[16,4096]{1,0:T(8,128)S(1)}) custom-call(f32[16,256]{1,0:T(8,128)S(1)} %bitcast.27, f32[16,256]{1,0:T(8,128)S(1)} %bitcast.29), custom_call_target="tpu_custom_call" | custom-call | tf_op jit(solution)/shard_map/tables/pallas_call | solution.py:34
  14.5 0.0 collective-permute-done.1.g0
  14.5 7.3 %features.1 = (bf16[32,144,128]{2,1,0:T(8,128)(2,1)S(1)}, f32[32,128,128]{2,1,0:T(8,128)S(1)}, f32[32,128,128]{2,1,0:T(8,128)S(1)}, f32[32,128,128]{2,1,0:T(8,12...) custom-call(bf16[128,4096]{1,0:T(8,128)(2,1)S(1)} %bitcast.19, ...), custom_call_target="tpu_custom_call" | custom-call | tf_op jit(solution)/shard_map/features/pallas_call | solution.py:34
  21.8 0.0 collective-permute-done.2.g1
  21.8 0.1 collective-permute-start.3
  21.9 2.1 %collective-permute-start.5 = (bf16[48,4096]{1,0:T(8,128)(2,1)S(1)}, bf16[48,4096]{1,0:T(8,128)(2,1)S(1)}, u32[]{:S(2)}, u32[]{:S(2)}) collective-permute-start(bf16[48,4096]{1,0:T(8,128)(2,1)S(1)} %get-tuple-element.166), channel_id=1, source_target_pairs={{0,96},{32,0},{64,32},{96,64},{1,97},{33,1},{65,33},{97,65},{2,98}... | collective-permute-start | bytes 1179656 | tf_op jit(solution)/shard_map/ppermute | solution.py:581
  24.0 0.0 collective-permute-done.3
  24.0 0.1 multiply_add_fusion
  24.1 0.5 collective-permute-start.7
  24.7 0.7 collective-permute-start.6
  25.3 1.9 %collective-permute-start.4 = (f32[16,2048]{1,0:T(8,128)S(1)}, f32[16,2048]{1,0:T(8,128)S(1)}, u32[]{:S(2)}, u32[]{:S(2)}) collective-permute-start(f32[16,2048]{1,0:T(8,128)S(1)} %slice_select_fusion.1), channel_id=1, source_target_pairs={{0,2},{1,3},{2,4},{3,5},{4,6},{5,7},{6,0},{7,1},{8,10},{9,11},{10,... | collective-permute-start | bytes 393224 | tf_op jit(solution)/shard_map/ppermute | solution.py:500
  27.2 5.2 %collective-permute-done.5.g2 = bf16[48,4096]{1,0:T(8,128)(2,1)S(1)} collective-permute-done((bf16[48,4096]{1,0:T(8,128)(2,1)S(1)}, bf16[48,4096]{1,0:T(8,128)(2,1)S(1)}, u32[]{:S(2)}, u32[]{:S(2)}) %collective-permute-start.5) | collective-permute-done | bytes 393248 | tf_op jit(solution)/shard_map/ppermute | solution.py:581
  32.5 2.1 %adjoint.1 = (bf16[32,128,128]{2,1,0:T(8,128)(2,1)S(1)}, bf16[16,4096]{1,0:T(8,128)(2,1)S(1)}, f32[64,4096]{1,0:T(8,128)S(1)}) custom-call(bf16[32,4096]{1,0:T(8,128)(2,1)S(1)} %collective-permute-done.1.g0, bf16[48,4096]{1,0:T(8,128)(2,1)S(1)} %collective-permute-done.2.g1, bf16[48,4096]{1,0:T(8,128)(2,1)S(1)} %collective-permute-done.5.g2, ...), custom_call_target="tpu_custom_call" | custom-call | tf_op jit(solution)/shard_map/adjoint/pallas_call | solution.py:34
  34.6 2.3 %backward.1.back = f32[32,128,128]{2,1,0:T(8,128)S(1)} custom-call(bf16[32,128,128]{2,1,0:T(8,128)(2,1)S(1)} %get-tuple-element.100.gm, f32[2,256,128]{2,1,0:T(8,128)S(1)} %get-tuple-element.85.kk), custom_call_target="tpu_custom_call" | custom-call | tf_op jit(solution)/shard_map/backward/pallas_call | solution.py:34
  36.9 0.0 collective-permute-done.6
  36.9 0.0 collective-permute-done.4
  36.9 1.1 %collective-permute-start.8 = (bf16[16,4096]{1,0:T(8,128)(2,1)S(1)}, bf16[16,4096]{1,0:T(8,128)(2,1)S(1)}, u32[]{:S(2)}, u32[]{:S(2)}) collective-permute-start(bf16[16,4096]{1,0:T(8,128)(2,1)S(1)} %get-tuple-element.112), channel_id=1, source_target_pairs={{0,1},{1,0},{2,3},{3,2},{4,5},{5,4},{6,7},{7,6},{8,9},{9,8},{10,11... | collective-permute-start | bytes 393224 | tf_op jit(solution)/shard_map/ppermute | solution.py:500
  38.0 1.0 %collective-permute-done.8 = bf16[16,4096]{1,0:T(8,128)(2,1)S(1)} collective-permute-done((bf16[16,4096]{1,0:T(8,128)(2,1)S(1)}, bf16[16,4096]{1,0:T(8,128)(2,1)S(1)}, u32[]{:S(2)}, u32[]{:S(2)}) %collective-permute-start.8) | collective-permute-done | bytes 131104 | tf_op jit(solution)/shard_map/ppermute | solution.py:500
  39.0 0.1 fusion
  39.1 1.5 %collective-permute-start.10 = (bf16[16,2048]{1,0:T(8,128)(2,1)S(1)}, bf16[16,2048]{1,0:T(8,128)(2,1)S(1)}, u32[]{:S(2)}, u32[]{:S(2)}) collective-permute-start(bf16[16,2048]{1,0:T(8,128)(2,1)S(1)} %fusion.14), channel_id=1, source_target_pairs={{0,4},{1,5},{2,6},{3,7},{4,0},{5,1},{6,2},{7,3},{8,12},{9,13},{10,... | collective-permute-start | bytes 196616 | tf_op jit(solution)/shard_map/ppermute | solution.py:500
  40.6 1.6 %collective-permute-start.11 = (bf16[16,2048]{1,0:T(8,128)(2,1)S(1)}, bf16[16,2048]{1,0:T(8,128)(2,1)S(1)}, u32[]{:S(2)}, u32[]{:S(2)}) collective-permute-start(bf16[16,2048]{1,0:T(8,128)(2,1)S(1)} %fusion.14), channel_id=1, source_target_pairs={{0,2},{1,3},{2,4},{3,5},{4,6},{5,7},{6,0},{7,1},{8,10},{9,11},{10,... | collective-permute-start | bytes 196616 | tf_op jit(solution)/shard_map/ppermute | solution.py:500
  42.2 0.0 collective-permute-start.9
  42.2 1.6 %collective-permute-done.10 = bf16[16,2048]{1,0:T(8,128)(2,1)S(1)} collective-permute-done((bf16[16,2048]{1,0:T(8,128)(2,1)S(1)}, bf16[16,2048]{1,0:T(8,128)(2,1)S(1)}, u32[]{:S(2)}, u32[]{:S(2)}) %collective-permute-start.10) | collective-permute-done | bytes 65568 | tf_op jit(solution)/shard_map/ppermute | solution.py:500
  43.8 0.2 collective-permute-done.11
  44.0 2.5 %collective-permute-done.9 = bf16[16,2048]{1,0:T(8,128)(2,1)S(1)} collective-permute-done((bf16[16,2048]{1,0:T(8,128)(2,1)S(1)}, bf16[16,2048]{1,0:T(8,128)(2,1)S(1)}, u32[]{:S(2)}, u32[]{:S(2)}) %collective-permute-start.9) | collective-permute-done | bytes 65568 | tf_op jit(solution)/shard_map/ppermute | solution.py:500
  46.5 0.2 convert_select_fusion.2
  46.7 1.3 %collective-permute-start.12 = (f32[16,2048]{1,0:T(8,128)S(1)}, f32[16,2048]{1,0:T(8,128)S(1)}, u32[]{:S(2)}, u32[]{:S(2)}) collective-permute-start(f32[16,2048]{1,0:T(8,128)S(1)} %get-tuple-element.162), channel_id=1, source_target_pairs={{0,8},{1,9},{2,10},{3,11},{4,12},{5,13},{6,14},{7,15},{8,16},{9,17... | collective-permute-start | bytes 393224 | tf_op jit(solution)/shard_map/ppermute | solution.py:538
  48.0 2.5 %collective-permute-start.13 = (f32[16,2048]{1,0:T(8,128)S(1)}, f32[16,2048]{1,0:T(8,128)S(1)}, u32[]{:S(2)}, u32[]{:S(2)}) collective-permute-start(f32[16,2048]{1,0:T(8,128)S(1)} %get-tuple-element.172), channel_id=1, source_target_pairs={{0,16},{1,17},{2,18},{3,19},{4,20},{5,21},{6,22},{7,23},{8,24},{9,... | collective-permute-start | bytes 393224 | tf_op jit(solution)/shard_map/ppermute | solution.py:538
  50.6 1.1 %collective-permute-start.14 = (f32[16,2048]{1,0:T(8,128)S(1)}, f32[16,2048]{1,0:T(8,128)S(1)}, u32[]{:S(2)}, u32[]{:S(2)}) collective-permute-start(f32[16,2048]{1,0:T(8,128)S(1)} %get-tuple-element.173), channel_id=1, source_target_pairs={{0,24},{1,25},{2,26},{3,27},{4,28},{5,29},{6,30},{7,31},{8,0},{9,1... | collective-permute-start | bytes 393224 | tf_op jit(solution)/shard_map/ppermute | solution.py:538
  51.7 6.7 %lags.1.by_lag = f32[256,128]{1,0:T(8,128)S(1)} custom-call(bf16[2,32,128,128]{3,2,1,0:T(8,128)(2,1)S(1)} %get-tuple-element.120.p, bf16[32,128,128]{2,1,0:T(8,128)(2,1)S(1)} %get-tuple-element.100.gm), custom_call_target="tpu_custom_call" | custom-call | flops 6000000000 | bytes 3276800 | tf_op jit(solution)/shard_map/lags/pallas_call | solution.py:34
  58.4 0.0 collective-permute-done.13
  58.4 0.2 multiply_add_fusion.1
  58.6 0.0 copy-start.5
  58.6 0.2 fusion.13
  58.8 3.2 %collective-permute-start.15 = (f32[32,2048]{1,0:T(8,128)S(1)}, f32[32,2048]{1,0:T(8,128)S(1)}, u32[]{:S(2)}, u32[]{:S(2)}) collective-permute-start(f32[32,2048]{1,0:T(8,128)S(1)} %pad_maximum_fusion.1), channel_id=1, source_target_pairs={{0,1},{1,0},{2,3},{3,2},{4,5},{5,4},{6,7},{7,6},{8,9},{9,8},{10,11... | collective-permute-start | bytes 786440 | tf_op jit(solution)/shard_map/ppermute | solution.py:557
  62.0 1.2 %collective-permute-done.15 = f32[32,2048]{1,0:T(8,128)S(1)} collective-permute-done((f32[32,2048]{1,0:T(8,128)S(1)}, f32[32,2048]{1,0:T(8,128)S(1)}, u32[]{:S(2)}, u32[]{:S(2)}) %collective-permute-start.15) | collective-permute-done | bytes 262176 | tf_op jit(solution)/shard_map/ppermute | solution.py:557
  63.2 0.2 fusion.2
  63.4 6.3 %output.1 = (bf16[128,4096]{1,0:T(8,128)(2,1)}, f32[32,136,128]{2,1,0:T(8,128)S(1)}, f32[8,4096]{1,0:T(8,128)S(1)}) custom-call(f32[32,128,128]{2,1,0:T(8,128)S(1)} %get-tuple-element.87.inside, bf16[32,2,64,128]{3,2,1,0:T(8,128)(2,1)S(1)} %get-tuple-element.88.lrw, f32[16,4096]{1,0:T(8,128)S(1)} %get-tuple-element.169.e, ...), custom_call_target="tpu_custom_call" | custom-call | flops 8000000000 | bytes 15958016 | tf_op jit(solution)/shard_map/output/pallas_call | solution.py:34
  69.7 8.8 %mixer.1 = (f32[32,128,128]{2,1,0:T(8,128)S(1)}, f32[16,4096]{1,0:T(8,128)S(1)}, f32[128,128]{1,0:T(8,128)S(1)}, bf16[8,4096]{1,0:T(8,128)(2,1)S(1)}) custom-call(f32[32,128,128]{2,1,0:T(8,128)S(1)} %backward.1.back, bf16[32,2,64,128]{3,2,1,0:T(8,128)(2,1)S(1)} %get-tuple-element.88.lrw, bf16[16,4096]{1,0:T(8,128)(2,1)S(1)} %get-tuple-element.168.a, ...), custom_call_target="tpu_custom_call" | custom-call | flops 10000000000 | bytes 17485824 | tf_op jit(solution)/shard_map/mixer/pallas_call | solution.py:34
  78.5 2.3 %collective-permute-start.16 = (bf16[8,4096]{1,0:T(8,128)(2,1)S(1)}, bf16[8,4096]{1,0:T(8,128)(2,1)S(1)}, u32[]{:S(2)}, u32[]{:S(2)}) collective-permute-start(bf16[8,4096]{1,0:T(8,128)(2,1)S(1)} %get-tuple-element.152), channel_id=1, source_target_pairs={{1,0},{2,1},{3,2},{4,3},{5,4},{6,5},{7,6},{8,7},{9,8},{10,9},{11,1... | collective-permute-start | bytes 196616 | tf_op jit(solution)/shard_map/ppermute | solution.py:759
  80.8 2.4 %modes.1 = (f32[16,256]{1,0:T(8,128)}, f32[16,256]{1,0:T(8,128)}) custom-call(bf16[16,4096]{1,0:T(8,128)(2,1)S(1)} %get-tuple-element.168.a, f32[64,4096]{1,0:T(8,128)S(1)} %get-tuple-element.143.b, f32[16,4096]{1,0:T(8,128)S(1)} %get-tuple-element.169.e, f32[64,4096]{1,0:T(8,128)S(1)} %get-tuple-element.138.f, f32[16,4096]{1,0:T(8,128)S(1)} %get-tuple-element.86.r_e, ...), custom_call_target="tpu_custom_call" | custom-call | flops 3000000000 | bytes 3211264 | tf_op jit(solution)/shard_map/modes/pallas_call | solution.py:34
  83.2 3.0 %collective-permute-done.16.part = bf16[8,4096]{1,0:T(8,128)(2,1)S(1)} collective-permute-done((bf16[8,4096]{1,0:T(8,128)(2,1)S(1)}, bf16[8,4096]{1,0:T(8,128)(2,1)S(1)}, u32[]{:S(2)}, u32[]{:S(2)}) %collective-permute-start.16) | collective-permute-done | bytes 65568 | tf_op jit(solution)/shard_map/ppermute | solution.py:759
  86.2 2.6 %final.1 = (bf16[128,4096]{1,0:T(8,128)(2,1)}, f32[23,1,4096]{2,1,0:T(1,128)}) custom-call(f32[32,128,128]{2,1,0:T(8,128)S(1)} %get-tuple-element.148.gn, bf16[32,4096]{1,0:T(8,128)(2,1)S(1)} %collective-permute-done.1.g0, bf16[48,4096]{1,0:T(8,128)(2,1)S(1)} %collective-permute-done.2.g1, bf16[48,4096]{1,0:T(8,128)(2,1)S(1)} %collective-permute-done.5.g2, ...), custom_call_target="tpu_custom_call" | custom-call | flops 4000000000 | bytes 7294976 | tf_op jit(solution)/shard_map/final/pallas_call | solution.py:34
  (21 shorter events, 0.1 us)
Async XLA Ops:
  0.6 6.3 %copy-start = (bf16[1,128,4096]{2,1,0:T(8,128)(2,1)S(1)}, bf16[1,128,4096]{2,1,0:T(8,128)(2,1)}, u32[]{:S(2)}) copy-start(bf16[1,128,4096]{2,1,0:T(8,128)(2,1)} %param.7) | copy-start | bytes 3145732
  0.6 10.5 %copy-start.3 = (f32[1,16,256]{2,1,0:T(8,128)S(1)}, f32[1,16,256]{2,1,0:T(8,128)}, u32[]{:S(2)}) copy-start(f32[1,16,256]{2,1,0:T(8,128)} %param.11) | copy-start | bytes 49156
  0.7 10.5 %copy-start.4 = (f32[1,16,256]{2,1,0:T(8,128)S(1)}, f32[1,16,256]{2,1,0:T(8,128)}, u32[]{:S(2)}) copy-start(f32[1,16,256]{2,1,0:T(8,128)} %param.12) | copy-start | bytes 49156
  0.7 13.8 %copy-start.1 = (f32[1,21,4096]{2,0,1:T(1,128)S(1)}, f32[1,21,4096]{2,0,1:T(1,128)}, u32[]{:S(2)}) copy-start(f32[1,21,4096]{2,0,1:T(1,128)} %param.10) | copy-start | bytes 1032196
  0.7 13.8 %copy-start.2 = (f32[1,4096]{1,0:T(1,128)S(1)}, f32[1,4096]{1,0:T(1,128)}, u32[]{:S(2)}) copy-start(f32[1,4096]{1,0:T(1,128)} %gain_all.1) | copy-start | bytes 49156
  1.8 12.7 %collective-permute-start.1 = (bf16[32,4096]{1,0:T(8,128)(2,1)S(1)}, bf16[32,4096]{1,0:T(8,128)(2,1)S(1)}, u32[]{:S(2)}, u32[]{:S(2)}) collective-permute-start(bf16[32,4096]{1,0:T(8,128)(2,1)S(1)} %slice_bitcast_fusion.2), channel_id=1, source_target_pairs={{0,96},{32,0},{64,32},{96,64},{1,97},{33,1},{65,33},{97,65},{2,98}... | collective-permute-start | bytes 786440 | tf_op jit(solution)/shard_map/ppermute | solution.py:581
  6.7 15.0 %collective-permute-start.2 = (bf16[48,4096]{1,0:T(8,128)(2,1)S(1)}, bf16[48,4096]{1,0:T(8,128)(2,1)S(1)}, u32[]{:S(2)}, u32[]{:S(2)}) collective-permute-start(bf16[48,4096]{1,0:T(8,128)(2,1)S(1)} %get-tuple-element.167), channel_id=1, source_target_pairs={{0,96},{32,0},{64,32},{96,64},{1,97},{33,1},{65,33},{97,65},{2,98}... | collective-permute-start | bytes 1179656 | tf_op jit(solution)/shard_map/ppermute | solution.py:581
  7.0 7.5 %collective-permute-start = (bf16[8,4096]{1,0:T(8,128)(2,1)S(1)}, bf16[8,4096]{1,0:T(8,128)(2,1)S(1)}, u32[]{:S(2)}, u32[]{:S(2)}) collective-permute-start(bf16[8,4096]{1,0:T(8,128)(2,1)S(1)} %slice_bitcast_fusion.3), channel_id=1, source_target_pairs={{0,1},{1,2},{2,3},{3,4},{4,5},{5,6},{6,7},{7,8},{8,9},{9,10},{10,1... | collective-permute-start | bytes 196616 | tf_op jit(solution)/shard_map/ppermute | solution.py:585
  21.8 2.2 %collective-permute-start.3 = (f32[16,4096]{1,0:T(8,128)S(1)}, f32[16,4096]{1,0:T(8,128)S(1)}, u32[]{:S(2)}, u32[]{:S(2)}) collective-permute-start(f32[16,4096]{1,0:T(8,128)S(1)} %get-tuple-element.90), channel_id=1, source_target_pairs={{0,1},{1,0},{2,3},{3,2},{4,5},{5,4},{6,7},{7,6},{8,9},{9,8},{10,11... | collective-permute-start | bytes 786440 | tf_op jit(solution)/shard_map/ppermute | solution.py:500
  21.9 10.6 %collective-permute-start.5 = (bf16[48,4096]{1,0:T(8,128)(2,1)S(1)}, bf16[48,4096]{1,0:T(8,128)(2,1)S(1)}, u32[]{:S(2)}, u32[]{:S(2)}) collective-permute-start(bf16[48,4096]{1,0:T(8,128)(2,1)S(1)} %get-tuple-element.166), channel_id=1, source_target_pairs={{0,96},{32,0},{64,32},{96,64},{1,97},{33,1},{65,33},{97,65},{2,98}... | collective-permute-start | bytes 1179656 | tf_op jit(solution)/shard_map/ppermute | solution.py:581
  24.1 12.8 %collective-permute-start.7 = (f32[16,2048]{1,0:T(8,128)S(1)}, f32[16,2048]{1,0:T(8,128)S(1)}, u32[]{:S(2)}, u32[]{:S(2)}) collective-permute-start(f32[16,2048]{1,0:T(8,128)S(1)} %slice_select_fusion.1), channel_id=1, source_target_pairs={{0,6},{1,7},{2,0},{3,1},{4,2},{5,3},{6,4},{7,5},{8,14},{9,15},{10,... | collective-permute-start | bytes 393224 | tf_op jit(solution)/shard_map/ppermute | solution.py:500
  24.7 12.2 %collective-permute-start.6 = (f32[16,2048]{1,0:T(8,128)S(1)}, f32[16,2048]{1,0:T(8,128)S(1)}, u32[]{:S(2)}, u32[]{:S(2)}) collective-permute-start(f32[16,2048]{1,0:T(8,128)S(1)} %slice_select_fusion.1), channel_id=1, source_target_pairs={{0,4},{1,5},{2,6},{3,7},{4,0},{5,1},{6,2},{7,3},{8,12},{9,13},{10,... | collective-permute-start | bytes 393224 | tf_op jit(solution)/shard_map/ppermute | solution.py:500
  25.3 11.6 %collective-permute-start.4 = (f32[16,2048]{1,0:T(8,128)S(1)}, f32[16,2048]{1,0:T(8,128)S(1)}, u32[]{:S(2)}, u32[]{:S(2)}) collective-permute-start(f32[16,2048]{1,0:T(8,128)S(1)} %slice_select_fusion.1), channel_id=1, source_target_pairs={{0,2},{1,3},{2,4},{3,5},{4,6},{5,7},{6,0},{7,1},{8,10},{9,11},{10,... | collective-permute-start | bytes 393224 | tf_op jit(solution)/shard_map/ppermute | solution.py:500
  36.9 2.1 %collective-permute-start.8 = (bf16[16,4096]{1,0:T(8,128)(2,1)S(1)}, bf16[16,4096]{1,0:T(8,128)(2,1)S(1)}, u32[]{:S(2)}, u32[]{:S(2)}) collective-permute-start(bf16[16,4096]{1,0:T(8,128)(2,1)S(1)} %get-tuple-element.112), channel_id=1, source_target_pairs={{0,1},{1,0},{2,3},{3,2},{4,5},{5,4},{6,7},{7,6},{8,9},{9,8},{10,11... | collective-permute-start | bytes 393224 | tf_op jit(solution)/shard_map/ppermute | solution.py:500
  39.1 4.7 %collective-permute-start.10 = (bf16[16,2048]{1,0:T(8,128)(2,1)S(1)}, bf16[16,2048]{1,0:T(8,128)(2,1)S(1)}, u32[]{:S(2)}, u32[]{:S(2)}) collective-permute-start(bf16[16,2048]{1,0:T(8,128)(2,1)S(1)} %fusion.14), channel_id=1, source_target_pairs={{0,4},{1,5},{2,6},{3,7},{4,0},{5,1},{6,2},{7,3},{8,12},{9,13},{10,... | collective-permute-start | bytes 196616 | tf_op jit(solution)/shard_map/ppermute | solution.py:500
  40.6 3.4 %collective-permute-start.11 = (bf16[16,2048]{1,0:T(8,128)(2,1)S(1)}, bf16[16,2048]{1,0:T(8,128)(2,1)S(1)}, u32[]{:S(2)}, u32[]{:S(2)}) collective-permute-start(bf16[16,2048]{1,0:T(8,128)(2,1)S(1)} %fusion.14), channel_id=1, source_target_pairs={{0,2},{1,3},{2,4},{3,5},{4,6},{5,7},{6,0},{7,1},{8,10},{9,11},{10,... | collective-permute-start | bytes 196616 | tf_op jit(solution)/shard_map/ppermute | solution.py:500
  42.2 4.3 %collective-permute-start.9 = (bf16[16,2048]{1,0:T(8,128)(2,1)S(1)}, bf16[16,2048]{1,0:T(8,128)(2,1)S(1)}, u32[]{:S(2)}, u32[]{:S(2)}) collective-permute-start(bf16[16,2048]{1,0:T(8,128)(2,1)S(1)} %fusion.14), channel_id=1, source_target_pairs={{0,6},{1,7},{2,0},{3,1},{4,2},{5,3},{6,4},{7,5},{8,14},{9,15},{10,... | collective-permute-start | bytes 196616 | tf_op jit(solution)/shard_map/ppermute | solution.py:500
  46.7 11.7 %collective-permute-start.12 = (f32[16,2048]{1,0:T(8,128)S(1)}, f32[16,2048]{1,0:T(8,128)S(1)}, u32[]{:S(2)}, u32[]{:S(2)}) collective-permute-start(f32[16,2048]{1,0:T(8,128)S(1)} %get-tuple-element.162), channel_id=1, source_target_pairs={{0,8},{1,9},{2,10},{3,11},{4,12},{5,13},{6,14},{7,15},{8,16},{9,17... | collective-permute-start | bytes 393224 | tf_op jit(solution)/shard_map/ppermute | solution.py:538
  48.0 10.4 %collective-permute-start.13 = (f32[16,2048]{1,0:T(8,128)S(1)}, f32[16,2048]{1,0:T(8,128)S(1)}, u32[]{:S(2)}, u32[]{:S(2)}) collective-permute-start(f32[16,2048]{1,0:T(8,128)S(1)} %get-tuple-element.172), channel_id=1, source_target_pairs={{0,16},{1,17},{2,18},{3,19},{4,20},{5,21},{6,22},{7,23},{8,24},{9,... | collective-permute-start | bytes 393224 | tf_op jit(solution)/shard_map/ppermute | solution.py:538
  50.6 7.8 %collective-permute-start.14 = (f32[16,2048]{1,0:T(8,128)S(1)}, f32[16,2048]{1,0:T(8,128)S(1)}, u32[]{:S(2)}, u32[]{:S(2)}) collective-permute-start(f32[16,2048]{1,0:T(8,128)S(1)} %get-tuple-element.173), channel_id=1, source_target_pairs={{0,24},{1,25},{2,26},{3,27},{4,28},{5,29},{6,30},{7,31},{8,0},{9,1... | collective-permute-start | bytes 393224 | tf_op jit(solution)/shard_map/ppermute | solution.py:538
  58.6 4.8 %copy-start.5 = (f32[1,4096]{1,0:T(1,128)S(1)}, f32[1,4096]{1,0:T(1,128)}, u32[]{:S(2)}) copy-start(f32[1,4096]{1,0:T(1,128)} %skip.3) | copy-start | bytes 49156
  58.8 4.3 %collective-permute-start.15 = (f32[32,2048]{1,0:T(8,128)S(1)}, f32[32,2048]{1,0:T(8,128)S(1)}, u32[]{:S(2)}, u32[]{:S(2)}) collective-permute-start(f32[32,2048]{1,0:T(8,128)S(1)} %pad_maximum_fusion.1), channel_id=1, source_target_pairs={{0,1},{1,0},{2,3},{3,2},{4,5},{5,4},{6,7},{7,6},{8,9},{9,8},{10,11... | collective-permute-start | bytes 786440 | tf_op jit(solution)/shard_map/ppermute | solution.py:557
  78.5 7.7 %collective-permute-start.16 = (bf16[8,4096]{1,0:T(8,128)(2,1)S(1)}, bf16[8,4096]{1,0:T(8,128)(2,1)S(1)}, u32[]{:S(2)}, u32[]{:S(2)}) collective-permute-start(bf16[8,4096]{1,0:T(8,128)(2,1)S(1)} %get-tuple-element.152), channel_id=1, source_target_pairs={{1,0},{2,1},{3,2},{4,3},{5,4},{6,5},{7,6},{8,7},{9,8},{10,9},{11,1... | collective-permute-start | bytes 196616 | tf_op jit(solution)/shard_map/ppermute | solution.py:759

commit v4 on v3

--- a/solution.py
+++ b/solution.py
@@ -9,11 +9,11 @@
 F32 = jnp.float32
 BF16 = jnp.bfloat16
 LANES = 128
-STEP = 8
+STEP = 16
 WIDE = STEP * LANES
 BLOCK = 64
 TABLE_STEP = 16
-VMEM_LIMIT = 20 * 1024 * 1024
+VMEM_LIMIT = 26 * 1024 * 1024
 
 
 def iota(shape, axis):

time: 89 us -> 86.3 us (0.970)
  Pallas kernels: 41.7 us -> 39.2 us
    pallas_call x9, Pallas kernels: 41.7 us -> 39.2 us  [call(): pl.pallas_call(kernel, grid=grid, in_specs=[pl.BlockSpec(b, m) for _, b,...]
  transfers between devices with their start and end apart: 17 -> 17, of which waited for: 7 -> 6; matrix products, arithmetic and copies ran while one was open for 1% -> 2% of each run, Pallas kernels for 27% -> 26%
where the time goes in v4:
time: 86.3 us; the launch traced here: 86.1 us
  Pallas kernels  39.2 us (45%)
  starting transfers between devices  27.5 us (32%)
  waiting for transfers between devices  14.8 us (17%)
  local copies, waits for them, and re-layouts  2.27 us (3%)
  between operations  1.23 us (1%)
  other arithmetic  1.07 us (1%)
    pallas_call x9, Pallas kernels, call(): pl.pallas_call(kernel, grid=grid, in_specs=[pl.BlockSpec(b, m) for _, b,...  39.2 us
    ppermute x8, starting transfers between devices, send(): self.got.append(lax.ppermute(self.value, 'seq', pairs))  7.01 us
    ppermute x3, starting transfers between devices, on_device(): lax.ppermute(sent_grad[0, low:high], 'section', ring)  6.38 us
    ppermute x3, waiting for transfers between devices, on_device(): lax.ppermute(sent_grad[0, low:high], 'section', ring)  5.33 us
    ppermute x8, waiting for transfers between devices, send(): self.got.append(lax.ppermute(self.value, 'seq', pairs))  5.32 us
    ppermute x3, starting transfers between devices, send_both(): got.append(lax.ppermute(value, 'seq', pairs))  4.96 us
    ppermute x1, starting transfers between devices, on_device(): lax.ppermute(x[rows - 8:], 'seq', [(i, i + 1) for i in range(count - 1)])  3.9 us
    ppermute x1, waiting for transfers between devices, on_device(): part = lax.ppermute(part, 'seq', [(i + 1, i) for i in range(count - 1)])  2.99 us
  transfers between devices with their start and end apart: 17, of which 6 were waited for; matrix products, arithmetic and copies ran while one was open for 2% of the time, Pallas kernels for 26%

profile of v4, /device:TPU:25, one launch (start us, length us, event | category | flops | bytes accessed | tf_op | source)
XLA Modules:
  0.0 86.1 jit_solution(8931852199598425807)
XLA Ops:
  0.7 1.1 %slice_bitcast_fusion.2 = bf16[32,4096]{1,0:T(8,128)(2,1)S(1)} fusion(bf16[1,128,4096]{2,1,0:T(8,128)(2,1)} %param.8), kind=kLoop, calls=%fused_computation.17 | loop fusion | bytes 524288 | tf_op jit(solution)/shard_map/squeeze | solution.py:581
  1.8 3.8 %collective-permute-start.1 = (bf16[32,4096]{1,0:T(8,128)(2,1)S(1)}, bf16[32,4096]{1,0:T(8,128)(2,1)S(1)}, u32[]{:S(2)}, u32[]{:S(2)}) collective-permute-start(bf16[32,4096]{1,0:T(8,128)(2,1)S(1)} %slice_bitcast_fusion.2), channel_id=1, source_target_pairs={{0,96},{32,0},{64,32},{96,64},{1,97},{33,1},{65,33},{97,65},{2,98}... | collective-permute-start | bytes 786440 | tf_op jit(solution)/shard_map/ppermute | solution.py:581
  5.6 1.2 %slice_bitcast_fusion = (bf16[48,4096]{1,0:T(8,128)(2,1)S(1)}, bf16[48,4096]{1,0:T(8,128)(2,1)S(1)}) fusion(bf16[1,128,4096]{2,1,0:T(8,128)(2,1)} %param.8), kind=kLoop, calls=%fused_computation.2 | loop fusion | bytes 1572864 | tf_op jit(solution)/shard_map/squeeze | solution.py:581
  6.7 0.2 collective-permute-start.2
  7.0 3.9 %collective-permute-start = (bf16[8,4096]{1,0:T(8,128)(2,1)S(1)}, bf16[8,4096]{1,0:T(8,128)(2,1)S(1)}, u32[]{:S(2)}, u32[]{:S(2)}) collective-permute-start(bf16[8,4096]{1,0:T(8,128)(2,1)S(1)} %slice_bitcast_fusion.3), channel_id=1, source_target_pairs={{0,1},{1,2},{2,3},{3,4},{4,5},{5,6},{6,7},{7,8},{8,9},{9,10},{10,1... | collective-permute-start | bytes 196616 | tf_op jit(solution)/shard_map/ppermute | solution.py:585
  11.2 3.3 %tables.1 = (bf16[32,3,128,128]{3,2,1,0:T(8,128)(2,1)S(1)}, bf16[32,2,64,128]{3,2,1,0:T(8,128)(2,1)S(1)}, f32[2,256,128]{2,1,0:T(8,128)S(1)}, f32[16,4096]{1,0:T(8,128)S(1)}, f32[16,4096]{1,0:T(8,128)S(1)}) custom-call(f32[16,256]{1,0:T(8,128)S(1)} %bitcast.27, f32[16,256]{1,0:T(8,128)S(1)} %bitcast.29), custom_call_target="tpu_custom_call" | custom-call | tf_op jit(solution)/shard_map/tables/pallas_call | solution.py:34
  14.5 0.0 collective-permute-done.xh
  14.5 0.0 collective-permute-done.1.g0
  14.5 7.0 %features.1 = (bf16[32,144,128]{2,1,0:T(8,128)(2,1)S(1)}, f32[32,128,128]{2,1,0:T(8,128)S(1)}, f32[32,128,128]{2,1,0:T(8,128)S(1)}, f32[32,128,128]{2,1,0:T(8,12...) custom-call(bf16[128,4096]{1,0:T(8,128)(2,1)S(1)} %bitcast.19, ...), custom_call_target="tpu_custom_call" | custom-call | tf_op jit(solution)/shard_map/features/pallas_call | solution.py:34
  21.5 0.0 collective-permute-done.2.g1
  21.5 0.1 collective-permute-start.3
  21.6 2.4 %collective-permute-start.5 = (bf16[48,4096]{1,0:T(8,128)(2,1)S(1)}, bf16[48,4096]{1,0:T(8,128)(2,1)S(1)}, u32[]{:S(2)}, u32[]{:S(2)}) collective-permute-start(bf16[48,4096]{1,0:T(8,128)(2,1)S(1)} %get-tuple-element.166), channel_id=1, source_target_pairs={{0,96},{32,0},{64,32},{96,64},{1,97},{33,1},{65,33},{97,65},{2,98}... | collective-permute-start | bytes 1179656 | tf_op jit(solution)/shard_map/ppermute | solution.py:581
  23.9 0.0 collective-permute-done.3
  23.9 0.1 multiply_add_fusion
  24.1 0.5 collective-permute-start.7
  24.6 0.7 collective-permute-start.6
  25.3 1.9 %collective-permute-start.4 = (f32[16,2048]{1,0:T(8,128)S(1)}, f32[16,2048]{1,0:T(8,128)S(1)}, u32[]{:S(2)}, u32[]{:S(2)}) collective-permute-start(f32[16,2048]{1,0:T(8,128)S(1)} %slice_select_fusion.1), channel_id=1, source_target_pairs={{0,2},{1,3},{2,4},{3,5},{4,6},{5,7},{6,0},{7,1},{8,10},{9,11},{10,... | collective-permute-start | bytes 393224 | tf_op jit(solution)/shard_map/ppermute | solution.py:500
  27.2 5.3 %collective-permute-done.5.g2 = bf16[48,4096]{1,0:T(8,128)(2,1)S(1)} collective-permute-done((bf16[48,4096]{1,0:T(8,128)(2,1)S(1)}, bf16[48,4096]{1,0:T(8,128)(2,1)S(1)}, u32[]{:S(2)}, u32[]{:S(2)}) %collective-permute-start.5) | collective-permute-done | bytes 393248 | tf_op jit(solution)/shard_map/ppermute | solution.py:581
  32.5 1.8 %adjoint.1 = (bf16[32,128,128]{2,1,0:T(8,128)(2,1)S(1)}, bf16[16,4096]{1,0:T(8,128)(2,1)S(1)}, f32[64,4096]{1,0:T(8,128)S(1)}) custom-call(bf16[32,4096]{1,0:T(8,128)(2,1)S(1)} %collective-permute-done.1.g0, bf16[48,4096]{1,0:T(8,128)(2,1)S(1)} %collective-permute-done.2.g1, bf16[48,4096]{1,0:T(8,128)(2,1)S(1)} %collective-permute-done.5.g2, ...), custom_call_target="tpu_custom_call" | custom-call | tf_op jit(solution)/shard_map/adjoint/pallas_call | solution.py:34
  34.3 1.9 %backward.1.back = f32[32,128,128]{2,1,0:T(8,128)S(1)} custom-call(bf16[32,128,128]{2,1,0:T(8,128)(2,1)S(1)} %get-tuple-element.100.gm, f32[2,256,128]{2,1,0:T(8,128)S(1)} %get-tuple-element.85.kk), custom_call_target="tpu_custom_call" | custom-call | tf_op jit(solution)/shard_map/backward/pallas_call | solution.py:34
  36.2 0.0 collective-permute-done.4
  36.2 0.9 %collective-permute-start.8 = (bf16[16,4096]{1,0:T(8,128)(2,1)S(1)}, bf16[16,4096]{1,0:T(8,128)(2,1)S(1)}, u32[]{:S(2)}, u32[]{:S(2)}) collective-permute-start(bf16[16,4096]{1,0:T(8,128)(2,1)S(1)} %get-tuple-element.112), channel_id=1, source_target_pairs={{0,1},{1,0},{2,3},{3,2},{4,5},{5,4},{6,7},{7,6},{8,9},{9,8},{10,11... | collective-permute-start | bytes 393224 | tf_op jit(solution)/shard_map/ppermute | solution.py:500
  37.1 1.0 %collective-permute-done.8 = bf16[16,4096]{1,0:T(8,128)(2,1)S(1)} collective-permute-done((bf16[16,4096]{1,0:T(8,128)(2,1)S(1)}, bf16[16,4096]{1,0:T(8,128)(2,1)S(1)}, u32[]{:S(2)}, u32[]{:S(2)}) %collective-permute-start.8) | collective-permute-done | bytes 131104 | tf_op jit(solution)/shard_map/ppermute | solution.py:500
  38.0 0.1 fusion
  38.2 1.4 %collective-permute-start.10 = (bf16[16,2048]{1,0:T(8,128)(2,1)S(1)}, bf16[16,2048]{1,0:T(8,128)(2,1)S(1)}, u32[]{:S(2)}, u32[]{:S(2)}) collective-permute-start(bf16[16,2048]{1,0:T(8,128)(2,1)S(1)} %fusion.14), channel_id=1, source_target_pairs={{0,4},{1,5},{2,6},{3,7},{4,0},{5,1},{6,2},{7,3},{8,12},{9,13},{10,... | collective-permute-start | bytes 196616 | tf_op jit(solution)/shard_map/ppermute | solution.py:500
  39.5 1.6 %collective-permute-start.11 = (bf16[16,2048]{1,0:T(8,128)(2,1)S(1)}, bf16[16,2048]{1,0:T(8,128)(2,1)S(1)}, u32[]{:S(2)}, u32[]{:S(2)}) collective-permute-start(bf16[16,2048]{1,0:T(8,128)(2,1)S(1)} %fusion.14), channel_id=1, source_target_pairs={{0,2},{1,3},{2,4},{3,5},{4,6},{5,7},{6,0},{7,1},{8,10},{9,11},{10,... | collective-permute-start | bytes 196616 | tf_op jit(solution)/shard_map/ppermute | solution.py:500
  41.1 0.0 collective-permute-start.9
  41.1 1.7 %collective-permute-done.10 = bf16[16,2048]{1,0:T(8,128)(2,1)S(1)} collective-permute-done((bf16[16,2048]{1,0:T(8,128)(2,1)S(1)}, bf16[16,2048]{1,0:T(8,128)(2,1)S(1)}, u32[]{:S(2)}, u32[]{:S(2)}) %collective-permute-start.10) | collective-permute-done | bytes 65568 | tf_op jit(solution)/shard_map/ppermute | solution.py:500
  42.9 0.0 collective-permute-done.11
  42.9 2.6 %collective-permute-done.9 = bf16[16,2048]{1,0:T(8,128)(2,1)S(1)} collective-permute-done((bf16[16,2048]{1,0:T(8,128)(2,1)S(1)}, bf16[16,2048]{1,0:T(8,128)(2,1)S(1)}, u32[]{:S(2)}, u32[]{:S(2)}) %collective-permute-start.9) | collective-permute-done | bytes 65568 | tf_op jit(solution)/shard_map/ppermute | solution.py:500
  45.5 0.2 convert_select_fusion.2
  45.7 1.3 %collective-permute-start.12 = (f32[16,2048]{1,0:T(8,128)S(1)}, f32[16,2048]{1,0:T(8,128)S(1)}, u32[]{:S(2)}, u32[]{:S(2)}) collective-permute-start(f32[16,2048]{1,0:T(8,128)S(1)} %get-tuple-element.162), channel_id=1, source_target_pairs={{0,8},{1,9},{2,10},{3,11},{4,12},{5,13},{6,14},{7,15},{8,16},{9,17... | collective-permute-start | bytes 393224 | tf_op jit(solution)/shard_map/ppermute | solution.py:538
  47.0 2.5 %collective-permute-start.13 = (f32[16,2048]{1,0:T(8,128)S(1)}, f32[16,2048]{1,0:T(8,128)S(1)}, u32[]{:S(2)}, u32[]{:S(2)}) collective-permute-start(f32[16,2048]{1,0:T(8,128)S(1)} %get-tuple-element.172), channel_id=1, source_target_pairs={{0,16},{1,17},{2,18},{3,19},{4,20},{5,21},{6,22},{7,23},{8,24},{9,... | collective-permute-start | bytes 393224 | tf_op jit(solution)/shard_map/ppermute | solution.py:538
  49.5 1.2 %collective-permute-start.14 = (f32[16,2048]{1,0:T(8,128)S(1)}, f32[16,2048]{1,0:T(8,128)S(1)}, u32[]{:S(2)}, u32[]{:S(2)}) collective-permute-start(f32[16,2048]{1,0:T(8,128)S(1)} %get-tuple-element.173), channel_id=1, source_target_pairs={{0,24},{1,25},{2,26},{3,27},{4,28},{5,29},{6,30},{7,31},{8,0},{9,1... | collective-permute-start | bytes 393224 | tf_op jit(solution)/shard_map/ppermute | solution.py:538
  50.7 6.1 %lags.1.by_lag = f32[256,128]{1,0:T(8,128)S(1)} custom-call(bf16[2,32,128,128]{3,2,1,0:T(8,128)(2,1)S(1)} %get-tuple-element.120.p, bf16[32,128,128]{2,1,0:T(8,128)(2,1)S(1)} %get-tuple-element.100.gm), custom_call_target="tpu_custom_call" | custom-call | flops 6000000000 | bytes 3276800 | tf_op jit(solution)/shard_map/lags/pallas_call | solution.py:34
  56.8 0.0 collective-permute-done.14
  56.8 0.2 multiply_add_fusion.1
  57.0 0.0 copy-start.5
  57.0 0.2 fusion.13
  57.2 3.0 %collective-permute-start.15 = (f32[32,2048]{1,0:T(8,128)S(1)}, f32[32,2048]{1,0:T(8,128)S(1)}, u32[]{:S(2)}, u32[]{:S(2)}) collective-permute-start(f32[32,2048]{1,0:T(8,128)S(1)} %pad_maximum_fusion.1), channel_id=1, source_target_pairs={{0,1},{1,0},{2,3},{3,2},{4,5},{5,4},{6,7},{7,6},{8,9},{9,8},{10,11... | collective-permute-start | bytes 786440 | tf_op jit(solution)/shard_map/ppermute | solution.py:557
  60.2 1.2 %collective-permute-done.15 = f32[32,2048]{1,0:T(8,128)S(1)} collective-permute-done((f32[32,2048]{1,0:T(8,128)S(1)}, f32[32,2048]{1,0:T(8,128)S(1)}, u32[]{:S(2)}, u32[]{:S(2)}) %collective-permute-start.15) | collective-permute-done | bytes 262176 | tf_op jit(solution)/shard_map/ppermute | solution.py:557
  61.4 0.2 fusion.2
  61.6 6.0 %output.1 = (bf16[128,4096]{1,0:T(8,128)(2,1)}, f32[32,136,128]{2,1,0:T(8,128)S(1)}, f32[8,4096]{1,0:T(8,128)S(1)}) custom-call(f32[32,128,128]{2,1,0:T(8,128)S(1)} %get-tuple-element.87.inside, bf16[32,2,64,128]{3,2,1,0:T(8,128)(2,1)S(1)} %get-tuple-element.88.lrw, f32[16,4096]{1,0:T(8,128)S(1)} %get-tuple-element.169.e, ...), custom_call_target="tpu_custom_call" | custom-call | flops 8000000000 | bytes 15958016 | tf_op jit(solution)/shard_map/output/pallas_call | solution.py:34
  67.5 8.6 %mixer.1 = (f32[32,128,128]{2,1,0:T(8,128)S(1)}, f32[16,4096]{1,0:T(8,128)S(1)}, f32[128,128]{1,0:T(8,128)S(1)}, bf16[8,4096]{1,0:T(8,128)(2,1)S(1)}) custom-call(f32[32,128,128]{2,1,0:T(8,128)S(1)} %backward.1.back, bf16[32,2,64,128]{3,2,1,0:T(8,128)(2,1)S(1)} %get-tuple-element.88.lrw, bf16[16,4096]{1,0:T(8,128)(2,1)S(1)} %get-tuple-element.168.a, ...), custom_call_target="tpu_custom_call" | custom-call | flops 10000000000 | bytes 17485824 | tf_op jit(solution)/shard_map/mixer/pallas_call | solution.py:34
  76.2 2.3 %collective-permute-start.16 = (bf16[8,4096]{1,0:T(8,128)(2,1)S(1)}, bf16[8,4096]{1,0:T(8,128)(2,1)S(1)}, u32[]{:S(2)}, u32[]{:S(2)}) collective-permute-start(bf16[8,4096]{1,0:T(8,128)(2,1)S(1)} %get-tuple-element.152), channel_id=1, source_target_pairs={{1,0},{2,1},{3,2},{4,3},{5,4},{6,5},{7,6},{8,7},{9,8},{10,9},{11,1... | collective-permute-start | bytes 196616 | tf_op jit(solution)/shard_map/ppermute | solution.py:759
  78.4 2.4 %modes.1 = (f32[16,256]{1,0:T(8,128)}, f32[16,256]{1,0:T(8,128)}) custom-call(bf16[16,4096]{1,0:T(8,128)(2,1)S(1)} %get-tuple-element.168.a, f32[64,4096]{1,0:T(8,128)S(1)} %get-tuple-element.143.b, f32[16,4096]{1,0:T(8,128)S(1)} %get-tuple-element.169.e, f32[64,4096]{1,0:T(8,128)S(1)} %get-tuple-element.138.f, f32[16,4096]{1,0:T(8,128)S(1)} %get-tuple-element.86.r_e, ...), custom_call_target="tpu_custom_call" | custom-call | flops 3000000000 | bytes 3211264 | tf_op jit(solution)/shard_map/modes/pallas_call | solution.py:34
  80.9 3.0 %collective-permute-done.16.part = bf16[8,4096]{1,0:T(8,128)(2,1)S(1)} collective-permute-done((bf16[8,4096]{1,0:T(8,128)(2,1)S(1)}, bf16[8,4096]{1,0:T(8,128)(2,1)S(1)}, u32[]{:S(2)}, u32[]{:S(2)}) %collective-permute-start.16) | collective-permute-done | bytes 65568 | tf_op jit(solution)/shard_map/ppermute | solution.py:759
  83.8 2.2 %final.1 = (bf16[128,4096]{1,0:T(8,128)(2,1)}, f32[23,1,4096]{2,1,0:T(1,128)}) custom-call(f32[32,128,128]{2,1,0:T(8,128)S(1)} %get-tuple-element.148.gn, bf16[32,4096]{1,0:T(8,128)(2,1)S(1)} %collective-permute-done.1.g0, bf16[48,4096]{1,0:T(8,128)(2,1)S(1)} %collective-permute-done.2.g1, bf16[48,4096]{1,0:T(8,128)(2,1)S(1)} %collective-permute-done.5.g2, ...), custom_call_target="tpu_custom_call" | custom-call | flops 4000000000 | bytes 7294976 | tf_op jit(solution)/shard_map/final/pallas_call | solution.py:34
  (21 shorter events, 0.1 us)
Async XLA Ops:
  0.6 6.3 %copy-start = (bf16[1,128,4096]{2,1,0:T(8,128)(2,1)S(1)}, bf16[1,128,4096]{2,1,0:T(8,128)(2,1)}, u32[]{:S(2)}) copy-start(bf16[1,128,4096]{2,1,0:T(8,128)(2,1)} %param.7) | copy-start | bytes 3145732
  0.6 10.5 %copy-start.3 = (f32[1,16,256]{2,1,0:T(8,128)S(1)}, f32[1,16,256]{2,1,0:T(8,128)}, u32[]{:S(2)}) copy-start(f32[1,16,256]{2,1,0:T(8,128)} %param.11) | copy-start | bytes 49156
  0.7 10.5 %copy-start.4 = (f32[1,16,256]{2,1,0:T(8,128)S(1)}, f32[1,16,256]{2,1,0:T(8,128)}, u32[]{:S(2)}) copy-start(f32[1,16,256]{2,1,0:T(8,128)} %param.12) | copy-start | bytes 49156
  0.7 13.8 %copy-start.1 = (f32[1,21,4096]{2,0,1:T(1,128)S(1)}, f32[1,21,4096]{2,0,1:T(1,128)}, u32[]{:S(2)}) copy-start(f32[1,21,4096]{2,0,1:T(1,128)} %param.10) | copy-start | bytes 1032196
  0.7 13.8 %copy-start.2 = (f32[1,4096]{1,0:T(1,128)S(1)}, f32[1,4096]{1,0:T(1,128)}, u32[]{:S(2)}) copy-start(f32[1,4096]{1,0:T(1,128)} %gain_all.1) | copy-start | bytes 49156
  1.8 12.7 %collective-permute-start.1 = (bf16[32,4096]{1,0:T(8,128)(2,1)S(1)}, bf16[32,4096]{1,0:T(8,128)(2,1)S(1)}, u32[]{:S(2)}, u32[]{:S(2)}) collective-permute-start(bf16[32,4096]{1,0:T(8,128)(2,1)S(1)} %slice_bitcast_fusion.2), channel_id=1, source_target_pairs={{0,96},{32,0},{64,32},{96,64},{1,97},{33,1},{65,33},{97,65},{2,98}... | collective-permute-start | bytes 786440 | tf_op jit(solution)/shard_map/ppermute | solution.py:581
  6.7 14.7 %collective-permute-start.2 = (bf16[48,4096]{1,0:T(8,128)(2,1)S(1)}, bf16[48,4096]{1,0:T(8,128)(2,1)S(1)}, u32[]{:S(2)}, u32[]{:S(2)}) collective-permute-start(bf16[48,4096]{1,0:T(8,128)(2,1)S(1)} %get-tuple-element.167), channel_id=1, source_target_pairs={{0,96},{32,0},{64,32},{96,64},{1,97},{33,1},{65,33},{97,65},{2,98}... | collective-permute-start | bytes 1179656 | tf_op jit(solution)/shard_map/ppermute | solution.py:581
  7.0 7.5 %collective-permute-start = (bf16[8,4096]{1,0:T(8,128)(2,1)S(1)}, bf16[8,4096]{1,0:T(8,128)(2,1)S(1)}, u32[]{:S(2)}, u32[]{:S(2)}) collective-permute-start(bf16[8,4096]{1,0:T(8,128)(2,1)S(1)} %slice_bitcast_fusion.3), channel_id=1, source_target_pairs={{0,1},{1,2},{2,3},{3,4},{4,5},{5,6},{6,7},{7,8},{8,9},{9,10},{10,1... | collective-permute-start | bytes 196616 | tf_op jit(solution)/shard_map/ppermute | solution.py:585
  21.5 2.5 %collective-permute-start.3 = (f32[16,4096]{1,0:T(8,128)S(1)}, f32[16,4096]{1,0:T(8,128)S(1)}, u32[]{:S(2)}, u32[]{:S(2)}) collective-permute-start(f32[16,4096]{1,0:T(8,128)S(1)} %get-tuple-element.90), channel_id=1, source_target_pairs={{0,1},{1,0},{2,3},{3,2},{4,5},{5,4},{6,7},{7,6},{8,9},{9,8},{10,11... | collective-permute-start | bytes 786440 | tf_op jit(solution)/shard_map/ppermute | solution.py:500
  21.6 10.9 %collective-permute-start.5 = (bf16[48,4096]{1,0:T(8,128)(2,1)S(1)}, bf16[48,4096]{1,0:T(8,128)(2,1)S(1)}, u32[]{:S(2)}, u32[]{:S(2)}) collective-permute-start(bf16[48,4096]{1,0:T(8,128)(2,1)S(1)} %get-tuple-element.166), channel_id=1, source_target_pairs={{0,96},{32,0},{64,32},{96,64},{1,97},{33,1},{65,33},{97,65},{2,98}... | collective-permute-start | bytes 1179656 | tf_op jit(solution)/shard_map/ppermute | solution.py:581
  24.1 12.1 %collective-permute-start.7 = (f32[16,2048]{1,0:T(8,128)S(1)}, f32[16,2048]{1,0:T(8,128)S(1)}, u32[]{:S(2)}, u32[]{:S(2)}) collective-permute-start(f32[16,2048]{1,0:T(8,128)S(1)} %slice_select_fusion.1), channel_id=1, source_target_pairs={{0,6},{1,7},{2,0},{3,1},{4,2},{5,3},{6,4},{7,5},{8,14},{9,15},{10,... | collective-permute-start | bytes 393224 | tf_op jit(solution)/shard_map/ppermute | solution.py:500
  24.6 11.6 %collective-permute-start.6 = (f32[16,2048]{1,0:T(8,128)S(1)}, f32[16,2048]{1,0:T(8,128)S(1)}, u32[]{:S(2)}, u32[]{:S(2)}) collective-permute-start(f32[16,2048]{1,0:T(8,128)S(1)} %slice_select_fusion.1), channel_id=1, source_target_pairs={{0,4},{1,5},{2,6},{3,7},{4,0},{5,1},{6,2},{7,3},{8,12},{9,13},{10,... | collective-permute-start | bytes 393224 | tf_op jit(solution)/shard_map/ppermute | solution.py:500
  25.3 10.9 %collective-permute-start.4 = (f32[16,2048]{1,0:T(8,128)S(1)}, f32[16,2048]{1,0:T(8,128)S(1)}, u32[]{:S(2)}, u32[]{:S(2)}) collective-permute-start(f32[16,2048]{1,0:T(8,128)S(1)} %slice_select_fusion.1), channel_id=1, source_target_pairs={{0,2},{1,3},{2,4},{3,5},{4,6},{5,7},{6,0},{7,1},{8,10},{9,11},{10,... | collective-permute-start | bytes 393224 | tf_op jit(solution)/shard_map/ppermute | solution.py:500
  36.2 1.8 %collective-permute-start.8 = (bf16[16,4096]{1,0:T(8,128)(2,1)S(1)}, bf16[16,4096]{1,0:T(8,128)(2,1)S(1)}, u32[]{:S(2)}, u32[]{:S(2)}) collective-permute-start(bf16[16,4096]{1,0:T(8,128)(2,1)S(1)} %get-tuple-element.112), channel_id=1, source_target_pairs={{0,1},{1,0},{2,3},{3,2},{4,5},{5,4},{6,7},{7,6},{8,9},{9,8},{10,11... | collective-permute-start | bytes 393224 | tf_op jit(solution)/shard_map/ppermute | solution.py:500
  38.2 4.7 %collective-permute-start.10 = (bf16[16,2048]{1,0:T(8,128)(2,1)S(1)}, bf16[16,2048]{1,0:T(8,128)(2,1)S(1)}, u32[]{:S(2)}, u32[]{:S(2)}) collective-permute-start(bf16[16,2048]{1,0:T(8,128)(2,1)S(1)} %fusion.14), channel_id=1, source_target_pairs={{0,4},{1,5},{2,6},{3,7},{4,0},{5,1},{6,2},{7,3},{8,12},{9,13},{10,... | collective-permute-start | bytes 196616 | tf_op jit(solution)/shard_map/ppermute | solution.py:500
  39.5 3.3 %collective-permute-start.11 = (bf16[16,2048]{1,0:T(8,128)(2,1)S(1)}, bf16[16,2048]{1,0:T(8,128)(2,1)S(1)}, u32[]{:S(2)}, u32[]{:S(2)}) collective-permute-start(bf16[16,2048]{1,0:T(8,128)(2,1)S(1)} %fusion.14), channel_id=1, source_target_pairs={{0,2},{1,3},{2,4},{3,5},{4,6},{5,7},{6,0},{7,1},{8,10},{9,11},{10,... | collective-permute-start | bytes 196616 | tf_op jit(solution)/shard_map/ppermute | solution.py:500
  41.1 4.3 %collective-permute-start.9 = (bf16[16,2048]{1,0:T(8,128)(2,1)S(1)}, bf16[16,2048]{1,0:T(8,128)(2,1)S(1)}, u32[]{:S(2)}, u32[]{:S(2)}) collective-permute-start(bf16[16,2048]{1,0:T(8,128)(2,1)S(1)} %fusion.14), channel_id=1, source_target_pairs={{0,6},{1,7},{2,0},{3,1},{4,2},{5,3},{6,4},{7,5},{8,14},{9,15},{10,... | collective-permute-start | bytes 196616 | tf_op jit(solution)/shard_map/ppermute | solution.py:500
  45.7 11.1 %collective-permute-start.12 = (f32[16,2048]{1,0:T(8,128)S(1)}, f32[16,2048]{1,0:T(8,128)S(1)}, u32[]{:S(2)}, u32[]{:S(2)}) collective-permute-start(f32[16,2048]{1,0:T(8,128)S(1)} %get-tuple-element.162), channel_id=1, source_target_pairs={{0,8},{1,9},{2,10},{3,11},{4,12},{5,13},{6,14},{7,15},{8,16},{9,17... | collective-permute-start | bytes 393224 | tf_op jit(solution)/shard_map/ppermute | solution.py:538
  47.0 9.8 %collective-permute-start.13 = (f32[16,2048]{1,0:T(8,128)S(1)}, f32[16,2048]{1,0:T(8,128)S(1)}, u32[]{:S(2)}, u32[]{:S(2)}) collective-permute-start(f32[16,2048]{1,0:T(8,128)S(1)} %get-tuple-element.172), channel_id=1, source_target_pairs={{0,16},{1,17},{2,18},{3,19},{4,20},{5,21},{6,22},{7,23},{8,24},{9,... | collective-permute-start | bytes 393224 | tf_op jit(solution)/shard_map/ppermute | solution.py:538
  49.5 7.3 %collective-permute-start.14 = (f32[16,2048]{1,0:T(8,128)S(1)}, f32[16,2048]{1,0:T(8,128)S(1)}, u32[]{:S(2)}, u32[]{:S(2)}) collective-permute-start(f32[16,2048]{1,0:T(8,128)S(1)} %get-tuple-element.173), channel_id=1, source_target_pairs={{0,24},{1,25},{2,26},{3,27},{4,28},{5,29},{6,30},{7,31},{8,0},{9,1... | collective-permute-start | bytes 393224 | tf_op jit(solution)/shard_map/ppermute | solution.py:538
  57.0 4.6 %copy-start.5 = (f32[1,4096]{1,0:T(1,128)S(1)}, f32[1,4096]{1,0:T(1,128)}, u32[]{:S(2)}) copy-start(f32[1,4096]{1,0:T(1,128)} %skip.3) | copy-start | bytes 49156
  57.2 4.1 %collective-permute-start.15 = (f32[32,2048]{1,0:T(8,128)S(1)}, f32[32,2048]{1,0:T(8,128)S(1)}, u32[]{:S(2)}, u32[]{:S(2)}) collective-permute-start(f32[32,2048]{1,0:T(8,128)S(1)} %pad_maximum_fusion.1), channel_id=1, source_target_pairs={{0,1},{1,0},{2,3},{3,2},{4,5},{5,4},{6,7},{7,6},{8,9},{9,8},{10,11... | collective-permute-start | bytes 786440 | tf_op jit(solution)/shard_map/ppermute | solution.py:557
  76.2 7.7 %collective-permute-start.16 = (bf16[8,4096]{1,0:T(8,128)(2,1)S(1)}, bf16[8,4096]{1,0:T(8,128)(2,1)S(1)}, u32[]{:S(2)}, u32[]{:S(2)}) collective-permute-start(bf16[8,4096]{1,0:T(8,128)(2,1)S(1)} %get-tuple-element.152), channel_id=1, source_target_pairs={{1,0},{2,1},{3,2},{4,3},{5,4},{6,5},{7,6},{8,7},{9,8},{10,9},{11,1... | collective-permute-start | bytes 196616 | tf_op jit(solution)/shard_map/ppermute | solution.py:759
